TPU v7x, 256 devices: a whole 4x4x8 slice. The times are simulated.
256 devices in a mesh: dp: 32 (over x, y, core), vocab: 8 (over z).
Axes of the slice: x: 4, y: 4, z: 8, core: 2. Of those that a mesh axis runs over, the one named last changes fastest.
Arguments:
- queries: bfloat16 [1024, 4096], P('dp', 'vocab'), may hold values from -1200 to 1200
- own_keys: bfloat16 [1024, 2048], P('dp', 'vocab'), may hold values from -8 to 8
- own_values: bfloat16 [1024, 2048], P('dp', 'vocab'), may hold values from -6 to 6
- prompt_keys: bfloat16 [32, 128, 2048], P('dp', None, 'vocab'), may hold values from -6 to 6
- prompt_values: bfloat16 [32, 128, 2048], P('dp', None, 'vocab'), may hold values from -6 to 6
- prompt_lengths: int32 [32], replicated, may hold values from 1 to 128
- completion_prompt: int32 [128], replicated, may hold values from 0 to 31, as said below
- completion_lengths: int32 [128], replicated, may hold values from 2 to 8
- targets: int32 [1024], replicated, may hold values from 0 to 131071
- advantages: float32 [128], replicated, may hold values from -4 to 4
- residual: bfloat16 [1024, 5376], P('dp'), may hold values from -16 to 16
- out_proj: bfloat16 [4096, 5376], P('vocab'), may hold values from -0.25 to 0.25
- norm_gain: float32 [5376], replicated, may hold values from 0.5 to 1.5
- embedding: bfloat16 [131072, 5376], P(('dp', 'vocab')), may hold values from -4 to 4
Outputs:
- logprob: float32 [1024], P('dp')
- hidden_grad: float32 [1024, 5376], P('dp')
Inputs may be any that keep to these rules, and one draw needn't show every extreme that they name: `completion_prompt`: each prompt is named by the same number of completions.
All inputs are finite; a program needn't handle non-finite values.
Results may differ from a plain program's by a relative error of at most 0.023.
Values may be sent and summed in bfloat16 or wider, within the bound.
No kernel may reach another device: no remote copies, remote signals or barrier semaphores. Data moves between devices by JAX's collectives and lax.ppermute only.
A program may use at most 128 MiB of HBM per device.

v0:
```python
import jax
import jax.numpy as jnp
from jax import lax
from jax.sharding import PartitionSpec as P

HDIM = 128
CLEN = 8


score_scale = 168.0 ** (-0.5)
norm_epsilon = 1e-06


def joined(x, axis, combine):
    everything = jax.tree.map(lambda part: lax.all_gather(part, axis), x)
    leading = jax.tree.map(lambda part: part[0], everything)

    def step(k, so_far):
        return combine(so_far, jax.tree.map(lambda part: part[k], everything))

    return lax.fori_loop(1, lax.axis_size(axis), step, leading)


def attend_local(queries, key_block, value_block, visible):
    comp_count, step_count, heads_here, head_width = queries.shape
    key_heads = key_block.shape[2]
    group_size = heads_here // key_heads
    grouped = queries.reshape(comp_count, step_count, key_heads, group_size, head_width)
    scores = (
        jnp.einsum("ctkgd,cnkd->ctkgn", grouped, key_block, preferred_element_type=jnp.float32)
        * score_scale
    )
    scores = jnp.where(visible[:, :, None, None, :], scores, -jnp.inf)
    row_top = jnp.max(scores, axis=-1, keepdims=True)
    exp_scores = jnp.exp(scores - row_top)
    weights = (exp_scores / jnp.sum(exp_scores, axis=-1, keepdims=True)).astype(jnp.bfloat16)
    mixed_values = jnp.einsum(
        "ctkgn,cnkd->ctkgd", weights, value_block, preferred_element_type=jnp.float32
    )
    return mixed_values.reshape(comp_count * step_count, heads_here * head_width).astype(
        jnp.bfloat16
    )


def normalize(hidden, norm_gain):
    norm_factor = lax.rsqrt(jnp.mean(hidden * hidden, axis=-1, keepdims=True) + norm_epsilon)
    return ((hidden * norm_factor * norm_gain).astype(jnp.bfloat16), norm_factor)


def norm_backward(hidden, norm_factor, gradient, norm_gain):
    return norm_gain * norm_factor * gradient - hidden * norm_factor**3 * jnp.mean(
        norm_gain * gradient * hidden, axis=-1, keepdims=True
    )


def merge_stats(first, second):
    row_top = jnp.maximum(first[0], second[0])
    row_total = first[1] * jnp.exp(first[0] - row_top) + second[1] * jnp.exp(second[0] - row_top)
    return (row_top, row_total, first[2] + second[2])


def body(
    queries,
    own_keys,
    own_values,
    prompt_keys,
    prompt_values,
    prompt_lengths,
    completion_prompt,
    completion_lengths,
    targets,
    advantages,
    residual,
    out_proj,
    norm_gain,
    embedding,
):
    row_count = residual.shape[0]
    comp_count = row_count // CLEN
    heads_here = queries.shape[1] // HDIM
    key_heads = own_keys.shape[1] // HDIM
    prompt_span = prompt_keys.shape[1]
    vocab_slab = embedding.shape[0]
    dp_index = lax.axis_index("dp")
    vocab_count = lax.axis_size("vocab")
    vocab_index = lax.axis_index("vocab")
    every_key, every_value = (
        lax.all_gather(prompt_keys, "dp", axis=0, tiled=True),
        lax.all_gather(prompt_values, "dp", axis=0, tiled=True),
    )
    my_prompts = lax.dynamic_slice_in_dim(completion_prompt, dp_index * comp_count, comp_count)
    key_block = jnp.concatenate(
        [every_key[my_prompts], own_keys.reshape(comp_count, CLEN, -1)], axis=1
    )
    key_block = key_block.reshape(comp_count, prompt_span + CLEN, key_heads, HDIM)
    value_block = jnp.concatenate(
        [every_value[my_prompts], own_values.reshape(comp_count, CLEN, -1)], axis=1
    )
    value_block = value_block.reshape(comp_count, prompt_span + CLEN, key_heads, HDIM)
    inside = jnp.arange(prompt_span)[None, :] < prompt_lengths[my_prompts][:, None]
    causal = jnp.arange(CLEN)[:, None] >= jnp.arange(CLEN)[None, :]
    visible = jnp.concatenate(
        [
            jnp.broadcast_to(inside[:, None, :], (comp_count, CLEN, prompt_span)),
            jnp.broadcast_to(causal[None], (comp_count, CLEN, CLEN)),
        ],
        axis=2,
    )
    attended = attend_local(
        queries.reshape(comp_count, CLEN, heads_here, HDIM), key_block, value_block, visible
    )
    partial_value = jnp.dot(attended, out_proj, preferred_element_type=jnp.float32)
    head_total = lax.psum(partial_value, "vocab")
    hidden = residual.astype(jnp.float32) + head_total
    normed, norm_factor = normalize(hidden, norm_gain)
    logits = lax.dot_general(
        lax.all_gather(normed, "dp", axis=0, tiled=True),
        embedding,
        (((1,), (1,)), ((), ())),
        preferred_element_type=jnp.float32,
    )
    slab_index = dp_index * vocab_count + vocab_index
    local_target = targets - slab_index * vocab_slab
    column_ids = jnp.arange(vocab_slab, dtype=jnp.int32)
    target_hit = column_ids[None, :] == local_target[:, None]
    row_top = jnp.max(logits, axis=1)
    row_total = jnp.sum(jnp.exp(logits - row_top[:, None]), axis=1)
    picked = jnp.sum(jnp.where(target_hit, logits, 0.0), axis=1)
    row_top, row_total, picked = joined((row_top, row_total, picked), ("dp", "vocab"), merge_stats)
    log_total = row_top + jnp.log(row_total)
    every_logprob = picked - log_total
    logprob = lax.dynamic_slice_in_dim(every_logprob, dp_index * row_count, row_count)
    row_ids = jnp.arange(targets.shape[0], dtype=jnp.int32)
    position = row_ids % CLEN
    live_token = position < jnp.repeat(completion_lengths, CLEN)
    token_weight = jnp.where(live_token, -jnp.repeat(advantages, CLEN), 0.0)
    probability = jnp.exp(logits - log_total[:, None])
    logit_grad = (token_weight[:, None] * (target_hit.astype(jnp.float32) - probability)).astype(
        jnp.bfloat16
    )
    summed_rows = lax.psum_scatter(
        jnp.dot(logit_grad, embedding, preferred_element_type=jnp.float32).astype(jnp.bfloat16),
        "dp",
        scatter_dimension=0,
        tiled=True,
    ).astype(jnp.float32)
    normed_grad = lax.psum(summed_rows, "vocab")
    hidden_grad = norm_backward(hidden, norm_factor, normed_grad, norm_gain)
    return (logprob, hidden_grad)


def solution(mesh):
    placed = (
        P("dp", "vocab"),
        P("dp", "vocab"),
        P("dp", "vocab"),
        P("dp", None, "vocab"),
        P("dp", None, "vocab"),
        P(),
        P(),
        P(),
        P(),
        P(),
        P("dp", None),
        P("vocab", None),
        P(),
        P(("dp", "vocab"), None),
    )
    return jax.shard_map(
        body, mesh=mesh, in_specs=placed, out_specs=(P("dp"), P("dp", None)), check_vma=False
    )
```

profile of v0, /device:TPU:2, one launch (start us, length us, event | category | flops | bytes accessed | tf_op | source)
XLA Modules:
  0.0 968.4 jit_solution(2544872829198362145)
XLA Ops:
  9.5 1.3 gather_fusion.1
  10.9 51.1 %all-gather.10.cloned.1.call-done = bf16[32,128,256]{2,1,0:T(8,128)(2,1)} async-done(((bf16[1,128,256]{2,1,0:T(8,128)(2,1)}), bf16[32,128,256]{2,1,0:T(8,128)(2,1)}) %all-gather.10.cloned.1.call-update) | async-done | bytes 2097168 | tf_op jit(solution)/shard_map/all_gather | solution.py:89
  62.0 2.2 gather_fusion
  64.5 48.2 %all-gather.12.cloned.1.call-done = bf16[32,128,256]{2,1,0:T(8,128)(2,1)} async-done(((bf16[1,128,256]{2,1,0:T(8,128)(2,1)}), bf16[32,128,256]{2,1,0:T(8,128)(2,1)}) %all-gather.12.cloned.1.call-update) | async-done | bytes 2097168 | tf_op jit(solution)/shard_map/all_gather | solution.py:88
  112.7 2.2 gather_fusion.2
  116.1 4.5 fusion.34
  120.7 74.3 %all-reduce.3.cloned.1.call-done = f32[32,5376]{1,0:T(8,128)} async-done(((f32[32,5376]{1,0:T(8,128)}), f32[32,5376]{1,0:T(8,128)}) %all-reduce.3.cloned.1.call-update) | async-done | bytes 688144 | tf_op jit(solution)/shard_map/psum | solution.py:113
  195.0 1.3 multiply_reduce_fusion.1
  196.3 2.0 multiply_convert_fusion.2
  198.4 62.5 %all-gather.14.cloned.1.call-done = bf16[1024,5376]{1,0:T(8,128)(2,1)} async-done(((bf16[32,5376]{1,0:T(8,128)(2,1)}), bf16[1024,5376]{1,0:T(8,128)(2,1)}) %all-gather.14.cloned.1.call-update) | async-done | bytes 11010064 | tf_op jit(solution)/shard_map/all_gather | solution.py:117
  260.9 10.9 %fusion.33 = (f32[1024]{0:T(1024)}, f32[1024,512]{0,1:T(8,128)S(1)}) fusion(bf16[1024,5376]{1,0:T(8,128)(2,1)} %all-gather.14.cloned.1.call-done, bf16[512,5376]{1,0:T(8,128)(2,1)} %param.29), kind=kOutput, calls=%fused_computation.62 | convolution fusion | flops 5637667840 | bytes 18616320 | tf_op jit(solution)/shard_map/dot_general | solution.py:116
  271.9 1.8 select_reduce_fusion
  274.9 98.6 %all-gather.16.cloned.1.call-done = f32[262144]{0:T(1024)} async-done(((f32[1024]{0:T(1024)}), f32[262144]{0:T(1024)}) %all-gather.16.cloned.1.call-update) | async-done | bytes 1048592 | tf_op jit(solution)/shard_map/all_gather | solution.py:15
  373.5 1.4 reshape.120
  374.9 103.2 %all-gather.18.cloned.1.call-done = f32[262144]{0:T(1024)} async-done(((f32[1024]{0:T(1024)}), f32[262144]{0:T(1024)}) %all-gather.18.cloned.1.call-update) | async-done | bytes 1048592 | tf_op jit(solution)/shard_map/all_gather | solution.py:15
  478.2 2.4 reshape.121
  480.6 102.3 %all-gather.20.cloned.1.call-done = f32[262144]{0:T(1024)} async-done(((f32[1024]{0:T(1024)}), f32[262144]{0:T(1024)}) %all-gather.20.cloned.1.call-update) | async-done | bytes 1048592 | tf_op jit(solution)/shard_map/all_gather | solution.py:15
  582.9 2.4 reshape.122
  585.4 220.1 %while.19 = (s32[]{:T(128)}, f32[1024]{0:T(1024)S(1)}, f32[1024]{0:T(1024)S(1)}, f32[1024]{0:T(1024)S(1)}, f32[256,1024]{1,0:T(8,128)S(1)}, /*index=5*/f32[256,1...) while((s32[]{:T(128)}, f32[1024]{0:T(1024)S(1)}, f32[1024]{0:T(1024)S(1)}, ...), condition=%wide.region_8.9_spmd, body=%wide.region_7.8_spmd.sunk | while | flops 7173 | bytes 61591 | solution.py:21
  598.3 0.8 constant_dynamic-slice_fusion.5
  763.9 0.8 constant_dynamic-slice_fusion.5
  764.8 0.8 constant_dynamic-slice_fusion.5
  765.7 0.8 constant_dynamic-slice_fusion.5
  766.6 0.8 constant_dynamic-slice_fusion.5
  767.4 0.8 constant_dynamic-slice_fusion.5
  768.3 0.8 constant_dynamic-slice_fusion.5
  769.2 0.8 constant_dynamic-slice_fusion.5
  770.0 0.8 constant_dynamic-slice_fusion.5
  805.4 11.3 %convolution_convert_fusion = bf16[1024,5376]{1,0:T(8,128)(2,1)} fusion(bf16[512,5376]{1,0:T(8,128)(2,1)} %param.29, f32[1024,512]{0,1:T(8,128)S(1)} %get-tuple-element.208, f32[1024]{0:T(1024)S(1)} %get-tuple-element.202, f32[1024]{0:T(1024)S(1)} %fusion.17, s32[1024]{0:T(1024)S(1)} %broadcast_subtract_fusion), kind=kOutput, calls=%fused_computation.8 | convolution fusion | flops 5645795328 | bytes 18624512 | tf_op jit(solution)/shard_map/dot_general | solution.py:142
  817.3 105.3 %reduce-scatter.2.cloned.1.call-done = bf16[32,5376]{1,0:T(8,128)(2,1)} async-done(((bf16[1024,5376]{1,0:T(8,128)(2,1)}), bf16[32,5376]{1,0:T(8,128)(2,1)}) %reduce-scatter.2.cloned.1.call-update) | async-done | bytes 344080 | tf_op jit(solution)/shard_map/reduce_scatter | solution.py:141
  922.7 37.6 %all-reduce.4 = f32[32,5376]{1,0:T(8,128)S(1)} all-reduce(bf16[32,5376]{1,0:T(8,128)(2,1)} %reduce-scatter.2.cloned.1.call-done), channel_id=1, replica_groups=mesh['dp'=32,'vocab'=8] {'vocab'}, use_global_device_ids=true, to_apply=%region_10.11 | all-reduce | flops 172032 | bytes 1032192 | tf_op jit(solution)/shard_map/psum | solution.py:147
  960.5 1.1 multiply_subtract_fusion
  (1078 shorter events, 207.8 us)
Async XLA Ops:
  7.2 108.1 %copy-start = (bf16[32,512]{1,0:T(8,128)(2,1)S(1)}, bf16[32,512]{1,0:T(8,128)(2,1)}, u32[]{:S(2)}) copy-start(bf16[32,512]{1,0:T(8,128)(2,1)} %param.16) | copy-start | bytes 98308
  7.2 108.0 %copy-start.8 = (bf16[32,256]{1,0:T(8,128)(2,1)S(1)}, bf16[32,256]{1,0:T(8,128)(2,1)}, u32[]{:S(2)}) copy-start(bf16[32,256]{1,0:T(8,128)(2,1)} %param.17) | copy-start | bytes 49156
  7.2 54.8 %all-gather.10.cloned.1.call-start = ((), (), s32[]{:S(2)}) async-start(), calls=%async_computation.1 | async-start | bytes 2162688 | tf_op jit(solution)/shard_map/all_gather | solution.py:89
  7.9 104.8 %all-gather.12.cloned.1.call-start = ((), (), s32[]{:S(2)}) async-start(), calls=%async_computation.2 | async-start | bytes 2162688 | tf_op jit(solution)/shard_map/all_gather | solution.py:88
  8.7 186.3 %all-reduce.3.cloned.1.call-start = ((), (), s32[]{:S(2)}) async-start(), calls=%async_computation.3 | async-start | bytes 1376256 | tf_op jit(solution)/shard_map/psum | solution.py:113
  9.5 106.2 %copy-start.7 = (bf16[32,256]{1,0:T(8,128)(2,1)S(1)}, bf16[32,256]{1,0:T(8,128)(2,1)}, u32[]{:S(2)}) copy-start(bf16[32,256]{1,0:T(8,128)(2,1)} %param.18) | copy-start | bytes 49156
  116.1 78.9 %copy-start.2 = (bf16[32,5376]{1,0:T(8,128)(2,1)S(1)}, bf16[32,5376]{1,0:T(8,128)(2,1)}, u32[]{:S(2)}) copy-start(bf16[32,5376]{1,0:T(8,128)(2,1)} %param.26) | copy-start | bytes 1032196
  116.1 80.2 %copy-start.3 = (f32[5376]{0:T(1024)S(1)}, f32[5376]{0:T(1024)}, u32[]{:S(2)}) copy-start(f32[5376]{0:T(1024)} %param.28) | copy-start | bytes 64516
  120.7 140.2 %all-gather.14.cloned.1.call-start = ((), (), s32[]{:S(2)}) async-start(), calls=%async_computation.4 | async-start | bytes 11354112 | tf_op jit(solution)/shard_map/all_gather | solution.py:117
  198.3 73.6 %copy-start.5 = (s32[1024]{0:T(1024)S(1)}, s32[1024]{0:T(1024)}, u32[]{:S(2)}) copy-start(s32[1024]{0:T(1024)} %param.24) | copy-start | bytes 12292
  198.3 175.2 %all-gather.16.cloned.1.call-start = ((), (), s32[]{:S(2)}) async-start(), calls=%async_computation.6 | async-start | bytes 1052672 | tf_op jit(solution)/shard_map/all_gather | solution.py:15
  271.8 2.8 copy-start.9
  271.8 3.0 copy-start.6
  271.8 206.4 %all-gather.18.cloned.1.call-start = ((), (), s32[]{:S(2)}) async-start(), calls=%async_computation.7 | async-start | bytes 1052672 | tf_op jit(solution)/shard_map/all_gather | solution.py:15
  273.7 309.2 %all-gather.20.cloned.1.call-start = ((), (), s32[]{:S(2)}) async-start(), calls=%async_computation.8 | async-start | bytes 1052672 | tf_op jit(solution)/shard_map/all_gather | solution.py:15
  274.5 648.2 %reduce-scatter.2.cloned.1.call-start = ((), (), s32[]{:S(2)}) async-start(), calls=%async_computation.5 | async-start | bytes 11354112 | tf_op jit(solution)/shard_map/reduce_scatter | solution.py:141
  478.2 107.2 %slice-start = ((f32[262144]{0:T(1024)}), f32[1024]{0:T(1024)S(1)}, s32[]{:S(2)}) async-start(f32[262144]{0:T(1024)} %all-gather.16.cloned.1.call-done), calls=%async_computation.9 | async-start | bytes 8192 | tf_op jit(solution)/shard_map/slice | solution.py:16
  478.2 107.2 %slice-start.1 = ((f32[262144]{0:T(1024)}), f32[1024]{0:T(1024)S(1)}, s32[]{:S(2)}) async-start(f32[262144]{0:T(1024)} %all-gather.18.cloned.1.call-done), calls=%async_computation.10 | async-start | bytes 8192 | tf_op jit(solution)/shard_map/slice | solution.py:16
  582.9 2.4 slice-start.2
  816.7 143.6 %copy-start.1 = (f32[32,5376]{1,0:T(8,128)S(1)}, f32[32,5376]{1,0:T(8,128)}, u32[]{:S(2)}) copy-start(f32[32,5376]{1,0:T(8,128)} %all-reduce.3.cloned.1.call-done) | copy-start | bytes 2064388
  816.7 143.6 %copy-start.4 = (f32[5376]{0:T(1024)S(1)}, f32[5376]{0:T(1024)}, u32[]{:S(2)}) copy-start(f32[5376]{0:T(1024)} %param.28) | copy-start | bytes 64516
Sparse Core Ops, SparseCore 0:
  10.6 51.3 all-gather.9
  64.5 48.1 all-gather.11
  120.8 74.1 all-reduce.2
  198.4 62.3 all-gather.13
  271.9 101.5 all-gather.15
  377.1 100.9 all-gather.17
  481.9 100.9 all-gather.19
  816.8 105.7 reduce-scatter.1
where the time goes:
time: 987 us; the launch traced here: 968 us
  waiting for transfers between devices  648 us (66%)
  local copies, waits for them, and re-layouts  218 us (22%)
  blocking collectives  37.6 us (4%)
  matrix products  27.6 us (3%)
  between operations  14.4 us (1%)
  other arithmetic  11.4 us (1%)
  loops' own time  11.3 us (1%)
    all_gather x3, waiting for transfers between devices, joined(): everything = jax.tree.map(lambda part: lax.all_gather(part, axis), x)  304 us
    dynamic_slice x510, local copies, waits for them, and re-layouts, step(): return combine(so_far, jax.tree.map(lambda part: part[k], everything))  205 us
    reduce_scatter x1, waiting for transfers between devices, body(): lax.psum_scatter(jnp.dot(logit_grad, embedding, preferred_element_type=jn...  105 us
    psum x1, waiting for transfers between devices, body(): head_total = lax.psum(partial_value, 'vocab')  74.3 us
    all_gather x1, waiting for transfers between devices, body(): lax.all_gather(normed, 'dp', axis=0, tiled=True)  62.5 us
    all_gather x1, waiting for transfers between devices, body(): lax.all_gather(prompt_values, 'dp', axis=0, tiled=True)  51.1 us
    all_gather x1, waiting for transfers between devices, body(): lax.all_gather(prompt_keys, 'dp', axis=0, tiled=True)  48.2 us
    psum x1, blocking collectives, body(): normed_grad = lax.psum(summed_rows, 'vocab')  37.6 us
  transfers between devices with their start and end apart: 8, of which 8 were waited for; matrix products, arithmetic and copies ran while one was open for 1% of the time, Pallas kernels for 0%

commit v1 on v0

v1 whole, which is shorter than its diff:
```python
import jax
import jax.numpy as jnp
from jax import lax
from jax.sharding import Mesh
from jax.sharding import PartitionSpec as P

HDIM = 128
CLEN = 8
XS, YS, CS = 4, 4, 2

score_scale = 168.0 ** (-0.5)
norm_epsilon = 1e-06
SWAP = ((0, 1), (1, 0))


def spread(part, axes):
    count = lax.axis_size(axes)
    copies = jnp.broadcast_to(part[None], (count,) + part.shape)
    return lax.all_to_all(copies, axes, 0, 0, tiled=True)


def summed(rows, axes):
    count = lax.axis_size(axes)
    pieces = rows.reshape(count, rows.shape[0] // count, rows.shape[1])
    arrived = lax.all_to_all(pieces, axes, 0, 0, tiled=True)
    return jnp.sum(arrived.astype(jnp.float32), axis=0)


def attend_local(queries, key_block, value_block, visible):
    comp_count, step_count, heads_here, head_width = queries.shape
    key_heads = key_block.shape[2]
    group_size = heads_here // key_heads
    grouped = queries.reshape(comp_count, step_count, key_heads, group_size, head_width)
    scores = (
        jnp.einsum("ctkgd,cnkd->ctkgn", grouped, key_block, preferred_element_type=jnp.float32)
        * score_scale
    )
    scores = jnp.where(visible[:, :, None, None, :], scores, -jnp.inf)
    row_top = jnp.max(scores, axis=-1, keepdims=True)
    exp_scores = jnp.exp(scores - row_top)
    weights = (exp_scores / jnp.sum(exp_scores, axis=-1, keepdims=True)).astype(jnp.bfloat16)
    mixed_values = jnp.einsum(
        "ctkgn,cnkd->ctkgd", weights, value_block, preferred_element_type=jnp.float32
    )
    return mixed_values.reshape(comp_count * step_count, heads_here * head_width).astype(
        jnp.bfloat16
    )


def merged(stats):
    top = jnp.max(stats[:, 0], axis=0)
    total = jnp.sum(stats[:, 1] * jnp.exp(stats[:, 0] - top[None]), axis=0)
    return jnp.stack([top, total, jnp.sum(stats[:, 2], axis=0)])


def body(
    queries,
    own_keys,
    own_values,
    prompt_keys,
    prompt_values,
    prompt_lengths,
    completion_prompt,
    completion_lengths,
    targets,
    advantages,
    residual,
    out_proj,
    norm_gain,
    embedding,
):
    row_count, width = residual.shape
    comp_count = row_count // CLEN
    heads_here = queries.shape[1] // HDIM
    key_heads = own_keys.shape[1] // HDIM
    prompt_span = prompt_keys.shape[1]
    vocab_slab = embedding.shape[0]
    core = lax.axis_index("c")
    plane = lax.axis_index(("x", "y"))
    planes = XS * YS
    layer = lax.axis_index("z")
    layers = lax.axis_size("z")
    dp_index = plane * CS + core

    other_slab = lax.ppermute(embedding, "c", SWAP)

    held = jnp.concatenate([prompt_keys[0], prompt_values[0]], axis=1)
    arrived = spread(held, ("x", "y"))
    by_device = completion_prompt.reshape(planes * CS, comp_count)
    my_prompts = by_device[dp_index]
    partner_prompts = by_device[plane * CS + (1 - core)]
    mine = arrived[my_prompts // CS]
    for_partner = arrived[partner_prompts // CS]
    from_partner = lax.ppermute(for_partner, "c", SWAP)
    here = (my_prompts % CS) == core
    chosen = jnp.where(here[:, None, None], mine, from_partner)
    half = chosen.shape[2] // 2
    key_block = jnp.concatenate([chosen[:, :, :half], own_keys.reshape(comp_count, CLEN, -1)], axis=1)
    key_block = key_block.reshape(comp_count, prompt_span + CLEN, key_heads, HDIM)
    value_block = jnp.concatenate(
        [chosen[:, :, half:], own_values.reshape(comp_count, CLEN, -1)], axis=1
    )
    value_block = value_block.reshape(comp_count, prompt_span + CLEN, key_heads, HDIM)
    inside = jnp.arange(prompt_span)[None, :] < prompt_lengths[my_prompts][:, None]
    causal = jnp.arange(CLEN)[:, None] >= jnp.arange(CLEN)[None, :]
    visible = jnp.concatenate(
        [
            jnp.broadcast_to(inside[:, None, :], (comp_count, CLEN, prompt_span)),
            jnp.broadcast_to(causal[None], (comp_count, CLEN, CLEN)),
        ],
        axis=2,
    )
    attended = attend_local(
        queries.reshape(comp_count, CLEN, heads_here, HDIM), key_block, value_block, visible
    )
    partial_value = jnp.dot(attended, out_proj, preferred_element_type=jnp.float32)

    share = row_count // layers
    head_total = summed(partial_value, "z")
    my_residual = lax.dynamic_slice_in_dim(residual, layer * share, share)
    hidden = my_residual.astype(jnp.float32) + head_total
    norm_factor = lax.rsqrt(jnp.mean(hidden * hidden, axis=-1, keepdims=True) + norm_epsilon)
    normed = (hidden * norm_factor * norm_gain).astype(jnp.bfloat16)

    normed = spread(normed, "z").reshape(row_count, width)
    every_row = lax.all_gather(normed, ("x", "y"), axis=0, tiled=True)
    rows_here = planes * row_count

    contract_last = (((1,), (1,)), ((), ()))
    logits = [
        lax.dot_general(every_row, slab, contract_last, preferred_element_type=jnp.float32)
        for slab in (embedding, other_slab)
    ]
    my_targets = targets.reshape(planes, CS, row_count)[:, core].reshape(rows_here)
    column_ids = jnp.arange(vocab_slab, dtype=jnp.int32)
    hits = []
    for which in (core, 1 - core):
        slab_index = (plane * CS + which) * layers + layer
        local_target = my_targets - slab_index * vocab_slab
        hits.append(column_ids[None, :] == local_target[:, None])
    top = jnp.maximum(jnp.max(logits[0], axis=1), jnp.max(logits[1], axis=1))
    total = sum(jnp.sum(jnp.exp(part - top[:, None]), axis=1) for part in logits)
    picked = sum(jnp.sum(jnp.where(hit, part, 0.0), axis=1) for hit, part in zip(hits, logits))
    stats = jnp.stack([top, total, picked])
    stats = merged(spread(stats, "z"))
    stats = merged(spread(stats, ("x", "y")))
    log_total = stats[0] + jnp.log(stats[1])
    logprob = lax.dynamic_slice_in_dim(stats[2] - log_total, plane * row_count, row_count)

    position = jnp.arange(row_count, dtype=jnp.int32) % CLEN
    live_token = position[None, :] < jnp.repeat(
        completion_lengths.reshape(planes * CS, comp_count), CLEN, axis=1
    )
    weight_of = jnp.where(
        live_token, -jnp.repeat(advantages.reshape(planes * CS, comp_count), CLEN, axis=1), 0.0
    )
    token_weight = weight_of.reshape(planes, CS, row_count)[:, core].reshape(rows_here)
    grads = [
        (
            token_weight[:, None] * (hit.astype(jnp.float32) - jnp.exp(part - log_total[:, None]))
        ).astype(jnp.bfloat16)
        for hit, part in zip(hits, logits)
    ]
    terms = jnp.dot(grads[0], embedding, preferred_element_type=jnp.float32) + jnp.dot(
        grads[1], other_slab, preferred_element_type=jnp.float32
    )
    summed_rows = summed(terms.astype(jnp.bfloat16), ("x", "y"))
    normed_grad = summed(summed_rows, "z")
    hidden_grad = norm_gain * norm_factor * normed_grad - hidden * norm_factor**3 * jnp.mean(
        norm_gain * normed_grad * hidden, axis=-1, keepdims=True
    )
    hidden_grad = spread(hidden_grad, "z").reshape(row_count, width)
    return (logprob, hidden_grad)


def solution(mesh):
    fine = Mesh(mesh.devices.reshape(XS, YS, CS, -1), ("x", "y", "c", "z"))
    dp = ("x", "y", "c")
    placed = (
        P(dp, "z"),
        P(dp, "z"),
        P(dp, "z"),
        P(dp, None, "z"),
        P(dp, None, "z"),
        P(),
        P(),
        P(),
        P(),
        P(),
        P(dp, None),
        P("z", None),
        P(),
        P(dp + ("z",), None),
    )
    return jax.shard_map(
        body, mesh=fine, in_specs=placed, out_specs=(P(dp), P(dp, None)), check_vma=False
    )
```

time: 987 us -> 332 us (0.34); the launches traced: 968 us -> 329 us
  waiting for transfers between devices: 648 us -> 135 us
  local copies, waits for them, and re-layouts: 218 us -> 11 us
  blocking collectives: 37.6 us -> 101 us
  starting transfers between devices: 0.32 us -> 32.4 us
  loops' own time: 11.3 us -> 0 us
    all_gather x6 -> x1, waiting for transfers between devices: 466 us -> 57.5 us  [body(): every_row = lax.all_gather(normed, ('x', 'y'), axis=0, tiled=True)]
    dynamic_slice x511 -> x1, local copies, waits for them, and re-layouts: 205 us -> 0.59 us  [body(): lax.dynamic_slice_in_dim(stats[2] - log_total, plane * row_count, row_count)]
    reduce_scatter x1 -> x0, waiting for transfers between devices: 105 us -> none  [body(): lax.psum_scatter(jnp.dot(logit_grad, embedding, preferred_element_type=jn...]
    all_to_all x0 -> x3, blocking collectives: none -> 101 us  [the longest x2 84.6 us: summed(): arrived = lax.all_to_all(pieces, axes, 0, 0, tiled=True)]
    all_to_all x0 -> x5, waiting for transfers between devices: none -> 76.6 us  [the longest x4 55.4 us: spread(): return lax.all_to_all(copies, axes, 0, 0, tiled=True)]
    psum x1 -> x0, waiting for transfers between devices: 74.3 us -> none  [body(): head_total = lax.psum(partial_value, 'vocab')]
    psum x1 -> x0, blocking collectives: 37.6 us -> none  [body(): normed_grad = lax.psum(summed_rows, 'vocab')]
    all_to_all x0 -> x5, starting transfers between devices: none -> 32.2 us  [the longest x4 23.8 us: spread(): return lax.all_to_all(copies, axes, 0, 0, tiled=True)]
  transfers between devices with their start and end apart: 8 -> 8, of which waited for: 8 -> 7; matrix products, arithmetic and copies ran while one was open for 1% -> 3% of each run, Pallas kernels for 0% -> 0%
where the time goes in v1:
time: 332 us; the launch traced here: 329 us
  waiting for transfers between devices  135 us (41%)
  blocking collectives  101 us (30%)
  starting transfers between devices  32.4 us (10%)
  matrix products  30.8 us (9%)
  between operations  14.5 us (4%)
  local copies, waits for them, and re-layouts  11 us (3%)
  other arithmetic  3.64 us (1%)
    all_to_all x2, blocking collectives, summed(): arrived = lax.all_to_all(pieces, axes, 0, 0, tiled=True)  84.6 us
    all_gather x1, waiting for transfers between devices, body(): every_row = lax.all_gather(normed, ('x', 'y'), axis=0, tiled=True)  57.5 us
    all_to_all x4, waiting for transfers between devices, spread(): return lax.all_to_all(copies, axes, 0, 0, tiled=True)  55.4 us
    all_to_all x4, starting transfers between devices, spread(): return lax.all_to_all(copies, axes, 0, 0, tiled=True)  23.8 us
    all_to_all x1, waiting for transfers between devices, summed(): arrived = lax.all_to_all(pieces, axes, 0, 0, tiled=True)  21.3 us
    all_to_all x1, blocking collectives, spread(): return lax.all_to_all(copies, axes, 0, 0, tiled=True)  16.5 us
    dot_general x2, matrix products, body(): lax.dot_general(every_row, slab, contract_last, preferred_element_type=jn...  12.3 us
    all_to_all x1, starting transfers between devices, summed(): arrived = lax.all_to_all(pieces, axes, 0, 0, tiled=True)  8.47 us
  transfers between devices with their start and end apart: 8, of which 7 were waited for; matrix products, arithmetic and copies ran while one was open for 3% of the time, Pallas kernels for 0%

profile of v1, /device:TPU:2, one launch (start us, length us, event | category | flops | bytes accessed | tf_op | source)
XLA Modules:
  0.0 328.8 jit_solution(14387380070648966912)
XLA Ops:
  7.2 0.9 pad_maximum_fusion
  8.1 1.6 broadcast_in_dim.46
  9.7 7.5 %all-to-all-start = ((bf16[16,128,512]{2,1,0:T(8,128)(2,1)}), bf16[16,128,512]{2,1,0:T(8,128)(2,1)S(1)}, u32[]{:S(2)}, u32[]{:S(2)}) async-start(bf16[16,128,512]{2,1,0:T(8,128)(2,1)} %broadcast_in_dim.46), calls=%async_computation | async-start | bytes 4194304 | tf_op jit(solution)/shard_map/all_to_all | solution.py:19
  17.3 0.6 gather_fusion.2
  18.0 26.3 %all-to-all-done = bf16[16,128,512]{2,1,0:T(8,128)(2,1)S(1)} async-done(((bf16[16,128,512]{2,1,0:T(8,128)(2,1)}), bf16[16,128,512]{2,1,0:T(8,128)(2,1)S(1)}, u32[]{:S(2)}, u32[]{:S(2)}) %all-to-all-start) | async-done | bytes 2097184 | tf_op jit(solution)/shard_map/all_to_all | solution.py:19
  44.3 1.4 gather_fusion.1
  46.4 1.4 collective-permute-done
  48.7 1.2 fusion.51
  49.9 1.2 fusion.7
  51.2 4.4 %fusion.1 = f32[8,4,5376]{2,1,0:T(4,128)} fusion(bf16[8,4,512]{2,1,0:T(4,128)(2,1)S(1)} %convert_element_type.41, bf16[512,5376]{1,0:T(8,128)(2,1)} %param.25), kind=kOutput, calls=%fused_computation.6 | convolution fusion | flops 176160768 | bytes 6225920 | tf_op jit(solution)/shard_map/dot_general | solution.py:116
  55.6 8.5 %all-to-all-start.1 = ((f32[8,4,5376]{2,1,0:T(4,128)}), f32[8,4,5376]{2,1,0:T(4,128)S(1)}, u32[]{:S(2)}, u32[]{:S(2)}) async-start(f32[8,4,5376]{2,1,0:T(4,128)} %fusion.1), calls=%async_computation.1 | async-start | bytes 1376256 | tf_op jit(solution)/shard_map/all_to_all | solution.py:25
  64.1 21.3 %all-to-all-done.1 = f32[8,4,5376]{2,1,0:T(4,128)S(1)} async-done(((f32[8,4,5376]{2,1,0:T(4,128)}), f32[8,4,5376]{2,1,0:T(4,128)S(1)}, u32[]{:S(2)}, u32[]{:S(2)}) %all-to-all-start.1) | async-done | bytes 688160 | tf_op jit(solution)/shard_map/all_to_all | solution.py:25
  85.9 16.5 %all_to_all.40 = bf16[8,4,5376]{2,1,0:T(4,128)(2,1)S(1)} all-to-all(bf16[8,4,5376]{2,1,0:T(4,128)(2,1)S(1)} %broadcast_in_dim.52), channel_id=1, replica_groups=mesh['x'=4,'y'=4,'c'=2,'z'=8] {'z'}, dimensions={0} | all-to-all | bytes 688128 | tf_op jit(solution)/shard_map/all_to_all | solution.py:19
  102.4 0.8 reshape.387
  104.3 57.5 %all-gather.2.cloned.1.call-done = bf16[512,5376]{1,0:T(8,128)(2,1)} async-done(((bf16[32,5376]{1,0:T(8,128)(2,1)}), bf16[512,5376]{1,0:T(8,128)(2,1)}) %all-gather.2.cloned.1.call-update) | async-done | bytes 5505040 | tf_op jit(solution)/shard_map/all_gather | solution.py:126
  161.8 7.2 %fusion.52 = (f32[512]{0:T(512)S(1)}, f32[512,512]{0,1:T(8,128)S(1)}) fusion(bf16[512,5376]{1,0:T(8,128)(2,1)} %all-gather.2.cloned.1.call-done, bf16[512,5376]{1,0:T(8,128)(2,1)} %param.27), kind=kOutput, calls=%fused_computation.111 | convolution fusion | flops 2818833920 | bytes 12060672 | tf_op jit(solution)/shard_map/dot_general | solution.py:131
  169.0 5.1 %fusion.53 = (f32[512]{0:T(512)S(1)}, f32[512,512]{0,1:T(8,128)S(1)}) fusion(bf16[512,5376]{1,0:T(8,128)(2,1)S(1)} %copy-done.7, bf16[512,5376]{1,0:T(8,128)(2,1)} %collective-permute-done.1), kind=kOutput, calls=%fused_computation.112 | convolution fusion | flops 2818833920 | bytes 12060672 | tf_op jit(solution)/shard_map/dot_general | solution.py:131
  174.7 0.6 broadcast_in_dim.54
  175.3 7.0 %all-to-all-start.3 = ((f32[8,3,512]{2,1,0:T(4,128)}), f32[8,3,512]{2,1,0:T(4,128)S(1)}, u32[]{:S(2)}, u32[]{:S(2)}) async-start(f32[8,3,512]{2,1,0:T(4,128)} %broadcast_in_dim.54), calls=%async_computation.3 | async-start | bytes 131072 | tf_op jit(solution)/shard_map/all_to_all | solution.py:19
  182.3 8.4 %all-to-all-done.3 = f32[8,3,512]{2,1,0:T(4,128)S(1)} async-done(((f32[8,3,512]{2,1,0:T(4,128)}), f32[8,3,512]{2,1,0:T(4,128)S(1)}, u32[]{:S(2)}, u32[]{:S(2)}) %all-to-all-start.3) | async-done | bytes 49184 | tf_op jit(solution)/shard_map/all_to_all | solution.py:19
  190.8 0.7 broadcast_in_dim.55
  191.5 5.7 %all-to-all-start.4 = ((f32[16,3,512]{2,1,0:T(4,128)}), f32[16,3,512]{2,1,0:T(4,128)S(1)}, u32[]{:S(2)}, u32[]{:S(2)}) async-start(f32[16,3,512]{2,1,0:T(4,128)} %broadcast_in_dim.55), calls=%async_computation.4 | async-start | bytes 262144 | tf_op jit(solution)/shard_map/all_to_all | solution.py:19
  197.3 6.3 %all-to-all-done.4 = f32[16,3,512]{2,1,0:T(4,128)S(1)} async-done(((f32[16,3,512]{2,1,0:T(4,128)}), f32[16,3,512]{2,1,0:T(4,128)S(1)}, u32[]{:S(2)}, u32[]{:S(2)}) %all-to-all-start.4) | async-done | bytes 98336 | tf_op jit(solution)/shard_map/all_to_all | solution.py:19
  203.7 5.4 %fusion.8 = f32[512,5376]{1,0:T(8,128)S(1)} fusion(bf16[512,5376]{1,0:T(8,128)(2,1)} %param.27, f32[512,512]{0,1:T(8,128)S(1)} %get-tuple-element.30, f32[512]{0:T(512)S(1)} %get-tuple-element.15, f32[512]{0:T(512)S(1)} %mul.133, s32[512]{0:T(512)S(1)} %sub.111), kind=kOutput, calls=%fused_computation.23 | convolution fusion | flops 2820145152 | bytes 17569792 | tf_op jit(solution)/shard_map/dot_general | solution.py:164
  209.1 6.3 %add_convert_fusion = bf16[512,5376]{1,0:T(8,128)(2,1)S(1)} fusion(f32[512,5376]{1,0:T(8,128)S(1)} %fusion.8, bf16[512,5376]{1,0:T(8,128)(2,1)} %collective-permute-done.1, f32[512,512]{0,1:T(8,128)S(1)} %get-tuple-element.32, f32[512]{0:T(512)S(1)} %get-tuple-element.15, f32[512]{0:T(512)S(1)} %mul.133, s32[512]{0:T(512)S(1)} %sub.114), kind=kOutput, calls=%fused_computation.5 | convolution fusion | flops 2825650176 | bytes 23074816 | tf_op jit(solution)/shard_map/dot_general | solution.py:164
  215.4 65.3 %all_to_all.41 = bf16[16,32,5376]{2,1,0:T(8,128)(2,1)S(1)} all-to-all(bf16[16,32,5376]{2,1,0:T(8,128)(2,1)S(1)} %bitcast.113), channel_id=1, replica_groups=mesh['x'=4,'y'=4,'c'=2,'z'=8] {'x','y'}, dimensions={0} | all-to-all | bytes 11010048 | tf_op jit(solution)/shard_map/all_to_all | solution.py:25
  280.8 0.8 convert_reduce_fusion
  281.8 19.2 %all_to_all.42 = f32[8,4,5376]{2,1,0:T(4,128)S(1)} all-to-all(f32[8,4,5376]{2,1,0:T(4,128)S(1)} %reshape.392), channel_id=1, replica_groups=mesh['x'=4,'y'=4,'c'=2,'z'=8] {'z'}, dimensions={0} | all-to-all | bytes 1376256 | tf_op jit(solution)/shard_map/all_to_all | solution.py:25
  301.4 0.9 broadcast_in_dim.59
  302.4 3.5 %all-to-all-start.7 = ((f32[8,4,5376]{2,1,0:T(4,128)}), f32[8,4,5376]{2,1,0:T(4,128)S(1)}, u32[]{:S(2)}, u32[]{:S(2)}) async-start(f32[8,4,5376]{2,1,0:T(4,128)} %broadcast_in_dim.59), calls=%async_computation.7 | async-start | bytes 1376256 | tf_op jit(solution)/shard_map/all_to_all | solution.py:19
  306.5 14.4 %all-to-all-done.7 = f32[8,4,5376]{2,1,0:T(4,128)S(1)} async-done(((f32[8,4,5376]{2,1,0:T(4,128)}), f32[8,4,5376]{2,1,0:T(4,128)S(1)}, u32[]{:S(2)}, u32[]{:S(2)}) %all-to-all-start.7) | async-done | bytes 688160 | tf_op jit(solution)/shard_map/all_to_all | solution.py:19
  320.9 1.1 reshape.393
  (79 shorter events, 5.4 us)
Async XLA Ops:
  7.2 41.5 %copy-start = (bf16[32,512]{1,0:T(8,128)(2,1)S(1)}, bf16[32,512]{1,0:T(8,128)(2,1)}, u32[]{:S(2)}) copy-start(bf16[32,512]{1,0:T(8,128)(2,1)} %param.14) | copy-start | bytes 98308
  7.2 10.0 %copy-start.5 = (s32[128]{0:T(128)S(1)}, s32[128]{0:T(128)}, u32[]{:S(2)}) copy-start(s32[128]{0:T(128)} %param.20) | copy-start | bytes 1540
  7.2 10.1 %copy-start.1 = (s32[32]{0:T(128)S(1)}, s32[32]{0:T(128)}, u32[]{:S(2)}) copy-start(s32[32]{0:T(128)} %param.19) | copy-start | bytes 388
  9.7 34.6 %all-to-all-start = ((bf16[16,128,512]{2,1,0:T(8,128)(2,1)}), bf16[16,128,512]{2,1,0:T(8,128)(2,1)S(1)}, u32[]{:S(2)}, u32[]{:S(2)}) async-start(bf16[16,128,512]{2,1,0:T(8,128)(2,1)} %broadcast_in_dim.46), calls=%async_computation | async-start | bytes 4194304 | tf_op jit(solution)/shard_map/all_to_all | solution.py:19
  45.7 2.1 collective-permute-start
  48.7 36.8 %copy-start.3 = (bf16[32,5376]{1,0:T(8,128)(2,1)S(1)}, bf16[32,5376]{1,0:T(8,128)(2,1)}, u32[]{:S(2)}) copy-start(bf16[32,5376]{1,0:T(8,128)(2,1)} %param.24) | copy-start | bytes 1032196
  48.7 37.0 %copy-start.2 = (f32[5376]{0:T(1024)S(1)}, f32[5376]{0:T(1024)}, u32[]{:S(2)}) copy-start(f32[5376]{0:T(1024)} %param.26) | copy-start | bytes 64516
  51.1 52.2 %copy-start.8 = (f32[128]{0:T(128)S(1)}, f32[128]{0:T(128)}, u32[]{:S(2)}) copy-start(f32[128]{0:T(128)} %param.23) | copy-start | bytes 1540
  51.1 52.3 %copy-start.6 = (s32[128]{0:T(128)S(1)}, s32[128]{0:T(128)}, u32[]{:S(2)}) copy-start(s32[128]{0:T(128)} %param.21) | copy-start | bytes 1540
  51.1 52.4 %copy-start.4 = (s32[1024]{0:T(1024)S(1)}, s32[1024]{0:T(1024)}, u32[]{:S(2)}) copy-start(s32[1024]{0:T(1024)} %param.22) | copy-start | bytes 12292
  55.6 29.8 %all-to-all-start.1 = ((f32[8,4,5376]{2,1,0:T(4,128)}), f32[8,4,5376]{2,1,0:T(4,128)S(1)}, u32[]{:S(2)}, u32[]{:S(2)}) async-start(f32[8,4,5376]{2,1,0:T(4,128)} %fusion.1), calls=%async_computation.1 | async-start | bytes 1376256 | tf_op jit(solution)/shard_map/all_to_all | solution.py:25
  64.1 97.7 %all-gather.2.cloned.1.call-start = ((), (), s32[]{:S(2)}) async-start(), calls=%async_computation.8 | async-start | bytes 5849088 | tf_op jit(solution)/shard_map/all_gather | solution.py:126
  103.2 65.8 %collective-permute-start.1 = (bf16[512,5376]{1,0:T(8,128)(2,1)}, bf16[512,5376]{1,0:T(8,128)(2,1)}, u32[]{:S(2)}, u32[]{:S(2)}) collective-permute-start(bf16[512,5376]{1,0:T(8,128)(2,1)} %param.27), channel_id=1, source_target_pairs={{0,8},{8,0},{1,9},{9,1},{2,10},{10,2},{3,11},{11,3},{4,12},{12,4},... | collective-permute-start | bytes 16515080 | tf_op jit(solution)/shard_map/ppermute | solution.py:85
  161.8 7.2 %copy-start.7 = (bf16[512,5376]{1,0:T(8,128)(2,1)S(1)}, bf16[512,5376]{1,0:T(8,128)(2,1)}, u32[]{:S(2)}) copy-start(bf16[512,5376]{1,0:T(8,128)(2,1)} %all-gather.2.cloned.1.call-done) | copy-start | bytes 16515076
  175.3 15.4 %all-to-all-start.3 = ((f32[8,3,512]{2,1,0:T(4,128)}), f32[8,3,512]{2,1,0:T(4,128)S(1)}, u32[]{:S(2)}, u32[]{:S(2)}) async-start(f32[8,3,512]{2,1,0:T(4,128)} %broadcast_in_dim.54), calls=%async_computation.3 | async-start | bytes 131072 | tf_op jit(solution)/shard_map/all_to_all | solution.py:19
  191.5 12.1 %all-to-all-start.4 = ((f32[16,3,512]{2,1,0:T(4,128)}), f32[16,3,512]{2,1,0:T(4,128)S(1)}, u32[]{:S(2)}, u32[]{:S(2)}) async-start(f32[16,3,512]{2,1,0:T(4,128)} %broadcast_in_dim.55), calls=%async_computation.4 | async-start | bytes 262144 | tf_op jit(solution)/shard_map/all_to_all | solution.py:19
  302.4 18.5 %all-to-all-start.7 = ((f32[8,4,5376]{2,1,0:T(4,128)}), f32[8,4,5376]{2,1,0:T(4,128)S(1)}, u32[]{:S(2)}, u32[]{:S(2)}) async-start(f32[8,4,5376]{2,1,0:T(4,128)} %broadcast_in_dim.59), calls=%async_computation.7 | async-start | bytes 1376256 | tf_op jit(solution)/shard_map/all_to_all | solution.py:19
Sparse Core Ops, SparseCore 0:
  103.3 58.3 all-gather.1

commit v2 on v1

--- a/solution.py
+++ b/solution.py
@@ -11,6 +11,7 @@
 score_scale = 168.0 ** (-0.5)
 norm_epsilon = 1e-06
 SWAP = ((0, 1), (1, 0))
+Z = ("zh", "zl")
 
 
 def spread(part, axes):
@@ -78,11 +79,28 @@
     core = lax.axis_index("c")
     plane = lax.axis_index(("x", "y"))
     planes = XS * YS
-    layer = lax.axis_index("z")
-    layers = lax.axis_size("z")
+    layer = lax.axis_index(Z)
+    layers = lax.axis_size(Z)
+    parity = lax.axis_index("zl")
     dp_index = plane * CS + core
 
-    other_slab = lax.ppermute(embedding, "c", SWAP)
+    half_slab = vocab_slab // 2
+    ring = range(layers)
+    from_next = lax.ppermute(embedding[:half_slab], Z, [((k + 1) % layers, k) for k in ring])
+    from_prev = lax.ppermute(embedding[half_slab:], Z, [(k, (k + 1) % layers) for k in ring])
+    near = jnp.concatenate([from_next, from_prev], axis=0)
+    table = jnp.concatenate(
+        [embedding, lax.ppermute(embedding, "c", SWAP), near, lax.ppermute(near, "c", SWAP)], axis=0
+    )
+    slab_column = jnp.arange(vocab_slab, dtype=jnp.int32)
+    near_layer = jnp.where(slab_column < half_slab, layer + 1, layer - 1) % layers
+    entry = jnp.concatenate(
+        [
+            ((plane * CS + which) * layers + held_layer) * vocab_slab + slab_column
+            for held_layer in (layer, near_layer)
+            for which in (core, 1 - core)
+        ]
+    )
 
     held = jnp.concatenate([prompt_keys[0], prompt_values[0]], axis=1)
     arrived = spread(held, ("x", "y"))
@@ -116,81 +134,69 @@
     partial_value = jnp.dot(attended, out_proj, preferred_element_type=jnp.float32)
 
     share = row_count // layers
-    head_total = summed(partial_value, "z")
+    head_total = summed(partial_value, Z)
     my_residual = lax.dynamic_slice_in_dim(residual, layer * share, share)
     hidden = my_residual.astype(jnp.float32) + head_total
     norm_factor = lax.rsqrt(jnp.mean(hidden * hidden, axis=-1, keepdims=True) + norm_epsilon)
     normed = (hidden * norm_factor * norm_gain).astype(jnp.bfloat16)
 
-    normed = spread(normed, "z").reshape(row_count, width)
-    every_row = lax.all_gather(normed, ("x", "y"), axis=0, tiled=True)
-    rows_here = planes * row_count
-
-    contract_last = (((1,), (1,)), ((), ()))
-    logits = [
-        lax.dot_general(every_row, slab, contract_last, preferred_element_type=jnp.float32)
-        for slab in (embedding, other_slab)
-    ]
-    my_targets = targets.reshape(planes, CS, row_count)[:, core].reshape(rows_here)
-    column_ids = jnp.arange(vocab_slab, dtype=jnp.int32)
-    hits = []
-    for which in (core, 1 - core):
-        slab_index = (plane * CS + which) * layers + layer
-        local_target = my_targets - slab_index * vocab_slab
-        hits.append(column_ids[None, :] == local_target[:, None])
-    top = jnp.maximum(jnp.max(logits[0], axis=1), jnp.max(logits[1], axis=1))
-    total = sum(jnp.sum(jnp.exp(part - top[:, None]), axis=1) for part in logits)
-    picked = sum(jnp.sum(jnp.where(hit, part, 0.0), axis=1) for hit, part in zip(hits, logits))
+    pairs = layers // 2
+    normed = spread(normed, "zh").reshape(pairs * share, width)
+    rows_here = planes * pairs * share
+    every_row = spread(normed, ("x", "y")).reshape(rows_here, width)
+
+    def of_rows(values):
+        return values.reshape(planes, CS, pairs, 2, share)[:, core, :, parity].reshape(rows_here)
+
+    logits = lax.dot_general(
+        every_row, table, (((1,), (1,)), ((), ())), preferred_element_type=jnp.float32
+    )
+    hit = entry[None, :] == of_rows(targets)[:, None]
+    top = jnp.max(logits, axis=1)
+    total = jnp.sum(jnp.exp(logits - top[:, None]), axis=1)
+    picked = jnp.sum(jnp.where(hit, logits, 0.0), axis=1)
     stats = jnp.stack([top, total, picked])
-    stats = merged(spread(stats, "z"))
+    stats = merged(spread(stats, "zh"))
     stats = merged(spread(stats, ("x", "y")))
     log_total = stats[0] + jnp.log(stats[1])
-    logprob = lax.dynamic_slice_in_dim(stats[2] - log_total, plane * row_count, row_count)
-
-    position = jnp.arange(row_count, dtype=jnp.int32) % CLEN
-    live_token = position[None, :] < jnp.repeat(
-        completion_lengths.reshape(planes * CS, comp_count), CLEN, axis=1
-    )
-    weight_of = jnp.where(
-        live_token, -jnp.repeat(advantages.reshape(planes * CS, comp_count), CLEN, axis=1), 0.0
-    )
-    token_weight = weight_of.reshape(planes, CS, row_count)[:, core].reshape(rows_here)
-    grads = [
-        (
-            token_weight[:, None] * (hit.astype(jnp.float32) - jnp.exp(part - log_total[:, None]))
-        ).astype(jnp.bfloat16)
-        for hit, part in zip(hits, logits)
-    ]
-    terms = jnp.dot(grads[0], embedding, preferred_element_type=jnp.float32) + jnp.dot(
-        grads[1], other_slab, preferred_element_type=jnp.float32
-    )
+    first_row = (plane * pairs + lax.axis_index("zh")) * share
+    logprob = lax.dynamic_slice_in_dim(stats[2] - log_total, first_row, share)
+    logprob = spread(logprob, Z).reshape(row_count)
+
+    row_ids = jnp.arange(targets.shape[0], dtype=jnp.int32)
+    live_token = row_ids % CLEN < jnp.repeat(completion_lengths, CLEN)
+    token_weight = of_rows(jnp.where(live_token, -jnp.repeat(advantages, CLEN), 0.0))
+    logit_grad = (
+        token_weight[:, None] * (hit.astype(jnp.float32) - jnp.exp(logits - log_total[:, None]))
+    ).astype(jnp.bfloat16)
+    terms = jnp.dot(logit_grad, table, preferred_element_type=jnp.float32)
     summed_rows = summed(terms.astype(jnp.bfloat16), ("x", "y"))
-    normed_grad = summed(summed_rows, "z")
+    normed_grad = summed(summed_rows, "zh")
     hidden_grad = norm_gain * norm_factor * normed_grad - hidden * norm_factor**3 * jnp.mean(
         norm_gain * normed_grad * hidden, axis=-1, keepdims=True
     )
-    hidden_grad = spread(hidden_grad, "z").reshape(row_count, width)
-    return (logprob, hidden_grad)
+    hidden_grad = spread(hidden_grad.astype(jnp.bfloat16), Z).reshape(row_count, width)
+    return (logprob, hidden_grad.astype(jnp.float32))
 
 
 def solution(mesh):
-    fine = Mesh(mesh.devices.reshape(XS, YS, CS, -1), ("x", "y", "c", "z"))
+    fine = Mesh(mesh.devices.reshape(XS, YS, CS, -1, 2), ("x", "y", "c") + Z)
     dp = ("x", "y", "c")
     placed = (
-        P(dp, "z"),
-        P(dp, "z"),
-        P(dp, "z"),
-        P(dp, None, "z"),
-        P(dp, None, "z"),
+        P(dp, Z),
+        P(dp, Z),
+        P(dp, Z),
+        P(dp, None, Z),
+        P(dp, None, Z),
         P(),
         P(),
         P(),
         P(),
         P(),
         P(dp, None),
-        P("z", None),
-        P(),
-        P(dp + ("z",), None),
+        P(Z, None),
+        P(),
+        P(dp + Z, None),
     )
     return jax.shard_map(
         body, mesh=fine, in_specs=placed, out_specs=(P(dp), P(dp, None)), check_vma=False

time: 332 us -> 291 us (0.88)
  blocking collectives: 101 us -> 33.4 us
  local copies, waits for them, and re-layouts: 11 us -> 41.2 us
  starting transfers between devices: 32.4 us -> 57.3 us
  waiting for transfers between devices: 135 us -> 117 us
  between operations: 14.5 us -> 1.16 us
  other arithmetic: 3.64 us -> 9.83 us
    all_gather x1 -> x0, waiting for transfers between devices: 57.5 us -> none  [body(): every_row = lax.all_gather(normed, ('x', 'y'), axis=0, tiled=True)]
    all_to_all x2 -> x1, blocking collectives: 84.6 us -> 33.4 us  [summed(): arrived = lax.all_to_all(pieces, axes, 0, 0, tiled=True)]
    ppermute x1 -> x4, waiting for transfers between devices: 0.01 us -> 35.2 us  [the longest x1 35.2 us: body(): lax.ppermute(embedding[:half_slab], Z, [((k + 1) % layers, k) for k in ri...]
    unnamed x18 -> x38, local copies, waits for them, and re-layouts: 0.05 us -> 16.6 us
    all_to_all x1 -> x0, blocking collectives: 16.5 us -> none  [spread(): return lax.all_to_all(copies, axes, 0, 0, tiled=True)]
    all_to_all x4 -> x7, starting transfers between devices: 23.8 us -> 39.4 us  [spread(): return lax.all_to_all(copies, axes, 0, 0, tiled=True)]
    all_to_all x4 -> x7, waiting for transfers between devices: 55.4 us -> 70.7 us  [spread(): return lax.all_to_all(copies, axes, 0, 0, tiled=True)]
    all_to_all x1 -> x2, waiting for transfers between devices: 21.3 us -> 9.5 us  [summed(): arrived = lax.all_to_all(pieces, axes, 0, 0, tiled=True)]
  transfers between devices with their start and end apart: 8 -> 14, of which waited for: 7 -> 10; matrix products, arithmetic and copies ran while one was open for 3% -> 16% of each run, Pallas kernels for 0% -> 0%
where the time goes in v2:
time: 291 us; the launch traced here: 290 us
  waiting for transfers between devices  117 us (40%)
  starting transfers between devices  57.3 us (20%)
  local copies, waits for them, and re-layouts  41.2 us (14%)
  blocking collectives  33.4 us (11%)
  matrix products  29.9 us (10%)
  other arithmetic  9.83 us (3%)
    all_to_all x7, waiting for transfers between devices, spread(): return lax.all_to_all(copies, axes, 0, 0, tiled=True)  70.7 us
    all_to_all x7, starting transfers between devices, spread(): return lax.all_to_all(copies, axes, 0, 0, tiled=True)  39.4 us
    ppermute x1, waiting for transfers between devices, body(): lax.ppermute(embedding[:half_slab], Z, [((k + 1) % layers, k) for k in ri...  35.2 us
    all_to_all x1, blocking collectives, summed(): arrived = lax.all_to_all(pieces, axes, 0, 0, tiled=True)  33.4 us
    unnamed x38, local copies, waits for them, and re-layouts  16.6 us
    dot_general x1, matrix products, body(): terms = jnp.dot(logit_grad, table, preferred_element_type=jnp.float32)  14.2 us
    all_to_all x2, starting transfers between devices, summed(): arrived = lax.all_to_all(pieces, axes, 0, 0, tiled=True)  12.1 us
    dot_general x1, matrix products, body(): lax.dot_general(every_row, table, (((1,), (1,)), ((), ())), preferred_ele...  10.4 us
  transfers between devices with their start and end apart: 14, of which 10 were waited for; matrix products, arithmetic and copies ran while one was open for 16% of the time, Pallas kernels for 0%

profile of v2, /device:TPU:2, one launch (start us, length us, event | category | flops | bytes accessed | tf_op | source)
XLA Modules:
  0.0 289.5 jit_solution(10164192638563920110)
XLA Ops:
  1.5 1.6 broadcast_in_dim.62
  3.1 7.5 %all-to-all-start = ((bf16[16,128,512]{2,1,0:T(8,128)(2,1)}), bf16[16,128,512]{2,1,0:T(8,128)(2,1)S(1)}, u32[]{:S(2)}, u32[]{:S(2)}) async-start(bf16[16,128,512]{2,1,0:T(8,128)(2,1)} %broadcast_in_dim.62), calls=%async_computation | async-start | bytes 4194304 | tf_op jit(solution)/shard_map/all_to_all | solution.py:20
  10.6 5.4 %fusion.56 = (bf16[256,5376]{1,0:T(8,128)(2,1)}, bf16[256,5376]{1,0:T(8,128)(2,1)}) fusion(bf16[512,5376]{1,0:T(8,128)(2,1)} %param.27), kind=kLoop, calls=%fused_computation.129 | loop fusion | bytes 11010048 | tf_op jit(solution)/shard_map/slice | solution.py:90
  16.0 5.9 %collective-permute-start.2 = (bf16[256,5376]{1,0:T(8,128)(2,1)}, bf16[256,5376]{1,0:T(8,128)(2,1)}, u32[]{:S(2)}, u32[]{:S(2)}) collective-permute-start(bf16[256,5376]{1,0:T(8,128)(2,1)} %get-tuple-element.11), channel_id=1, source_target_pairs={{1,0},{2,1},{3,2},{4,3},{5,4},{6,5},{7,6},{0,7},{9,8},{10,9},{11,1... | collective-permute-start | bytes 8257544 | tf_op jit(solution)/shard_map/ppermute | solution.py:89
  22.8 14.9 %all-to-all-done = bf16[16,128,512]{2,1,0:T(8,128)(2,1)S(1)} async-done(((bf16[16,128,512]{2,1,0:T(8,128)(2,1)}), bf16[16,128,512]{2,1,0:T(8,128)(2,1)S(1)}, u32[]{:S(2)}, u32[]{:S(2)}) %all-to-all-start) | async-done | bytes 2097184 | tf_op jit(solution)/shard_map/all_to_all | solution.py:20
  43.1 4.4 %fusion.1 = f32[8,4,5376]{2,1,0:T(4,128)} fusion(bf16[8,4,512]{2,1,0:T(4,128)(2,1)S(1)} %convert_element_type.44, bf16[512,5376]{1,0:T(8,128)(2,1)} %param.25), kind=kOutput, calls=%fused_computation.6 | convolution fusion | flops 176160768 | bytes 6225920 | tf_op jit(solution)/shard_map/dot_general | solution.py:134
  47.5 8.6 %all-to-all-start.1 = ((f32[8,4,5376]{2,1,0:T(4,128)}), f32[8,4,5376]{2,1,0:T(4,128)S(1)}, u32[]{:S(2)}, u32[]{:S(2)}) async-start(f32[8,4,5376]{2,1,0:T(4,128)} %fusion.1), calls=%async_computation.1 | async-start | bytes 1376256 | tf_op jit(solution)/shard_map/all_to_all | solution.py:26
  56.1 35.2 %collective-permute-done.2 = bf16[256,5376]{1,0:T(8,128)(2,1)} collective-permute-done((bf16[256,5376]{1,0:T(8,128)(2,1)}, bf16[256,5376]{1,0:T(8,128)(2,1)}, u32[]{:S(2)}, u32[]{:S(2)}) %collective-permute-start.2) | collective-permute-done | bytes 2752544 | tf_op jit(solution)/shard_map/ppermute | solution.py:89
  91.3 5.4 %pad_maximum_fusion = bf16[512,5376]{1,0:T(8,128)(2,1)} fusion(bf16[256,5376]{1,0:T(8,128)(2,1)} %collective-permute-done.3, bf16[256,5376]{1,0:T(8,128)(2,1)} %collective-permute-done.2), kind=kLoop, calls=%fused_computation.5 | loop fusion | flops 11010048 | bytes 11010048 | tf_op jit(solution)/shard_map/concatenate | solution.py:91
  96.8 2.7 constant_dynamic-update-slice_fusion.4
  101.2 3.4 %all-to-all-start.2 = ((bf16[4,4,5376]{2,1,0:T(4,128)(2,1)}), bf16[4,4,5376]{2,1,0:T(4,128)(2,1)S(1)}, u32[]{:S(2)}, u32[]{:S(2)}) async-start(bf16[4,4,5376]{2,1,0:T(4,128)(2,1)} %broadcast_in_dim.67), calls=%async_computation.2 | async-start | bytes 344064 | tf_op jit(solution)/shard_map/all_to_all | solution.py:20
  105.3 9.4 %all-to-all-done.2 = bf16[4,4,5376]{2,1,0:T(4,128)(2,1)S(1)} async-done(((bf16[4,4,5376]{2,1,0:T(4,128)(2,1)}), bf16[4,4,5376]{2,1,0:T(4,128)(2,1)S(1)}, u32[]{:S(2)}, u32[]{:S(2)}) %all-to-all-start.2) | async-done | bytes 172064 | tf_op jit(solution)/shard_map/all_to_all | solution.py:20
  114.8 1.7 broadcast_in_dim.69
  116.6 7.2 %all-to-all-start.3 = ((bf16[16,16,5376]{2,1,0:T(8,128)(2,1)}), bf16[16,16,5376]{2,1,0:T(8,128)(2,1)S(1)}, u32[]{:S(2)}, u32[]{:S(2)}) async-start(bf16[16,16,5376]{2,1,0:T(8,128)(2,1)} %broadcast_in_dim.69), calls=%async_computation.3 | async-start | bytes 5505024 | tf_op jit(solution)/shard_map/all_to_all | solution.py:20
  123.8 5.4 %constant_dynamic-update-slice_fusion.3 = bf16[2048,5376]{1,0:T(8,128)(2,1)} fusion(bf16[2048,5376]{1,0:T(8,128)(2,1)} %constant_dynamic-update-slice_fusion.4, bf16[512,5376]{1,0:T(8,128)(2,1)} %collective-permute-done.1), kind=kLoop, calls=%fused_computation.61 | loop fusion | bytes 11010048
  129.2 3.6 %constant_dynamic-update-slice_fusion.2 = bf16[2048,5376]{1,0:T(8,128)(2,1)} fusion(bf16[2048,5376]{1,0:T(8,128)(2,1)} %constant_dynamic-update-slice_fusion.3, bf16[256,5376]{1,0:T(8,128)(2,1)} %collective-permute-done.2), kind=kLoop, calls=%fused_computation.60 | loop fusion | bytes 5505024
  132.7 3.5 %constant_dynamic-update-slice_fusion.1 = bf16[2048,5376]{1,0:T(8,128)(2,1)} fusion(bf16[2048,5376]{1,0:T(8,128)(2,1)} %constant_dynamic-update-slice_fusion.2, bf16[256,5376]{1,0:T(8,128)(2,1)} %collective-permute-done.3), kind=kLoop, calls=%fused_computation.59 | loop fusion | bytes 5505024
  136.2 5.3 %constant_dynamic-update-slice_fusion = bf16[2048,5376]{1,0:T(8,128)(2,1)} fusion(bf16[2048,5376]{1,0:T(8,128)(2,1)} %constant_dynamic-update-slice_fusion.1, bf16[512,5376]{1,0:T(8,128)(2,1)} %collective-permute-done.4), kind=kLoop, calls=%fused_computation.58 | loop fusion | bytes 11010048 | tf_op jit(solution)/shard_map/concatenate | solution.py:92
  141.5 15.8 %all-to-all-done.3 = bf16[16,16,5376]{2,1,0:T(8,128)(2,1)S(1)} async-done(((bf16[16,16,5376]{2,1,0:T(8,128)(2,1)}), bf16[16,16,5376]{2,1,0:T(8,128)(2,1)S(1)}, u32[]{:S(2)}, u32[]{:S(2)}) %all-to-all-start.3) | async-done | bytes 2752544 | tf_op jit(solution)/shard_map/all_to_all | solution.py:20
  157.3 10.4 %fusion.60 = (f32[256]{0:T(256)S(1)}, f32[256,2048]{1,0:T(8,128)S(1)}) fusion(bf16[256,5376]{1,0:T(8,128)(2,1)S(1)} %bitcast.115, bf16[2048,5376]{1,0:T(8,128)(2,1)} %constant_dynamic-update-slice_fusion), kind=kOutput, calls=%fused_computation.133 | convolution fusion | flops 5637668864 | bytes 26870784 | tf_op jit(solution)/shard_map/dot_general | solution.py:151
  170.3 4.2 %all-to-all-start.4 = ((f32[4,3,256]{2,1,0:T(4,128)}), f32[4,3,256]{2,1,0:T(4,128)S(1)}, u32[]{:S(2)}, u32[]{:S(2)}) async-start(f32[4,3,256]{2,1,0:T(4,128)} %broadcast_in_dim.74), calls=%async_computation.4 | async-start | bytes 32768 | tf_op jit(solution)/shard_map/all_to_all | solution.py:20
  174.5 7.8 %all-to-all-done.4 = f32[4,3,256]{2,1,0:T(4,128)S(1)} async-done(((f32[4,3,256]{2,1,0:T(4,128)}), f32[4,3,256]{2,1,0:T(4,128)S(1)}, u32[]{:S(2)}, u32[]{:S(2)}) %all-to-all-start.4) | async-done | bytes 12320 | tf_op jit(solution)/shard_map/all_to_all | solution.py:20
  183.0 7.4 %all-to-all-start.5 = ((f32[16,3,256]{2,1,0:T(4,128)}), f32[16,3,256]{2,1,0:T(4,128)S(1)}, u32[]{:S(2)}, u32[]{:S(2)}) async-start(f32[16,3,256]{2,1,0:T(4,128)} %broadcast_in_dim.75), calls=%async_computation.5 | async-start | bytes 131072 | tf_op jit(solution)/shard_map/all_to_all | solution.py:20
  190.7 6.0 %all-to-all-done.5 = f32[16,3,256]{2,1,0:T(4,128)S(1)} async-done(((f32[16,3,256]{2,1,0:T(4,128)}), f32[16,3,256]{2,1,0:T(4,128)S(1)}, u32[]{:S(2)}, u32[]{:S(2)}) %all-to-all-start.5) | async-done | bytes 49184 | tf_op jit(solution)/shard_map/all_to_all | solution.py:20
  196.8 14.2 %convolution_convert_fusion = bf16[256,5376]{1,0:T(8,128)(2,1)S(1)} fusion(bf16[2048,5376]{1,0:T(8,128)(2,1)} %constant_dynamic-update-slice_fusion, f32[256,2048]{1,0:T(8,128)} %copy-done.3, f32[256]{0:T(256)S(1)} %get-tuple-element.9, f32[256]{0:T(256)S(1)} %mul.147, s32[2048]{0:T(1024)S(1)} %pad_add_fusion.1, s32[256]{0:T(256)S(1)} %eq.34), kind=kOutput, calls=%fused_computation.4 | convolution fusion | flops 5641666560 | bytes 26881024 | tf_op jit(solution)/shard_map/dot_general | solution.py:172
  211.0 33.4 %all_to_all.51 = bf16[16,16,5376]{2,1,0:T(8,128)(2,1)S(1)} all-to-all(bf16[16,16,5376]{2,1,0:T(8,128)(2,1)S(1)} %bitcast.116), channel_id=1, replica_groups=mesh['x'=4,'y'=4,'c'=2,'zh'=4,'zl'=2] {'x','y'}, dimensions={0} | all-to-all | bytes 5505024 | tf_op jit(solution)/shard_map/all_to_all | solution.py:26
  245.6 3.5 %all-to-all-start.8 = ((f32[4,4,5376]{2,1,0:T(4,128)}), f32[4,4,5376]{2,1,0:T(4,128)S(1)}, u32[]{:S(2)}, u32[]{:S(2)}) async-start(f32[4,4,5376]{2,1,0:T(4,128)} %reshape.338), calls=%async_computation.8 | async-start | bytes 688128 | tf_op jit(solution)/shard_map/all_to_all | solution.py:26
  249.1 9.5 %all-to-all-done.8 = f32[4,4,5376]{2,1,0:T(4,128)S(1)} async-done(((f32[4,4,5376]{2,1,0:T(4,128)}), f32[4,4,5376]{2,1,0:T(4,128)S(1)}, u32[]{:S(2)}, u32[]{:S(2)}) %all-to-all-start.8) | async-done | bytes 344096 | tf_op jit(solution)/shard_map/all_to_all | solution.py:26
  259.2 6.2 %all-to-all-start.6 = ((f32[8,1,4]{2,1,0:T(1,128)}), f32[8,1,4]{2,1,0:T(1,128)S(1)}, u32[]{:S(2)}, u32[]{:S(2)}) async-start(f32[8,1,4]{2,1,0:T(1,128)} %broadcast_in_dim.76), calls=%async_computation.6 | async-start | bytes 8192 | tf_op jit(solution)/shard_map/all_to_all | solution.py:20
  265.9 7.2 %all-to-all-done.6 = f32[8,1,4]{2,1,0:T(1,128)S(1)} async-done(((f32[8,1,4]{2,1,0:T(1,128)}), f32[8,1,4]{2,1,0:T(1,128)S(1)}, u32[]{:S(2)}, u32[]{:S(2)}) %all-to-all-start.6) | async-done | bytes 160 | tf_op jit(solution)/shard_map/all_to_all | solution.py:20
  273.9 3.4 %all-to-all-start.9 = ((bf16[8,4,5376]{2,1,0:T(4,128)(2,1)}), bf16[8,4,5376]{2,1,0:T(4,128)(2,1)S(1)}, u32[]{:S(2)}, u32[]{:S(2)}) async-start(bf16[8,4,5376]{2,1,0:T(4,128)(2,1)} %broadcast_in_dim.139), calls=%async_computation.9 | async-start | bytes 688128 | tf_op jit(solution)/shard_map/all_to_all | solution.py:20
  279.1 9.5 %all-to-all-done.9 = bf16[8,4,5376]{2,1,0:T(4,128)(2,1)S(1)} async-done(((bf16[8,4,5376]{2,1,0:T(4,128)(2,1)}), bf16[8,4,5376]{2,1,0:T(4,128)(2,1)S(1)}, u32[]{:S(2)}, u32[]{:S(2)}) %all-to-all-start.9) | async-done | bytes 344096 | tf_op jit(solution)/shard_map/all_to_all | solution.py:20
  (115 shorter events, 18.8 us)
Async XLA Ops:
  0.6 41.5 %copy-start = (bf16[32,512]{1,0:T(8,128)(2,1)S(1)}, bf16[32,512]{1,0:T(8,128)(2,1)}, u32[]{:S(2)}) copy-start(bf16[32,512]{1,0:T(8,128)(2,1)} %param.14) | copy-start | bytes 98308
  3.1 34.6 %all-to-all-start = ((bf16[16,128,512]{2,1,0:T(8,128)(2,1)}), bf16[16,128,512]{2,1,0:T(8,128)(2,1)S(1)}, u32[]{:S(2)}, u32[]{:S(2)}) async-start(bf16[16,128,512]{2,1,0:T(8,128)(2,1)} %broadcast_in_dim.62), calls=%async_computation | async-start | bytes 4194304 | tf_op jit(solution)/shard_map/all_to_all | solution.py:20
  10.6 11.3 %copy-start.10 = (s32[128]{0:T(128)S(1)}, s32[128]{0:T(128)}, u32[]{:S(2)}) copy-start(s32[128]{0:T(128)} %param.20) | copy-start | bytes 1540
  10.6 11.4 %copy-start.14 = (f32[128]{0:T(128)S(1)}, f32[128]{0:T(128)}, u32[]{:S(2)}) copy-start(f32[128]{0:T(128)} %param.23) | copy-start | bytes 1540
  10.6 11.6 %copy-start.2 = (s32[32]{0:T(128)S(1)}, s32[32]{0:T(128)}, u32[]{:S(2)}) copy-start(s32[32]{0:T(128)} %param.19) | copy-start | bytes 388
  16.0 75.4 %collective-permute-start.2 = (bf16[256,5376]{1,0:T(8,128)(2,1)}, bf16[256,5376]{1,0:T(8,128)(2,1)}, u32[]{:S(2)}, u32[]{:S(2)}) collective-permute-start(bf16[256,5376]{1,0:T(8,128)(2,1)} %get-tuple-element.11), channel_id=1, source_target_pairs={{1,0},{2,1},{3,2},{4,3},{5,4},{6,5},{7,6},{0,7},{9,8},{10,9},{11,1... | collective-permute-start | bytes 8257544 | tf_op jit(solution)/shard_map/ppermute | solution.py:89
  21.8 69.5 %collective-permute-start.3 = (bf16[256,5376]{1,0:T(8,128)(2,1)}, bf16[256,5376]{1,0:T(8,128)(2,1)}, u32[]{:S(2)}, u32[]{:S(2)}) collective-permute-start(bf16[256,5376]{1,0:T(8,128)(2,1)} %get-tuple-element.10), channel_id=1, source_target_pairs={{0,1},{1,2},{2,3},{3,4},{4,5},{5,6},{6,7},{7,0},{8,9},{9,10},{10,1... | collective-permute-start | bytes 8257544 | tf_op jit(solution)/shard_map/ppermute | solution.py:90
  21.8 102.0 %collective-permute-start.1 = (bf16[512,5376]{1,0:T(8,128)(2,1)}, bf16[512,5376]{1,0:T(8,128)(2,1)}, u32[]{:S(2)}, u32[]{:S(2)}) collective-permute-start(bf16[512,5376]{1,0:T(8,128)(2,1)} %param.27), channel_id=1, source_target_pairs={{0,8},{8,0},{1,9},{9,1},{2,10},{10,2},{3,11},{11,3},{4,12},{12,4},... | collective-permute-start | bytes 16515080 | tf_op jit(solution)/shard_map/ppermute | solution.py:93
  39.1 2.1 collective-permute-start
  39.2 2.9 copy-start.13
  39.8 2.7 copy-start.12
  47.5 49.2 %slice-start = ((s8[5505024]{0:T(1024)(128)(4,1)}), s8[1310720]{0:T(1024)(128)(4,1)S(1)}, s32[]{:S(2)}) async-start(s8[5505024]{0:T(1024)(128)(4,1)} %bitcast.113), calls=%async_computation.10 | async-start | bytes 2621440
  47.5 52.1 %all-to-all-start.1 = ((f32[8,4,5376]{2,1,0:T(4,128)}), f32[8,4,5376]{2,1,0:T(4,128)S(1)}, u32[]{:S(2)}, u32[]{:S(2)}) async-start(f32[8,4,5376]{2,1,0:T(4,128)} %fusion.1), calls=%async_computation.1 | async-start | bytes 1376256 | tf_op jit(solution)/shard_map/all_to_all | solution.py:26
  56.1 40.7 %slice-start.1 = ((s8[5505024]{0:T(1024)(128)(4,1)}), s8[4194304]{0:T(1024)(128)(4,1)S(1)}, s32[]{:S(2)}) async-start(s8[5505024]{0:T(1024)(128)(4,1)} %bitcast.113), calls=%async_computation.11 | async-start | bytes 8388608
  96.7 39.5 %collective-permute-start.4 = (bf16[512,5376]{1,0:T(8,128)(2,1)}, bf16[512,5376]{1,0:T(8,128)(2,1)}, u32[]{:S(2)}, u32[]{:S(2)}) collective-permute-start(bf16[512,5376]{1,0:T(8,128)(2,1)} %pad_maximum_fusion), channel_id=1, source_target_pairs={{0,8},{8,0},{1,9},{9,1},{2,10},{10,2},{3,11},{11,3},{4,12},{12,4},... | collective-permute-start | bytes 16515080 | tf_op jit(solution)/shard_map/ppermute | solution.py:93
  96.8 2.9 %copy-start.5 = (bf16[32,5376]{1,0:T(8,128)(2,1)S(1)}, bf16[32,5376]{1,0:T(8,128)(2,1)}, u32[]{:S(2)}) copy-start(bf16[32,5376]{1,0:T(8,128)(2,1)} %param.24) | copy-start | bytes 1032196
  96.8 3.6 %copy-start.4 = (f32[5376]{0:T(1024)S(1)}, f32[5376]{0:T(1024)}, u32[]{:S(2)}) copy-start(f32[5376]{0:T(1024)} %param.26) | copy-start | bytes 64516
  96.8 7.8 %copy-start.6 = (s32[1024]{0:T(1024)S(1)}, s32[1024]{0:T(1024)}, u32[]{:S(2)}) copy-start(s32[1024]{0:T(1024)} %param.22) | copy-start | bytes 12292
  96.8 8.3 %copy-start.11 = (s32[128]{0:T(128)S(1)}, s32[128]{0:T(128)}, u32[]{:S(2)}) copy-start(s32[128]{0:T(128)} %param.21) | copy-start | bytes 1540
  100.4 4.4 %copy-start.7 = (f32[4]{0:T(128)}, f32[4]{0:T(128)S(1)}, u32[]{:S(2)}) copy-start(f32[4]{0:T(128)S(1)} %get-tuple-element.24) | copy-start | bytes 52
  101.2 13.6 %all-to-all-start.2 = ((bf16[4,4,5376]{2,1,0:T(4,128)(2,1)}), bf16[4,4,5376]{2,1,0:T(4,128)(2,1)S(1)}, u32[]{:S(2)}, u32[]{:S(2)}) async-start(bf16[4,4,5376]{2,1,0:T(4,128)(2,1)} %broadcast_in_dim.67), calls=%async_computation.2 | async-start | bytes 344064 | tf_op jit(solution)/shard_map/all_to_all | solution.py:20
  116.6 40.7 %all-to-all-start.3 = ((bf16[16,16,5376]{2,1,0:T(8,128)(2,1)}), bf16[16,16,5376]{2,1,0:T(8,128)(2,1)S(1)}, u32[]{:S(2)}, u32[]{:S(2)}) async-start(bf16[16,16,5376]{2,1,0:T(8,128)(2,1)} %broadcast_in_dim.69), calls=%async_computation.3 | async-start | bytes 5505024 | tf_op jit(solution)/shard_map/all_to_all | solution.py:20
  167.7 1.4 copy-start.3
  170.3 12.0 %all-to-all-start.4 = ((f32[4,3,256]{2,1,0:T(4,128)}), f32[4,3,256]{2,1,0:T(4,128)S(1)}, u32[]{:S(2)}, u32[]{:S(2)}) async-start(f32[4,3,256]{2,1,0:T(4,128)} %broadcast_in_dim.74), calls=%async_computation.4 | async-start | bytes 32768 | tf_op jit(solution)/shard_map/all_to_all | solution.py:20
  183.0 13.7 %all-to-all-start.5 = ((f32[16,3,256]{2,1,0:T(4,128)}), f32[16,3,256]{2,1,0:T(4,128)S(1)}, u32[]{:S(2)}, u32[]{:S(2)}) async-start(f32[16,3,256]{2,1,0:T(4,128)} %broadcast_in_dim.75), calls=%async_computation.5 | async-start | bytes 131072 | tf_op jit(solution)/shard_map/all_to_all | solution.py:20
  244.4 21.3 %copy-start.8 = (f32[4]{0:T(128)S(1)}, f32[4]{0:T(128)}, u32[]{:S(2)}) copy-start(f32[4]{0:T(128)} %copy-done.7) | copy-start | bytes 52
  244.4 21.3 %copy-start.9 = (f32[4]{0:T(128)S(1)}, f32[4]{0:T(128)}, u32[]{:S(2)}) copy-start(f32[4]{0:T(128)} %get-tuple-element.23) | copy-start | bytes 52
  244.4 45.1 %copy-start.1 = (bf16[32,512]{1,0:T(8,128)(2,1)S(1)}, bf16[32,512]{1,0:T(8,128)(2,1)}, u32[]{:S(2)}) copy-start(bf16[32,512]{1,0:T(8,128)(2,1)} %param.14) | copy-start | bytes 98308
  245.6 13.1 %all-to-all-start.8 = ((f32[4,4,5376]{2,1,0:T(4,128)}), f32[4,4,5376]{2,1,0:T(4,128)S(1)}, u32[]{:S(2)}, u32[]{:S(2)}) async-start(f32[4,4,5376]{2,1,0:T(4,128)} %reshape.338), calls=%async_computation.8 | async-start | bytes 688128 | tf_op jit(solution)/shard_map/all_to_all | solution.py:26
  259.2 13.8 %all-to-all-start.6 = ((f32[8,1,4]{2,1,0:T(1,128)}), f32[8,1,4]{2,1,0:T(1,128)S(1)}, u32[]{:S(2)}, u32[]{:S(2)}) async-start(f32[8,1,4]{2,1,0:T(1,128)} %broadcast_in_dim.76), calls=%async_computation.6 | async-start | bytes 8192 | tf_op jit(solution)/shard_map/all_to_all | solution.py:20
  273.9 14.7 %all-to-all-start.9 = ((bf16[8,4,5376]{2,1,0:T(4,128)(2,1)}), bf16[8,4,5376]{2,1,0:T(4,128)(2,1)S(1)}, u32[]{:S(2)}, u32[]{:S(2)}) async-start(bf16[8,4,5376]{2,1,0:T(4,128)(2,1)} %broadcast_in_dim.139), calls=%async_computation.9 | async-start | bytes 688128 | tf_op jit(solution)/shard_map/all_to_all | solution.py:20

commit v3 on v2

--- a/solution.py
+++ b/solution.py
@@ -1,6 +1,8 @@
 import jax
 import jax.numpy as jnp
 from jax import lax
+from jax.experimental import pallas as pl
+from jax.experimental.pallas import tpu as pltpu
 from jax.sharding import Mesh
 from jax.sharding import PartitionSpec as P
 
@@ -52,6 +54,122 @@
     top = jnp.max(stats[:, 0], axis=0)
     total = jnp.sum(stats[:, 1] * jnp.exp(stats[:, 0] - top[None]), axis=0)
     return jnp.stack([top, total, jnp.sum(stats[:, 2], axis=0)])
+
+
+NT = (((1,), (1,)), ((), ()))
+VMEM_BYTES = 44 * 1024 * 1024
+
+
+def logits_kernel(rows, target_column, *refs):
+    slabs, (logits, stats, held, arrivals) = refs[:4], refs[4:]
+    depth = held.shape[1]
+    chunk = depth // 2
+    steps = [(k, part) for k in range(len(slabs)) for part in range(2)]
+    copies = [
+        pltpu.make_async_copy(
+            slabs[k].at[pl.ds(part * chunk, chunk)],
+            held.at[k, pl.ds(part * chunk, chunk)],
+            arrivals.at[2 * k + part],
+        )
+        for k, part in steps
+    ]
+    for copy in copies:
+        copy.start()
+    top = None
+    for (k, part), copy in zip(steps, copies):
+        copy.wait()
+        block = lax.dot_general(
+            held[k, pl.ds(part * chunk, chunk), :],
+            rows[...],
+            NT,
+            preferred_element_type=jnp.float32,
+        )
+        logits[pl.ds(k * depth + part * chunk, chunk), :] = block
+        block_top = jnp.max(block, axis=0, keepdims=True)
+        top = block_top if top is None else jnp.maximum(top, block_top)
+    total = jnp.zeros_like(top)
+    picked = jnp.zeros_like(top)
+    for k, part in steps:
+        start = k * depth + part * chunk
+        block = logits[pl.ds(start, chunk), :]
+        hit = lax.broadcasted_iota(jnp.int32, block.shape, 0) + start == target_column[...]
+        total += jnp.sum(jnp.exp(block - top), axis=0, keepdims=True)
+        picked += jnp.sum(jnp.where(hit, block, 0.0), axis=0, keepdims=True)
+    line = lax.broadcasted_iota(jnp.int32, stats.shape, 0)
+    stats[...] = jnp.where(line == 0, top, jnp.where(line == 1, total, picked))
+
+
+def gradient_kernel(logits, target_column, log_total, token_weight, *refs):
+    slabs, (terms, grad) = refs[:4], refs[4:]
+    depth = slabs[0].shape[0]
+    chunk = depth // 2
+
+    @pl.when(pl.program_id(0) == 0)
+    def _():
+        for start in range(0, len(slabs) * depth, chunk):
+            block = logits[pl.ds(start, chunk), :]
+            hit = lax.broadcasted_iota(jnp.int32, block.shape, 0) + start == target_column[...]
+            block = jnp.where(hit, 1.0, 0.0) - jnp.exp(block - log_total[...])
+            grad[:, pl.ds(start, chunk)] = (token_weight[...] * block).T.astype(jnp.bfloat16)
+
+    sums = [
+        jnp.dot(
+            grad[:, pl.ds(k * depth, depth)], slab[...], preferred_element_type=jnp.float32
+        )
+        for k, slab in enumerate(slabs)
+    ]
+    terms[...] = ((sums[0] + sums[1]) + (sums[2] + sums[3])).astype(jnp.bfloat16)
+
+
+def slab_logits(rows, target_column, slabs):
+    depth, width = slabs[0].shape
+    count, entries = rows.shape[0], depth * len(slabs)
+    whole = pl.BlockSpec(memory_space=pltpu.VMEM)
+    return pl.pallas_call(
+        logits_kernel,
+        out_shape=(
+            jax.ShapeDtypeStruct((entries, count), jnp.float32),
+            jax.ShapeDtypeStruct((8, count), jnp.float32),
+        ),
+        in_specs=[whole, whole] + [pl.BlockSpec(memory_space=pl.ANY)] * len(slabs),
+        out_specs=[whole, whole],
+        scratch_shapes=[
+            pltpu.VMEM((len(slabs), depth, width), jnp.bfloat16),
+            pltpu.SemaphoreType.DMA((2 * len(slabs),)),
+        ],
+        compiler_params=pltpu.CompilerParams(vmem_limit_bytes=VMEM_BYTES),
+        cost_estimate=pl.CostEstimate(
+            flops=2 * count * entries * width,
+            bytes_accessed=2 * entries * width,
+            transcendentals=count * entries,
+        ),
+    )(rows, target_column, *slabs)
+
+
+def slab_gradient(logits, target_column, log_total, token_weight, slabs):
+    depth, width = slabs[0].shape
+    entries, count = logits.shape
+    tile = next(t for t in (768, 512, 256, 128) if width % t == 0)
+
+    def fixed(shape):
+        return pl.BlockSpec(shape, lambda i: (0, 0))
+
+    return pl.pallas_call(
+        gradient_kernel,
+        grid=(width // tile,),
+        out_shape=jax.ShapeDtypeStruct((count, width), jnp.bfloat16),
+        in_specs=[fixed((entries, count))]
+        + [fixed((1, count))] * 3
+        + [pl.BlockSpec((depth, tile), lambda i: (0, i))] * len(slabs),
+        out_specs=pl.BlockSpec((count, tile), lambda i: (0, i)),
+        scratch_shapes=[pltpu.VMEM((count, entries), jnp.bfloat16)],
+        compiler_params=pltpu.CompilerParams(vmem_limit_bytes=VMEM_BYTES),
+        cost_estimate=pl.CostEstimate(
+            flops=2 * count * entries * width,
+            bytes_accessed=2 * entries * width,
+            transcendentals=count * entries,
+        ),
+    )(logits, target_column, log_total, token_weight, *slabs)
 
 
 def body(
@@ -81,23 +199,36 @@
     planes = XS * YS
     layer = lax.axis_index(Z)
     layers = lax.axis_size(Z)
-    parity = lax.axis_index("zl")
+    odd_layer = lax.axis_index("zl")
+    odd_x = lax.axis_index("x") % 2
+    parity = (odd_x + odd_layer) % 2
     dp_index = plane * CS + core
 
-    half_slab = vocab_slab // 2
-    ring = range(layers)
-    from_next = lax.ppermute(embedding[:half_slab], Z, [((k + 1) % layers, k) for k in ring])
-    from_prev = lax.ppermute(embedding[half_slab:], Z, [(k, (k + 1) % layers) for k in ring])
-    near = jnp.concatenate([from_next, from_prev], axis=0)
-    table = jnp.concatenate(
-        [embedding, lax.ppermute(embedding, "c", SWAP), near, lax.ppermute(near, "c", SWAP)], axis=0
-    )
+    quarter = vocab_slab // 4
+
+    def from_neighbour(part, axes, ahead):
+        size = lax.axis_size(axes)
+        pairs = [((k + ahead) % size, k) for k in range(size)]
+        return lax.ppermute(embedding[part * quarter : (part + 1) * quarter], axes, pairs)
+
+    pieces = (
+        from_neighbour(0, Z, 1),
+        from_neighbour(1, Z, -1),
+        from_neighbour(2, "x", 1),
+        from_neighbour(3, "x", -1),
+    )
+    across = lax.ppermute(embedding, "c", SWAP)
+    along_x = lax.axis_index("x")
     slab_column = jnp.arange(vocab_slab, dtype=jnp.int32)
-    near_layer = jnp.where(slab_column < half_slab, layer + 1, layer - 1) % layers
+    near_layer = jnp.where(slab_column < quarter, layer + 1, layer)
+    near_layer = jnp.where(slab_column // quarter == 1, layer - 1, near_layer) % layers
+    near_x = jnp.where(slab_column // quarter == 2, along_x + 1, along_x)
+    near_x = jnp.where(slab_column // quarter == 3, along_x - 1, near_x) % XS
+    near_plane = near_x * YS + lax.axis_index("y")
     entry = jnp.concatenate(
         [
-            ((plane * CS + which) * layers + held_layer) * vocab_slab + slab_column
-            for held_layer in (layer, near_layer)
+            ((at_plane * CS + which) * layers + at_layer) * vocab_slab + slab_column
+            for at_plane, at_layer in ((plane, layer), (near_plane, near_layer))
             for which in (core, 1 - core)
         ]
     )
@@ -133,45 +264,60 @@
     )
     partial_value = jnp.dot(attended, out_proj, preferred_element_type=jnp.float32)
 
+    partial_value, pieces, across = lax.optimization_barrier((partial_value, pieces, across))
+    near = jnp.concatenate(pieces, axis=0)
+    near_across = lax.ppermute(near, "c", SWAP)
+
     share = row_count // layers
     head_total = summed(partial_value, Z)
+    head_total, near_across = lax.optimization_barrier((head_total, near_across))
+    slabs = (embedding, across, near, near_across)
     my_residual = lax.dynamic_slice_in_dim(residual, layer * share, share)
     hidden = my_residual.astype(jnp.float32) + head_total
     norm_factor = lax.rsqrt(jnp.mean(hidden * hidden, axis=-1, keepdims=True) + norm_epsilon)
     normed = (hidden * norm_factor * norm_gain).astype(jnp.bfloat16)
 
     pairs = layers // 2
-    normed = spread(normed, "zh").reshape(pairs * share, width)
+    by_parity = spread(normed, Z).reshape(pairs, 2, share, width).transpose(1, 0, 2, 3)
+    by_parity = by_parity.reshape(2, pairs * share, width)
     rows_here = planes * pairs * share
-    every_row = spread(normed, ("x", "y")).reshape(rows_here, width)
+    for_even_x = jnp.where(odd_layer == 0, by_parity[0], by_parity[1])
+    for_odd_x = jnp.where(odd_layer == 0, by_parity[1], by_parity[0])
+    to_odd_x = (jnp.arange(planes) // YS % 2 == 1)[:, None, None]
+    outgoing = jnp.where(to_odd_x, for_odd_x[None], for_even_x[None])
+    every_row = lax.all_to_all(outgoing, ("x", "y"), 0, 0, tiled=True).reshape(rows_here, width)
 
     def of_rows(values):
         return values.reshape(planes, CS, pairs, 2, share)[:, core, :, parity].reshape(rows_here)
 
-    logits = lax.dot_general(
-        every_row, table, (((1,), (1,)), ((), ())), preferred_element_type=jnp.float32
-    )
-    hit = entry[None, :] == of_rows(targets)[:, None]
-    top = jnp.max(logits, axis=1)
-    total = jnp.sum(jnp.exp(logits - top[:, None]), axis=1)
-    picked = jnp.sum(jnp.where(hit, logits, 0.0), axis=1)
-    stats = jnp.stack([top, total, picked])
-    stats = merged(spread(stats, "zh"))
-    stats = merged(spread(stats, ("x", "y")))
-    log_total = stats[0] + jnp.log(stats[1])
-    first_row = (plane * pairs + lax.axis_index("zh")) * share
-    logprob = lax.dynamic_slice_in_dim(stats[2] - log_total, first_row, share)
-    logprob = spread(logprob, Z).reshape(row_count)
+    def even_first(both, odd):
+        return jnp.where(odd == 0, both, both[::-1])
+
+    hit = entry[:, None] == of_rows(targets)[None, :]
+    numbers = jnp.arange(entry.shape[0], dtype=jnp.int32)[:, None]
+    target_column = jnp.max(jnp.where(hit, numbers, -1), axis=0, keepdims=True)
+    logits, stats = slab_logits(every_row, target_column, slabs)
+    column = spread(stats[:3], Z).reshape(pairs, 2, 3, rows_here)
+    column = even_first(jnp.stack([merged(column[:, 0]), merged(column[:, 1])]), odd_x)
+    stats = spread(column, ("x", "y"))
+    stats = jnp.stack([merged(stats[:, 0]), merged(stats[:, 1])])
+    log_total = stats[:, 0] + jnp.log(stats[:, 1])
+    every_logprob = (stats[:, 2] - log_total).reshape(2, planes, pairs, share)
+    logprob = every_logprob[:, plane].transpose(1, 0, 2).reshape(row_count)
 
     row_ids = jnp.arange(targets.shape[0], dtype=jnp.int32)
     live_token = row_ids % CLEN < jnp.repeat(completion_lengths, CLEN)
     token_weight = of_rows(jnp.where(live_token, -jnp.repeat(advantages, CLEN), 0.0))
-    logit_grad = (
-        token_weight[:, None] * (hit.astype(jnp.float32) - jnp.exp(logits - log_total[:, None]))
-    ).astype(jnp.bfloat16)
-    terms = jnp.dot(logit_grad, table, preferred_element_type=jnp.float32)
-    summed_rows = summed(terms.astype(jnp.bfloat16), ("x", "y"))
-    normed_grad = summed(summed_rows, "zh")
+    terms = slab_gradient(
+        logits, target_column, log_total[parity][None], token_weight[None], slabs
+    )
+    arrived = lax.all_to_all(
+        terms.reshape(planes, pairs * share, width), ("x", "y"), 0, 0, tiled=True
+    )
+    arrived = arrived.reshape(XS // 2, 2, YS, pairs * share, width).astype(jnp.float32)
+    both = even_first(jnp.sum(arrived, axis=(0, 2)), odd_layer)
+    both = both.reshape(2, pairs, share, width).transpose(1, 0, 2, 3).reshape(row_count, width)
+    normed_grad = summed(both.astype(jnp.bfloat16), Z)
     hidden_grad = norm_gain * norm_factor * normed_grad - hidden * norm_factor**3 * jnp.mean(
         norm_gain * normed_grad * hidden, axis=-1, keepdims=True
     )

time: 291 us -> 311 us (1.069)
  Pallas kernels: 0 us -> 25.8 us
  matrix products: 29.9 us -> 4.5 us
  waiting for transfers between devices: 117 us -> 139 us
  blocking collectives: 33.4 us -> 48.4 us
  starting transfers between devices: 57.3 us -> 49 us
  local copies, waits for them, and re-layouts: 41.2 us -> 35.3 us
  other arithmetic: 9.83 us -> 6.56 us
    all_to_all x0 -> x1, blocking collectives: none -> 34.7 us  [body(): lax.all_to_all(terms.reshape(planes, pairs * share, width), ('x', 'y'), 0...]
    all_to_all x0 -> x1, waiting for transfers between devices: none -> 34.5 us  [body(): lax.all_to_all(outgoing, ('x', 'y'), 0, 0, tiled=True)]
    pallas_call x0 -> x2, Pallas kernels: none -> 25.8 us  [the longest x1 14.1 us: slab_logits(): pl.pallas_call(logits_kernel, out_shape=(jax.ShapeDtypeStruct((entries, c...]
    dot_general x2 -> x0, matrix products: 24.5 us -> none  [the longest x1 14.2 us: body(): terms = jnp.dot(logit_grad, table, preferred_element_type=jnp.float32)]
    all_to_all x1, blocking collectives: 33.4 us -> 13.7 us  [summed(): arrived = lax.all_to_all(pieces, axes, 0, 0, tiled=True)]
    all_to_all x7 -> x5, starting transfers between devices: 39.4 us -> 26.1 us  [spread(): return lax.all_to_all(copies, axes, 0, 0, tiled=True)]
    all_to_all x7 -> x5, waiting for transfers between devices: 70.7 us -> 57.9 us  [spread(): return lax.all_to_all(copies, axes, 0, 0, tiled=True)]
    all_to_all x2 -> x1, waiting for transfers between devices: 9.5 us -> 21.7 us  [summed(): arrived = lax.all_to_all(pieces, axes, 0, 0, tiled=True)]
  transfers between devices with their start and end apart: 14 -> 14, of which waited for: 10 -> 11; matrix products, arithmetic and copies ran while one was open for 16% -> 6% of each run, Pallas kernels for 0% -> 0%
where the time goes in v3:
time: 311 us; the launch traced here: 310 us
  waiting for transfers between devices  139 us (45%)
  starting transfers between devices  49 us (16%)
  blocking collectives  48.4 us (16%)
  local copies, waits for them, and re-layouts  35.3 us (11%)
  Pallas kernels  25.8 us (8%)
  other arithmetic  6.56 us (2%)
  matrix products  4.5 us (1%)
    all_to_all x5, waiting for transfers between devices, spread(): return lax.all_to_all(copies, axes, 0, 0, tiled=True)  57.9 us
    all_to_all x1, blocking collectives, body(): lax.all_to_all(terms.reshape(planes, pairs * share, width), ('x', 'y'), 0...  34.7 us
    all_to_all x1, waiting for transfers between devices, body(): lax.all_to_all(outgoing, ('x', 'y'), 0, 0, tiled=True)  34.5 us
    all_to_all x5, starting transfers between devices, spread(): return lax.all_to_all(copies, axes, 0, 0, tiled=True)  26.1 us
    ppermute x4, waiting for transfers between devices, from_neighbour(): lax.ppermute(embedding[part * quarter:(part + 1) * quarter], axes, pairs)  24 us
    all_to_all x1, waiting for transfers between devices, summed(): arrived = lax.all_to_all(pieces, axes, 0, 0, tiled=True)  21.7 us
    unnamed x43, local copies, waits for them, and re-layouts  15.7 us
    pallas_call x1, Pallas kernels, slab_logits(): pl.pallas_call(logits_kernel, out_shape=(jax.ShapeDtypeStruct((entries, c...  14.1 us
  transfers between devices with their start and end apart: 14, of which 11 were waited for; matrix products, arithmetic and copies ran while one was open for 6% of the time, Pallas kernels for 0%

profile of v3, /device:TPU:2, one launch (start us, length us, event | category | flops | bytes accessed | tf_op | source)
XLA Modules:
  0.0 310.1 jit_solution(14849228577097683445)
XLA Ops:
  3.2 7.5 %all-to-all-start = ((bf16[16,128,512]{2,1,0:T(8,128)(2,1)}), bf16[16,128,512]{2,1,0:T(8,128)(2,1)S(1)}, u32[]{:S(2)}, u32[]{:S(2)}) async-start(bf16[16,128,512]{2,1,0:T(8,128)(2,1)} %broadcast_in_dim.161), calls=%async_computation | async-start | bytes 4194304 | tf_op jit(solution)/shard_map/all_to_all | solution.py:22
  10.7 5.1 %fusion.67 = (bf16[128,5376]{1,0:T(8,128)(2,1)}, bf16[128,5376]{1,0:T(8,128)(2,1)}, bf16[128,5376]{1,0:T(8,128)(2,1)}, bf16[128,5376]{1,0:T(8,128)(2,1)}) fusion(bf16[512,5376]{1,0:T(8,128)(2,1)} %refs_0_.3), kind=kLoop, calls=%fused_computation.176 | loop fusion | bytes 11010048 | tf_op jit(solution)/shard_map/slice | solution.py:212
  17.8 1.9 collective-permute-start.2
  19.8 20.0 %all-to-all-done = bf16[16,128,512]{2,1,0:T(8,128)(2,1)S(1)} async-done(((bf16[16,128,512]{2,1,0:T(8,128)(2,1)}), bf16[16,128,512]{2,1,0:T(8,128)(2,1)S(1)}, u32[]{:S(2)}, u32[]{:S(2)}) %all-to-all-start) | async-done | bytes 2097184 | tf_op jit(solution)/shard_map/all_to_all | solution.py:22
  42.5 5.9 %collective-permute-start.1 = (bf16[128,5376]{1,0:T(8,128)(2,1)}, bf16[128,5376]{1,0:T(8,128)(2,1)}, u32[]{:S(2)}, u32[]{:S(2)}) collective-permute-start(bf16[128,5376]{1,0:T(8,128)(2,1)} %get-tuple-element.35), channel_id=1, source_target_pairs={{1,0},{2,1},{3,2},{4,3},{5,4},{6,5},{7,6},{0,7},{9,8},{10,9},{11,1... | collective-permute-start | bytes 4128776 | tf_op jit(solution)/shard_map/ppermute | solution.py:212
  50.8 3.6 %fusion.72 = f32[32,5376]{1,0:T(8,128)S(1)} fusion(bf16[32,512]{1,0:T(8,128)(2,1)S(1)} %bitcast.197, bf16[512,5376]{1,0:T(8,128)(2,1)} %param.25), kind=kOutput, calls=%fused_computation.181 | convolution fusion | flops 176160768 | bytes 6225920 | tf_op jit(solution)/shard_map/dot_general | solution.py:265
  54.4 11.8 %collective-permute-done.4 = bf16[128,5376]{1,0:T(8,128)(2,1)} collective-permute-done((bf16[128,5376]{1,0:T(8,128)(2,1)}, bf16[128,5376]{1,0:T(8,128)(2,1)}, u32[]{:S(2)}, u32[]{:S(2)}) %collective-permute-start.4) | collective-permute-done | bytes 1376288 | tf_op jit(solution)/shard_map/ppermute | solution.py:212
  67.6 10.8 %collective-permute-done.1 = bf16[128,5376]{1,0:T(8,128)(2,1)} collective-permute-done((bf16[128,5376]{1,0:T(8,128)(2,1)}, bf16[128,5376]{1,0:T(8,128)(2,1)}, u32[]{:S(2)}, u32[]{:S(2)}) %collective-permute-start.1) | collective-permute-done | bytes 1376288 | tf_op jit(solution)/shard_map/ppermute | solution.py:212
  78.4 2.5 constant_dynamic-update-slice_fusion.3
  80.9 2.6 constant_dynamic-update-slice_fusion.2
  83.4 2.5 constant_dynamic-update-slice_fusion.1
  85.9 2.6 constant_dynamic-update-slice_fusion.refs_2_
  89.6 5.1 %all-to-all-start.1 = ((f32[8,4,5376]{2,1,0:T(4,128)}), f32[8,4,5376]{2,1,0:T(4,128)S(1)}, u32[]{:S(2)}, u32[]{:S(2)}) async-start(f32[8,4,5376]{2,1,0:T(4,128)} %reshape.394), calls=%async_computation.1 | async-start | bytes 1376256 | tf_op jit(solution)/shard_map/all_to_all | solution.py:28
  94.7 21.7 %all-to-all-done.1 = f32[8,4,5376]{2,1,0:T(4,128)S(1)} async-done(((f32[8,4,5376]{2,1,0:T(4,128)}), f32[8,4,5376]{2,1,0:T(4,128)S(1)}, u32[]{:S(2)}, u32[]{:S(2)}) %all-to-all-start.1) | async-done | bytes 688160 | tf_op jit(solution)/shard_map/all_to_all | solution.py:28
  118.1 3.4 %all-to-all-start.2 = ((bf16[8,4,5376]{2,1,0:T(4,128)(2,1)}), bf16[8,4,5376]{2,1,0:T(4,128)(2,1)S(1)}, u32[]{:S(2)}, u32[]{:S(2)}) async-start(bf16[8,4,5376]{2,1,0:T(4,128)(2,1)} %broadcast_in_dim.166), calls=%async_computation.2 | async-start | bytes 688128 | tf_op jit(solution)/shard_map/all_to_all | solution.py:22
  121.6 14.0 %all-to-all-done.2 = bf16[8,4,5376]{2,1,0:T(4,128)(2,1)S(1)} async-done(((bf16[8,4,5376]{2,1,0:T(4,128)(2,1)}), bf16[8,4,5376]{2,1,0:T(4,128)(2,1)S(1)}, u32[]{:S(2)}, u32[]{:S(2)}) %all-to-all-start.2) | async-done | bytes 344096 | tf_op jit(solution)/shard_map/all_to_all | solution.py:22
  135.8 1.8 broadcast_select_fusion
  137.7 7.8 %all-to-all-start.3 = ((bf16[16,16,5376]{2,1,0:T(8,128)(2,1)}), bf16[16,16,5376]{2,1,0:T(8,128)(2,1)S(1)}, u32[]{:S(2)}, u32[]{:S(2)}) async-start(bf16[16,16,5376]{2,1,0:T(8,128)(2,1)} %broadcast_select_fusion), calls=%async_computation.3 | async-start | bytes 5505024 | tf_op jit(solution)/shard_map/all_to_all | solution.py:288
  147.5 34.5 %all-to-all-done.3 = bf16[16,16,5376]{2,1,0:T(8,128)(2,1)S(1)} async-done(((bf16[16,16,5376]{2,1,0:T(8,128)(2,1)}), bf16[16,16,5376]{2,1,0:T(8,128)(2,1)S(1)}, u32[]{:S(2)}, u32[]{:S(2)}) %all-to-all-start.3) | async-done | bytes 2752544 | tf_op jit(solution)/shard_map/all_to_all | solution.py:288
  182.1 2.6 copy-done.2
  184.6 14.1 %shard_map.149 = (f32[2048,256]{1,0:T(8,128)S(1)}, f32[8,256]{1,0:T(8,128)S(1)}) custom-call(bf16[256,5376]{1,0:T(8,128)(2,1)S(1)} %bitcast.176, s32[1,256]{1,0:T(1,128)S(1)} %bitcast.178, bf16[512,5376]{1,0:T(8,128)(2,1)S(1)} %copy-done.2, bf16[512,5376]{1,0:T(8,128)(2,1)} %collective-permute-done.5.refs_1_, ...), custom_call_target="tpu_custom_call" | custom-call | flops 5637144576 | bytes 22020096 | tf_op jit(solution)/shard_map/pallas_call | solution.py:128
  200.7 3.3 %all-to-all-start.4 = ((f32[8,3,256]{2,1,0:T(4,128)}), f32[8,3,256]{2,1,0:T(4,128)S(1)}, u32[]{:S(2)}, u32[]{:S(2)}) async-start(f32[8,3,256]{2,1,0:T(4,128)} %broadcast_in_dim.178), calls=%async_computation.4 | async-start | bytes 65536 | tf_op jit(solution)/shard_map/all_to_all | solution.py:22
  204.1 7.9 %all-to-all-done.4 = f32[8,3,256]{2,1,0:T(4,128)S(1)} async-done(((f32[8,3,256]{2,1,0:T(4,128)}), f32[8,3,256]{2,1,0:T(4,128)S(1)}, u32[]{:S(2)}, u32[]{:S(2)}) %all-to-all-start.4) | async-done | bytes 24608 | tf_op jit(solution)/shard_map/all_to_all | solution.py:22
  213.0 8.4 %all-to-all-start.5 = ((f32[16,2,3,256]{3,1,2,0:T(2,128)}), f32[16,2,3,256]{3,1,2,0:T(2,128)S(1)}, u32[]{:S(2)}, u32[]{:S(2)}) async-start(f32[16,2,3,256]{3,1,2,0:T(2,128)} %broadcast_in_dim.179), calls=%async_computation.5 | async-start | bytes 196608 | tf_op jit(solution)/shard_map/all_to_all | solution.py:22
  222.3 5.4 %all-to-all-done.5 = f32[16,2,3,256]{3,1,2,0:T(2,128)S(1)} async-done(((f32[16,2,3,256]{3,1,2,0:T(2,128)}), f32[16,2,3,256]{3,1,2,0:T(2,128)S(1)}, u32[]{:S(2)}, u32[]{:S(2)}) %all-to-all-start.5) | async-done | bytes 98336 | tf_op jit(solution)/shard_map/all_to_all | solution.py:22
  228.1 2.6 copy-done.3
  230.6 1.6 copy-done.5
  232.2 11.7 %shard_map.150 = bf16[256,5376]{1,0:T(8,128)(2,1)S(1)} custom-call(f32[2048,256]{1,0:T(8,128)S(1)} %copy-done.5, s32[1,256]{1,0:T(1,128)S(1)} %bitcast.179, f32[1,256]{1,0:T(1,128)S(1)} %fusion.44.log_total, f32[1,256]{1,0:T(1,128)S(1)} %broadcast_in_dim_reshape_squeeze.4.token_weight, bf16[512,5376]{1,0:T(8,128)(2,1)S(1)} %copy-done.3, ...), custom_call_target="tpu_custom_call" | custom-call | flops 5637144576 | bytes 22020096 | tf_op jit(solution)/shard_map/pallas_call | solution.py:157
  243.9 34.7 %all_to_all.45 = bf16[16,16,5376]{2,1,0:T(8,128)(2,1)S(1)} all-to-all(bf16[16,16,5376]{2,1,0:T(8,128)(2,1)S(1)} %bitcast.177), channel_id=1, replica_groups=mesh['x'=4,'y'=4,'c'=2,'zh'=4,'zl'=2] {'x','y'}, dimensions={0} | all-to-all | bytes 5505024 | tf_op jit(solution)/shard_map/all_to_all | solution.py:314
  279.4 13.7 %all_to_all.46 = bf16[8,4,5376]{2,1,0:T(4,128)(2,1)S(1)} all-to-all(bf16[8,4,5376]{2,1,0:T(4,128)(2,1)S(1)} %bitcast.183), channel_id=1, replica_groups=mesh['x'=4,'y'=4,'c'=2,'zh'=4,'zl'=2] {'zh','zl'}, dimensions={0} | all-to-all | bytes 688128 | tf_op jit(solution)/shard_map/all_to_all | solution.py:28
  294.5 3.4 %all-to-all-start.8 = ((bf16[8,4,5376]{2,1,0:T(4,128)(2,1)}), bf16[8,4,5376]{2,1,0:T(4,128)(2,1)S(1)}, u32[]{:S(2)}, u32[]{:S(2)}) async-start(bf16[8,4,5376]{2,1,0:T(4,128)(2,1)} %broadcast_in_dim.184), calls=%async_computation.8 | async-start | bytes 688128 | tf_op jit(solution)/shard_map/all_to_all | solution.py:22
  298.7 10.5 %all-to-all-done.8 = bf16[8,4,5376]{2,1,0:T(4,128)(2,1)S(1)} async-done(((bf16[8,4,5376]{2,1,0:T(4,128)(2,1)}), bf16[8,4,5376]{2,1,0:T(4,128)(2,1)S(1)}, u32[]{:S(2)}, u32[]{:S(2)}) %all-to-all-start.8) | async-done | bytes 344096 | tf_op jit(solution)/shard_map/all_to_all | solution.py:22
  (139 shorter events, 23.8 us)
Async XLA Ops:
  0.6 49.2 %copy-start = (bf16[32,512]{1,0:T(8,128)(2,1)S(1)}, bf16[32,512]{1,0:T(8,128)(2,1)}, u32[]{:S(2)}) copy-start(bf16[32,512]{1,0:T(8,128)(2,1)} %param.14) | copy-start | bytes 98308
  0.6 77.7 %collective-permute-start.5 = (bf16[512,5376]{1,0:T(8,128)(2,1)}, bf16[512,5376]{1,0:T(8,128)(2,1)}, u32[]{:S(2)}, u32[]{:S(2)}) collective-permute-start(bf16[512,5376]{1,0:T(8,128)(2,1)} %refs_0_.3), channel_id=1, source_target_pairs={{0,8},{8,0},{1,9},{9,1},{2,10},{10,2},{3,11},{11,3},{4,12},{12,4},... | collective-permute-start | bytes 16515080 | tf_op jit(solution)/shard_map/ppermute | solution.py:220
  3.2 36.7 %all-to-all-start = ((bf16[16,128,512]{2,1,0:T(8,128)(2,1)}), bf16[16,128,512]{2,1,0:T(8,128)(2,1)S(1)}, u32[]{:S(2)}, u32[]{:S(2)}) async-start(bf16[16,128,512]{2,1,0:T(8,128)(2,1)} %broadcast_in_dim.161), calls=%async_computation | async-start | bytes 4194304 | tf_op jit(solution)/shard_map/all_to_all | solution.py:22
  10.7 9.0 %copy-start.13 = (s32[128]{0:T(128)S(1)}, s32[128]{0:T(128)}, u32[]{:S(2)}) copy-start(s32[128]{0:T(128)} %param.20) | copy-start | bytes 1540
  10.7 29.9 %copy-start.6 = (s32[32]{0:T(128)S(1)}, s32[32]{0:T(128)}, u32[]{:S(2)}) copy-start(s32[32]{0:T(128)} %param.19) | copy-start | bytes 388
  15.8 50.4 %collective-permute-start.4 = (bf16[128,5376]{1,0:T(8,128)(2,1)}, bf16[128,5376]{1,0:T(8,128)(2,1)}, u32[]{:S(2)}, u32[]{:S(2)}) collective-permute-start(bf16[128,5376]{1,0:T(8,128)(2,1)} %get-tuple-element.32), channel_id=1, source_target_pairs={{192,0},{0,64},{64,128},{128,192},{193,1},{1,65},{65,129},{129,193... | collective-permute-start | bytes 4128776 | tf_op jit(solution)/shard_map/ppermute | solution.py:212
  17.2 50.4 %collective-permute-start.3 = (bf16[128,5376]{1,0:T(8,128)(2,1)}, bf16[128,5376]{1,0:T(8,128)(2,1)}, u32[]{:S(2)}, u32[]{:S(2)}) collective-permute-start(bf16[128,5376]{1,0:T(8,128)(2,1)} %get-tuple-element.33), channel_id=1, source_target_pairs={{64,0},{128,64},{192,128},{0,192},{65,1},{129,65},{193,129},{1,193... | collective-permute-start | bytes 4128776 | tf_op jit(solution)/shard_map/ppermute | solution.py:212
  17.8 49.8 %collective-permute-start.2 = (bf16[128,5376]{1,0:T(8,128)(2,1)}, bf16[128,5376]{1,0:T(8,128)(2,1)}, u32[]{:S(2)}, u32[]{:S(2)}) collective-permute-start(bf16[128,5376]{1,0:T(8,128)(2,1)} %get-tuple-element.34), channel_id=1, source_target_pairs={{7,0},{0,1},{1,2},{2,3},{3,4},{4,5},{5,6},{6,7},{15,8},{8,9},{9,10... | collective-permute-start | bytes 4128776 | tf_op jit(solution)/shard_map/ppermute | solution.py:212
  40.5 2.0 collective-permute-start
  42.5 35.9 %collective-permute-start.1 = (bf16[128,5376]{1,0:T(8,128)(2,1)}, bf16[128,5376]{1,0:T(8,128)(2,1)}, u32[]{:S(2)}, u32[]{:S(2)}) collective-permute-start(bf16[128,5376]{1,0:T(8,128)(2,1)} %get-tuple-element.35), channel_id=1, source_target_pairs={{1,0},{2,1},{3,2},{4,3},{5,4},{6,5},{7,6},{0,7},{9,8},{10,9},{11,1... | collective-permute-start | bytes 4128776 | tf_op jit(solution)/shard_map/ppermute | solution.py:212
  48.4 1.5 copy-start.16
  49.0 1.4 copy-start.15
  85.9 30.5 %copy-start.8 = (bf16[32,5376]{1,0:T(8,128)(2,1)S(1)}, bf16[32,5376]{1,0:T(8,128)(2,1)}, u32[]{:S(2)}) copy-start(bf16[32,5376]{1,0:T(8,128)(2,1)} %param.24) | copy-start | bytes 1032196
  85.9 31.2 %copy-start.7 = (f32[5376]{0:T(1024)S(1)}, f32[5376]{0:T(1024)}, u32[]{:S(2)}) copy-start(f32[5376]{0:T(1024)} %param.26) | copy-start | bytes 64516
  88.5 27.9 %collective-permute-start.6 = (bf16[512,5376]{1,0:T(8,128)(2,1)}, bf16[512,5376]{1,0:T(8,128)(2,1)}, u32[]{:S(2)}, u32[]{:S(2)}) collective-permute-start(bf16[512,5376]{1,0:T(8,128)(2,1)} %constant_dynamic-update-slice_fusion.refs_2_), channel_id=1, source_target_pairs={{0,8},{8,0},{1,9},{9,1},{2,10},{10,2},{3,11},{11,3},{4,12},{12,4},... | collective-permute-start | bytes 16515080 | tf_op jit(solution)/shard_map/ppermute | solution.py:269
  89.6 26.8 %all-to-all-start.1 = ((f32[8,4,5376]{2,1,0:T(4,128)}), f32[8,4,5376]{2,1,0:T(4,128)S(1)}, u32[]{:S(2)}, u32[]{:S(2)}) async-start(f32[8,4,5376]{2,1,0:T(4,128)} %reshape.394), calls=%async_computation.1 | async-start | bytes 1376256 | tf_op jit(solution)/shard_map/all_to_all | solution.py:28
  117.2 20.5 %copy-start.10 = (f32[4]{0:T(128)}, f32[4]{0:T(128)S(1)}, u32[]{:S(2)}) copy-start(f32[4]{0:T(128)S(1)} %get-tuple-element.48) | copy-start | bytes 52
  118.1 17.5 %all-to-all-start.2 = ((bf16[8,4,5376]{2,1,0:T(4,128)(2,1)}), bf16[8,4,5376]{2,1,0:T(4,128)(2,1)S(1)}, u32[]{:S(2)}, u32[]{:S(2)}) async-start(bf16[8,4,5376]{2,1,0:T(4,128)(2,1)} %broadcast_in_dim.166), calls=%async_computation.2 | async-start | bytes 688128 | tf_op jit(solution)/shard_map/all_to_all | solution.py:22
  137.7 7.8 %copy-start.17 = (f32[128]{0:T(128)S(1)}, f32[128]{0:T(128)}, u32[]{:S(2)}) copy-start(f32[128]{0:T(128)} %param.23) | copy-start | bytes 1540
  137.7 8.0 %copy-start.14 = (s32[128]{0:T(128)S(1)}, s32[128]{0:T(128)}, u32[]{:S(2)}) copy-start(s32[128]{0:T(128)} %param.21) | copy-start | bytes 1540
  137.7 8.1 %copy-start.9 = (s32[1024]{0:T(1024)S(1)}, s32[1024]{0:T(1024)}, u32[]{:S(2)}) copy-start(s32[1024]{0:T(1024)} %param.22) | copy-start | bytes 12292
  137.7 44.4 %all-to-all-start.3 = ((bf16[16,16,5376]{2,1,0:T(8,128)(2,1)}), bf16[16,16,5376]{2,1,0:T(8,128)(2,1)S(1)}, u32[]{:S(2)}, u32[]{:S(2)}) async-start(bf16[16,16,5376]{2,1,0:T(8,128)(2,1)} %broadcast_select_fusion), calls=%async_computation.3 | async-start | bytes 5505024 | tf_op jit(solution)/shard_map/all_to_all | solution.py:288
  182.1 2.6 copy-start.2
  198.8 1.3 copy-start.4
  200.7 11.3 %all-to-all-start.4 = ((f32[8,3,256]{2,1,0:T(4,128)}), f32[8,3,256]{2,1,0:T(4,128)S(1)}, u32[]{:S(2)}, u32[]{:S(2)}) async-start(f32[8,3,256]{2,1,0:T(4,128)} %broadcast_in_dim.178), calls=%async_computation.4 | async-start | bytes 65536 | tf_op jit(solution)/shard_map/all_to_all | solution.py:22
  213.0 14.7 %all-to-all-start.5 = ((f32[16,2,3,256]{3,1,2,0:T(2,128)}), f32[16,2,3,256]{3,1,2,0:T(2,128)S(1)}, u32[]{:S(2)}, u32[]{:S(2)}) async-start(f32[16,2,3,256]{3,1,2,0:T(2,128)} %broadcast_in_dim.179), calls=%async_computation.5 | async-start | bytes 196608 | tf_op jit(solution)/shard_map/all_to_all | solution.py:22
  228.0 2.6 copy-start.3
  230.6 1.6 copy-start.5
  278.6 14.9 %copy-start.11 = (f32[4]{0:T(128)S(1)}, f32[4]{0:T(128)}, u32[]{:S(2)}) copy-start(f32[4]{0:T(128)} %copy-done.10) | copy-start | bytes 52
  278.6 14.9 %copy-start.12 = (f32[4]{0:T(128)S(1)}, f32[4]{0:T(128)}, u32[]{:S(2)}) copy-start(f32[4]{0:T(128)} %get-tuple-element.47) | copy-start | bytes 52
  278.9 31.1 %copy-start.1 = (bf16[32,512]{1,0:T(8,128)(2,1)S(1)}, bf16[32,512]{1,0:T(8,128)(2,1)}, u32[]{:S(2)}) copy-start(bf16[32,512]{1,0:T(8,128)(2,1)} %param.14) | copy-start | bytes 98308
  294.5 14.7 %all-to-all-start.8 = ((bf16[8,4,5376]{2,1,0:T(4,128)(2,1)}), bf16[8,4,5376]{2,1,0:T(4,128)(2,1)S(1)}, u32[]{:S(2)}, u32[]{:S(2)}) async-start(bf16[8,4,5376]{2,1,0:T(4,128)(2,1)} %broadcast_in_dim.184), calls=%async_computation.8 | async-start | bytes 688128 | tf_op jit(solution)/shard_map/all_to_all | solution.py:22

commit v4 on v3

--- a/solution.py
+++ b/solution.py
@@ -57,44 +57,65 @@
 
 
 NT = (((1,), (1,)), ((), ()))
-VMEM_BYTES = 44 * 1024 * 1024
-
-
-def logits_kernel(rows, target_column, *refs):
-    slabs, (logits, stats, held, arrivals) = refs[:4], refs[4:]
-    depth = held.shape[1]
-    chunk = depth // 2
-    steps = [(k, part) for k in range(len(slabs)) for part in range(2)]
+
+
+def join_kernel(*refs):
+    parts, (whole, arrivals) = refs[:-2], refs[-2:]
+    depth = parts[0].shape[0]
     copies = [
-        pltpu.make_async_copy(
-            slabs[k].at[pl.ds(part * chunk, chunk)],
-            held.at[k, pl.ds(part * chunk, chunk)],
-            arrivals.at[2 * k + part],
-        )
-        for k, part in steps
+        pltpu.make_async_copy(part, whole.at[pl.ds(k * depth, depth)], arrivals.at[k])
+        for k, part in enumerate(parts)
     ]
     for copy in copies:
         copy.start()
-    top = None
-    for (k, part), copy in zip(steps, copies):
+    for copy in copies:
         copy.wait()
+
+
+def join(parts):
+    depth, width = parts[0].shape
+    anywhere = pl.BlockSpec(memory_space=pl.ANY)
+    return pl.pallas_call(
+        join_kernel,
+        out_shape=jax.ShapeDtypeStruct((depth * len(parts), width), parts[0].dtype),
+        in_specs=[anywhere] * len(parts),
+        out_specs=anywhere,
+        scratch_shapes=[pltpu.SemaphoreType.DMA((len(parts),))],
+    )(*parts)
+
+
+def logits_kernel(rows, target_column, *refs):
+    slabs, (logits, stats, held, held_rows, arrivals, rows_arrival) = refs[:4], refs[4:]
+    depth = held.shape[1]
+    half = depth // 2
+    rows_copy = pltpu.make_async_copy(rows, held_rows, rows_arrival)
+    rows_copy.start()
+    copies = [
+        pltpu.make_async_copy(
+            slab.at[pl.ds(start, half)], held.at[k, pl.ds(start, half)], arrivals.at[k, part]
+        )
+        for k, slab in enumerate(slabs)
+        for part, start in enumerate((0, half))
+    ]
+    for copy in copies:
+        copy.start()
+    rows_copy.wait()
+    top = total = picked = None
+    for k in range(len(slabs)):
+        copies[2 * k].wait()
+        copies[2 * k + 1].wait()
         block = lax.dot_general(
-            held[k, pl.ds(part * chunk, chunk), :],
-            rows[...],
-            NT,
-            preferred_element_type=jnp.float32,
+            held[k], held_rows[...], NT, preferred_element_type=jnp.float32
         )
-        logits[pl.ds(k * depth + part * chunk, chunk), :] = block
+        logits[pl.ds(k * depth, depth), :] = block
+        hit = lax.broadcasted_iota(jnp.int32, block.shape, 0) + k * depth == target_column[...]
+        block_picked = jnp.sum(jnp.where(hit, block, 0.0), axis=0, keepdims=True)
         block_top = jnp.max(block, axis=0, keepdims=True)
-        top = block_top if top is None else jnp.maximum(top, block_top)
-    total = jnp.zeros_like(top)
-    picked = jnp.zeros_like(top)
-    for k, part in steps:
-        start = k * depth + part * chunk
-        block = logits[pl.ds(start, chunk), :]
-        hit = lax.broadcasted_iota(jnp.int32, block.shape, 0) + start == target_column[...]
-        total += jnp.sum(jnp.exp(block - top), axis=0, keepdims=True)
-        picked += jnp.sum(jnp.where(hit, block, 0.0), axis=0, keepdims=True)
+        new_top = block_top if k == 0 else jnp.maximum(top, block_top)
+        block_total = jnp.sum(jnp.exp(block - new_top), axis=0, keepdims=True)
+        total = block_total if k == 0 else total * jnp.exp(top - new_top) + block_total
+        picked = block_picked if k == 0 else picked + block_picked
+        top = new_top
     line = lax.broadcasted_iota(jnp.int32, stats.shape, 0)
     stats[...] = jnp.where(line == 0, top, jnp.where(line == 1, total, picked))
 
@@ -125,19 +146,22 @@
     depth, width = slabs[0].shape
     count, entries = rows.shape[0], depth * len(slabs)
     whole = pl.BlockSpec(memory_space=pltpu.VMEM)
+    anywhere = pl.BlockSpec(memory_space=pl.ANY)
     return pl.pallas_call(
         logits_kernel,
         out_shape=(
             jax.ShapeDtypeStruct((entries, count), jnp.float32),
             jax.ShapeDtypeStruct((8, count), jnp.float32),
         ),
-        in_specs=[whole, whole] + [pl.BlockSpec(memory_space=pl.ANY)] * len(slabs),
+        in_specs=[anywhere, whole] + [anywhere] * len(slabs),
         out_specs=[whole, whole],
         scratch_shapes=[
             pltpu.VMEM((len(slabs), depth, width), jnp.bfloat16),
-            pltpu.SemaphoreType.DMA((2 * len(slabs),)),
+            pltpu.VMEM((count, width), jnp.bfloat16),
+            pltpu.SemaphoreType.DMA((len(slabs), 2)),
+            pltpu.SemaphoreType.DMA,
         ],
-        compiler_params=pltpu.CompilerParams(vmem_limit_bytes=VMEM_BYTES),
+        compiler_params=pltpu.CompilerParams(vmem_limit_bytes=36 * 1024 * 1024),
         cost_estimate=pl.CostEstimate(
             flops=2 * count * entries * width,
             bytes_accessed=2 * entries * width,
@@ -163,7 +187,7 @@
         + [pl.BlockSpec((depth, tile), lambda i: (0, i))] * len(slabs),
         out_specs=pl.BlockSpec((count, tile), lambda i: (0, i)),
         scratch_shapes=[pltpu.VMEM((count, entries), jnp.bfloat16)],
-        compiler_params=pltpu.CompilerParams(vmem_limit_bytes=VMEM_BYTES),
+        compiler_params=pltpu.CompilerParams(vmem_limit_bytes=20 * 1024 * 1024),
         cost_estimate=pl.CostEstimate(
             flops=2 * count * entries * width,
             bytes_accessed=2 * entries * width,
@@ -217,7 +241,6 @@
         from_neighbour(2, "x", 1),
         from_neighbour(3, "x", -1),
     )
-    across = lax.ppermute(embedding, "c", SWAP)
     along_x = lax.axis_index("x")
     slab_column = jnp.arange(vocab_slab, dtype=jnp.int32)
     near_layer = jnp.where(slab_column < quarter, layer + 1, layer)
@@ -264,14 +287,13 @@
     )
     partial_value = jnp.dot(attended, out_proj, preferred_element_type=jnp.float32)
 
-    partial_value, pieces, across = lax.optimization_barrier((partial_value, pieces, across))
-    near = jnp.concatenate(pieces, axis=0)
-    near_across = lax.ppermute(near, "c", SWAP)
+    partial_value, pieces = lax.optimization_barrier((partial_value, pieces))
 
     share = row_count // layers
     head_total = summed(partial_value, Z)
-    head_total, near_across = lax.optimization_barrier((head_total, near_across))
-    slabs = (embedding, across, near, near_across)
+    head_total, pieces, own = lax.optimization_barrier((head_total, pieces, embedding))
+    near = join(pieces)
+    slabs = (embedding, lax.ppermute(own, "c", SWAP), near, lax.ppermute(near, "c", SWAP))
     my_residual = lax.dynamic_slice_in_dim(residual, layer * share, share)
     hidden = my_residual.astype(jnp.float32) + head_total
     norm_factor = lax.rsqrt(jnp.mean(hidden * hidden, axis=-1, keepdims=True) + norm_epsilon)
@@ -297,10 +319,14 @@
     numbers = jnp.arange(entry.shape[0], dtype=jnp.int32)[:, None]
     target_column = jnp.max(jnp.where(hit, numbers, -1), axis=0, keepdims=True)
     logits, stats = slab_logits(every_row, target_column, slabs)
-    column = spread(stats[:3], Z).reshape(pairs, 2, 3, rows_here)
-    column = even_first(jnp.stack([merged(column[:, 0]), merged(column[:, 1])]), odd_x)
-    stats = spread(column, ("x", "y"))
-    stats = jnp.stack([merged(stats[:, 0]), merged(stats[:, 1])])
+    every = spread(stats[:3], ("x", "y") + Z)
+    every = every.reshape(XS // 2, 2, YS, pairs, 2, 3, rows_here)
+
+    def of_parity(odd):
+        picks = [every[:, at_x, :, :, (at_x + odd) % 2] for at_x in range(2)]
+        return merged(jnp.stack(picks).reshape(-1, 3, rows_here))
+
+    stats = jnp.stack([of_parity(0), of_parity(1)])
     log_total = stats[:, 0] + jnp.log(stats[:, 1])
     every_logprob = (stats[:, 2] - log_total).reshape(2, planes, pairs, share)
     logprob = every_logprob[:, plane].transpose(1, 0, 2).reshape(row_count)

time: 311 us -> 452 us (1.45)
  Pallas kernels: 25.8 us -> 192 us
  waiting for transfers between devices: 139 us -> 116 us
  local copies, waits for them, and re-layouts: 35.3 us -> 27 us
    pallas_call x0 -> x1, Pallas kernels: none -> 168 us  [join(): pl.pallas_call(join_kernel, out_shape=jax.ShapeDtypeStruct((depth * len(p...]
    all_to_all x5 -> x4, waiting for transfers between devices: 57.9 us -> 41 us  [spread(): return lax.all_to_all(copies, axes, 0, 0, tiled=True)]
    ppermute x4, waiting for transfers between devices: 24 us -> 17.5 us  [from_neighbour(): lax.ppermute(embedding[part * quarter:(part + 1) * quarter], axes, pairs)]
    unnamed x43 -> x36, local copies, waits for them, and re-layouts: 15.7 us -> 10.1 us
    all_to_all x5 -> x4, starting transfers between devices: 26.1 us -> 29.3 us  [spread(): return lax.all_to_all(copies, axes, 0, 0, tiled=True)]
  transfers between devices with their start and end apart: 14 -> 13, of which waited for: 11 -> 9; matrix products, arithmetic and copies ran while one was open for 6% -> 4% of each run, Pallas kernels for 0% -> 37%
where the time goes in v4:
time: 452 us; the launch traced here: 451 us
  Pallas kernels  192 us (42%)
  waiting for transfers between devices  116 us (26%)
  starting transfers between devices  52.5 us (12%)
  blocking collectives  51.9 us (11%)
  local copies, waits for them, and re-layouts  27 us (6%)
  other arithmetic  5.37 us (1%)
    pallas_call x1, Pallas kernels, join(): pl.pallas_call(join_kernel, out_shape=jax.ShapeDtypeStruct((depth * len(p...  168 us
    all_to_all x4, waiting for transfers between devices, spread(): return lax.all_to_all(copies, axes, 0, 0, tiled=True)  41 us
    all_to_all x1, blocking collectives, body(): lax.all_to_all(terms.reshape(planes, pairs * share, width), ('x', 'y'), 0...  37.4 us
    all_to_all x1, waiting for transfers between devices, body(): lax.all_to_all(outgoing, ('x', 'y'), 0, 0, tiled=True)  35.6 us
    all_to_all x4, starting transfers between devices, spread(): return lax.all_to_all(copies, axes, 0, 0, tiled=True)  29.3 us
    all_to_all x1, waiting for transfers between devices, summed(): arrived = lax.all_to_all(pieces, axes, 0, 0, tiled=True)  20.5 us
    ppermute x4, waiting for transfers between devices, from_neighbour(): lax.ppermute(embedding[part * quarter:(part + 1) * quarter], axes, pairs)  17.5 us
    all_to_all x1, blocking collectives, summed(): arrived = lax.all_to_all(pieces, axes, 0, 0, tiled=True)  14.5 us
  transfers between devices with their start and end apart: 13, of which 9 were waited for; matrix products, arithmetic and copies ran while one was open for 4% of the time, Pallas kernels for 37%

profile of v4, /device:TPU:2, one launch (start us, length us, event | category | flops | bytes accessed | tf_op | source)
XLA Modules:
  0.0 450.5 jit_solution(13676603212587200125)
XLA Ops:
  1.5 1.6 broadcast_in_dim.153
  3.1 7.5 %all-to-all-start = ((bf16[16,128,512]{2,1,0:T(8,128)(2,1)}), bf16[16,128,512]{2,1,0:T(8,128)(2,1)S(1)}, u32[]{:S(2)}, u32[]{:S(2)}) async-start(bf16[16,128,512]{2,1,0:T(8,128)(2,1)} %broadcast_in_dim.153), calls=%async_computation | async-start | bytes 4194304 | tf_op jit(solution)/shard_map/all_to_all | solution.py:22
  10.6 5.1 %fusion.61 = (bf16[128,5376]{1,0:T(8,128)(2,1)}, bf16[128,5376]{1,0:T(8,128)(2,1)}, bf16[128,5376]{1,0:T(8,128)(2,1)}, bf16[128,5376]{1,0:T(8,128)(2,1)}) fusion(bf16[512,5376]{1,0:T(8,128)(2,1)} %refs_0_.3), kind=kLoop, calls=%fused_computation.156 | loop fusion | bytes 11010048 | tf_op jit(solution)/shard_map/slice | solution.py:236
  15.7 5.9 %collective-permute-start.1 = (bf16[128,5376]{1,0:T(8,128)(2,1)}, bf16[128,5376]{1,0:T(8,128)(2,1)}, u32[]{:S(2)}, u32[]{:S(2)}) collective-permute-start(bf16[128,5376]{1,0:T(8,128)(2,1)} %get-tuple-element.37), channel_id=1, source_target_pairs={{1,0},{2,1},{3,2},{4,3},{5,4},{6,5},{7,6},{0,7},{9,8},{10,9},{11,1... | collective-permute-start | bytes 4128776 | tf_op jit(solution)/shard_map/ppermute | solution.py:236
  21.6 1.9 collective-permute-start.4
  24.4 14.1 %all-to-all-done = bf16[16,128,512]{2,1,0:T(8,128)(2,1)S(1)} async-done(((bf16[16,128,512]{2,1,0:T(8,128)(2,1)}), bf16[16,128,512]{2,1,0:T(8,128)(2,1)S(1)}, u32[]{:S(2)}, u32[]{:S(2)}) %all-to-all-start) | async-done | bytes 2097184 | tf_op jit(solution)/shard_map/all_to_all | solution.py:22
  38.4 1.4 gather_fusion.1
  40.6 1.4 collective-permute-done
  43.8 3.6 fusion.65
  47.4 3.3 collective-permute-done.1.refs_0_
  50.7 3.4 collective-permute-done.2.refs_1_
  54.1 10.7 %collective-permute-done.3.refs_2_ = bf16[128,5376]{1,0:T(8,128)(2,1)} collective-permute-done((bf16[128,5376]{1,0:T(8,128)(2,1)}, bf16[128,5376]{1,0:T(8,128)(2,1)}, u32[]{:S(2)}, u32[]{:S(2)}) %collective-permute-start.3) | collective-permute-done | bytes 1376288 | tf_op jit(solution)/shard_map/ppermute | solution.py:236
  64.8 1.0 reshape.397
  65.9 8.5 %all-to-all-start.1 = ((f32[8,4,5376]{2,1,0:T(4,128)}), f32[8,4,5376]{2,1,0:T(4,128)S(1)}, u32[]{:S(2)}, u32[]{:S(2)}) async-start(f32[8,4,5376]{2,1,0:T(4,128)} %reshape.397), calls=%async_computation.1 | async-start | bytes 1376256 | tf_op jit(solution)/shard_map/all_to_all | solution.py:28
  74.4 20.5 %all-to-all-done.1 = f32[8,4,5376]{2,1,0:T(4,128)S(1)} async-done(((f32[8,4,5376]{2,1,0:T(4,128)}), f32[8,4,5376]{2,1,0:T(4,128)S(1)}, u32[]{:S(2)}, u32[]{:S(2)}) %all-to-all-start.1) | async-done | bytes 688160 | tf_op jit(solution)/shard_map/all_to_all | solution.py:28
  96.1 3.4 all-to-all-start.2
  99.7 167.9 %shard_map.149.refs_2_ = bf16[512,5376]{1,0:T(8,128)(2,1)} custom-call(bf16[128,5376]{1,0:T(8,128)(2,1)} %collective-permute-done.1.refs_0_, bf16[128,5376]{1,0:T(8,128)(2,1)} %collective-permute-done.2.refs_1_, bf16[128,5376]{1,0:T(8,128)(2,1)} %collective-permute-done.3.refs_2_, bf16[128,5376]{1,0:T(8,128)(2,1)} %collective-permute-done.4.refs_3_), custom_call_target="tpu_custom_call" | custom-call | tf_op jit(solution)/shard_map/pallas_call | solution.py:78
  268.4 1.8 broadcast_select_fusion
  270.2 6.2 %all-to-all-start.3 = ((bf16[16,16,5376]{2,1,0:T(8,128)(2,1)}), bf16[16,16,5376]{2,1,0:T(8,128)(2,1)S(1)}, u32[]{:S(2)}, u32[]{:S(2)}) async-start(bf16[16,16,5376]{2,1,0:T(8,128)(2,1)} %broadcast_select_fusion), calls=%async_computation.3 | async-start | bytes 5505024 | tf_op jit(solution)/shard_map/all_to_all | solution.py:310
  277.4 35.6 %all-to-all-done.3 = bf16[16,16,5376]{2,1,0:T(8,128)(2,1)S(1)} async-done(((bf16[16,16,5376]{2,1,0:T(8,128)(2,1)}), bf16[16,16,5376]{2,1,0:T(8,128)(2,1)S(1)}, u32[]{:S(2)}, u32[]{:S(2)}) %all-to-all-start.3) | async-done | bytes 2752544 | tf_op jit(solution)/shard_map/all_to_all | solution.py:310
  313.0 2.6 copy-done.2
  315.6 13.7 %shard_map.150 = (f32[2048,256]{1,0:T(8,128)S(1)}, f32[8,256]{1,0:T(8,128)S(1)}) custom-call(bf16[256,5376]{1,0:T(8,128)(2,1)S(1)} %bitcast.150, s32[1,256]{1,0:T(1,128)S(1)} %bitcast.152, bf16[512,5376]{1,0:T(8,128)(2,1)S(1)} %copy-done.2, bf16[512,5376]{1,0:T(8,128)(2,1)} %collective-permute-done.5.refs_1_, bf16[512,5376]{1,0:T(8,128)(2,1)} %shard_map.149.refs_2_, ...), custom_call_target="tpu_custom_call" | custom-call | flops 5637144576 | bytes 22020096 | tf_op jit(solution)/shard_map/pallas_call | solution.py:150
  329.3 1.3 copy-done.5
  331.5 15.0 %all-to-all-start.4 = ((f32[128,3,256]{2,1,0:T(4,128)}), f32[128,3,256]{2,1,0:T(4,128)S(1)}, u32[]{:S(2)}, u32[]{:S(2)}) async-start(f32[128,3,256]{2,1,0:T(4,128)} %broadcast_in_dim.170), calls=%async_computation.4 | async-start | bytes 1048576 | tf_op jit(solution)/shard_map/all_to_all | solution.py:22
  347.1 16.4 %all-to-all-done.4 = f32[128,3,256]{2,1,0:T(4,128)S(1)} async-done(((f32[128,3,256]{2,1,0:T(4,128)}), f32[128,3,256]{2,1,0:T(4,128)S(1)}, u32[]{:S(2)}, u32[]{:S(2)}) %all-to-all-start.4) | async-done | bytes 393248 | tf_op jit(solution)/shard_map/all_to_all | solution.py:22
  365.2 2.6 copy-done.3
  367.8 2.6 copy-done.4
  370.4 10.5 %shard_map.151 = bf16[256,5376]{1,0:T(8,128)(2,1)S(1)} custom-call(f32[2048,256]{1,0:T(8,128)S(1)} %copy-done.6, s32[1,256]{1,0:T(1,128)S(1)} %bitcast.153, f32[1,256]{1,0:T(1,128)S(1)} %fusion.38.log_total, f32[1,256]{1,0:T(1,128)S(1)} %broadcast_in_dim_reshape_squeeze.4.token_weight, bf16[512,5376]{1,0:T(8,128)(2,1)S(1)} %copy-done.3, ...), custom_call_target="tpu_custom_call" | custom-call | flops 5637144576 | bytes 22020096 | tf_op jit(solution)/shard_map/pallas_call | solution.py:181
  380.9 37.4 %all_to_all.40 = bf16[16,16,5376]{2,1,0:T(8,128)(2,1)S(1)} all-to-all(bf16[16,16,5376]{2,1,0:T(8,128)(2,1)S(1)} %bitcast.151), channel_id=1, replica_groups=mesh['x'=4,'y'=4,'c'=2,'zh'=4,'zl'=2] {'x','y'}, dimensions={0} | all-to-all | bytes 5505024 | tf_op jit(solution)/shard_map/all_to_all | solution.py:340
  419.1 14.5 %all_to_all.41 = bf16[8,4,5376]{2,1,0:T(4,128)(2,1)S(1)} all-to-all(bf16[8,4,5376]{2,1,0:T(4,128)(2,1)S(1)} %bitcast.158), channel_id=1, replica_groups=mesh['x'=4,'y'=4,'c'=2,'zh'=4,'zl'=2] {'zh','zl'}, dimensions={0} | all-to-all | bytes 688128 | tf_op jit(solution)/shard_map/all_to_all | solution.py:28
  434.9 3.4 all-to-all-start.7
  439.1 10.5 %all-to-all-done.7 = bf16[8,4,5376]{2,1,0:T(4,128)(2,1)S(1)} async-done(((bf16[8,4,5376]{2,1,0:T(4,128)(2,1)}), bf16[8,4,5376]{2,1,0:T(4,128)(2,1)S(1)}, u32[]{:S(2)}, u32[]{:S(2)}) %all-to-all-start.7) | async-done | bytes 344096 | tf_op jit(solution)/shard_map/all_to_all | solution.py:22
  (123 shorter events, 14.2 us)
Async XLA Ops:
  0.6 42.2 %copy-start = (bf16[32,512]{1,0:T(8,128)(2,1)S(1)}, bf16[32,512]{1,0:T(8,128)(2,1)}, u32[]{:S(2)}) copy-start(bf16[32,512]{1,0:T(8,128)(2,1)} %param.14) | copy-start | bytes 98308
  3.1 35.4 %all-to-all-start = ((bf16[16,128,512]{2,1,0:T(8,128)(2,1)}), bf16[16,128,512]{2,1,0:T(8,128)(2,1)S(1)}, u32[]{:S(2)}, u32[]{:S(2)}) async-start(bf16[16,128,512]{2,1,0:T(8,128)(2,1)} %broadcast_in_dim.153), calls=%async_computation | async-start | bytes 4194304 | tf_op jit(solution)/shard_map/all_to_all | solution.py:22
  10.6 13.0 %copy-start.11 = (s32[128]{0:T(128)S(1)}, s32[128]{0:T(128)}, u32[]{:S(2)}) copy-start(s32[128]{0:T(128)} %param.20) | copy-start | bytes 1540
  10.6 13.1 %copy-start.7 = (s32[32]{0:T(128)S(1)}, s32[32]{0:T(128)}, u32[]{:S(2)}) copy-start(s32[32]{0:T(128)} %param.19) | copy-start | bytes 388
  15.7 35.1 %collective-permute-start.1 = (bf16[128,5376]{1,0:T(8,128)(2,1)}, bf16[128,5376]{1,0:T(8,128)(2,1)}, u32[]{:S(2)}, u32[]{:S(2)}) collective-permute-start(bf16[128,5376]{1,0:T(8,128)(2,1)} %get-tuple-element.37), channel_id=1, source_target_pairs={{1,0},{2,1},{3,2},{4,3},{5,4},{6,5},{7,6},{0,7},{9,8},{10,9},{11,1... | collective-permute-start | bytes 4128776 | tf_op jit(solution)/shard_map/ppermute | solution.py:236
  21.5 32.6 %collective-permute-start.2 = (bf16[128,5376]{1,0:T(8,128)(2,1)}, bf16[128,5376]{1,0:T(8,128)(2,1)}, u32[]{:S(2)}, u32[]{:S(2)}) collective-permute-start(bf16[128,5376]{1,0:T(8,128)(2,1)} %get-tuple-element.36), channel_id=1, source_target_pairs={{7,0},{0,1},{1,2},{2,3},{3,4},{4,5},{5,6},{6,7},{15,8},{8,9},{9,10... | collective-permute-start | bytes 4128776 | tf_op jit(solution)/shard_map/ppermute | solution.py:236
  21.5 43.3 %collective-permute-start.3 = (bf16[128,5376]{1,0:T(8,128)(2,1)}, bf16[128,5376]{1,0:T(8,128)(2,1)}, u32[]{:S(2)}, u32[]{:S(2)}) collective-permute-start(bf16[128,5376]{1,0:T(8,128)(2,1)} %get-tuple-element.35), channel_id=1, source_target_pairs={{64,0},{128,64},{192,128},{0,192},{65,1},{129,65},{193,129},{1,193... | collective-permute-start | bytes 4128776 | tf_op jit(solution)/shard_map/ppermute | solution.py:236
  21.6 43.2 %collective-permute-start.4 = (bf16[128,5376]{1,0:T(8,128)(2,1)}, bf16[128,5376]{1,0:T(8,128)(2,1)}, u32[]{:S(2)}, u32[]{:S(2)}) collective-permute-start(bf16[128,5376]{1,0:T(8,128)(2,1)} %get-tuple-element.34), channel_id=1, source_target_pairs={{192,0},{0,64},{64,128},{128,192},{193,1},{1,65},{65,129},{129,193... | collective-permute-start | bytes 4128776 | tf_op jit(solution)/shard_map/ppermute | solution.py:236
  39.8 2.1 collective-permute-start
  40.5 2.3 copy-start.14
  42.1 1.2 copy-start.13
  47.4 47.6 %copy-start.9 = (bf16[32,5376]{1,0:T(8,128)(2,1)S(1)}, bf16[32,5376]{1,0:T(8,128)(2,1)}, u32[]{:S(2)}) copy-start(bf16[32,5376]{1,0:T(8,128)(2,1)} %param.24) | copy-start | bytes 1032196
  47.4 47.8 %copy-start.8 = (f32[5376]{0:T(1024)S(1)}, f32[5376]{0:T(1024)}, u32[]{:S(2)}) copy-start(f32[5376]{0:T(1024)} %param.26) | copy-start | bytes 64516
  65.9 29.0 %all-to-all-start.1 = ((f32[8,4,5376]{2,1,0:T(4,128)}), f32[8,4,5376]{2,1,0:T(4,128)S(1)}, u32[]{:S(2)}, u32[]{:S(2)}) async-start(f32[8,4,5376]{2,1,0:T(4,128)} %reshape.397), calls=%async_computation.1 | async-start | bytes 1376256 | tf_op jit(solution)/shard_map/all_to_all | solution.py:28
  96.1 172.0 %all-to-all-start.2 = ((bf16[8,4,5376]{2,1,0:T(4,128)(2,1)}), bf16[8,4,5376]{2,1,0:T(4,128)(2,1)S(1)}, u32[]{:S(2)}, u32[]{:S(2)}) async-start(bf16[8,4,5376]{2,1,0:T(4,128)(2,1)} %broadcast_in_dim.158), calls=%async_computation.2 | async-start | bytes 688128 | tf_op jit(solution)/shard_map/all_to_all | solution.py:22
  99.6 213.5 %collective-permute-start.5 = (bf16[512,5376]{1,0:T(8,128)(2,1)}, bf16[512,5376]{1,0:T(8,128)(2,1)}, u32[]{:S(2)}, u32[]{:S(2)}) collective-permute-start(bf16[512,5376]{1,0:T(8,128)(2,1)} %refs_0_.3), channel_id=1, source_target_pairs={{0,8},{8,0},{1,9},{9,1},{2,10},{10,2},{3,11},{11,3},{4,12},{12,4},... | collective-permute-start | bytes 16515080 | tf_op jit(solution)/shard_map/ppermute | solution.py:296
  267.6 45.4 %collective-permute-start.6 = (bf16[512,5376]{1,0:T(8,128)(2,1)}, bf16[512,5376]{1,0:T(8,128)(2,1)}, u32[]{:S(2)}, u32[]{:S(2)}) collective-permute-start(bf16[512,5376]{1,0:T(8,128)(2,1)} %shard_map.149.refs_2_), channel_id=1, source_target_pairs={{0,8},{8,0},{1,9},{9,1},{2,10},{10,2},{3,11},{11,3},{4,12},{12,4},... | collective-permute-start | bytes 16515080 | tf_op jit(solution)/shard_map/ppermute | solution.py:296
  270.2 6.2 %copy-start.10 = (s32[1024]{0:T(1024)S(1)}, s32[1024]{0:T(1024)}, u32[]{:S(2)}) copy-start(s32[1024]{0:T(1024)} %param.22) | copy-start | bytes 12292
  270.2 42.8 %all-to-all-start.3 = ((bf16[16,16,5376]{2,1,0:T(8,128)(2,1)}), bf16[16,16,5376]{2,1,0:T(8,128)(2,1)S(1)}, u32[]{:S(2)}, u32[]{:S(2)}) async-start(bf16[16,16,5376]{2,1,0:T(8,128)(2,1)} %broadcast_select_fusion), calls=%async_computation.3 | async-start | bytes 5505024 | tf_op jit(solution)/shard_map/all_to_all | solution.py:310
  313.0 2.6 copy-start.2
  315.6 30.9 %copy-start.15 = (f32[128]{0:T(128)S(1)}, f32[128]{0:T(128)}, u32[]{:S(2)}) copy-start(f32[128]{0:T(128)} %param.23) | copy-start | bytes 1540
  315.6 31.0 %copy-start.12 = (s32[128]{0:T(128)S(1)}, s32[128]{0:T(128)}, u32[]{:S(2)}) copy-start(s32[128]{0:T(128)} %param.21) | copy-start | bytes 1540
  329.2 1.4 copy-start.5
  331.5 32.0 %all-to-all-start.4 = ((f32[128,3,256]{2,1,0:T(4,128)}), f32[128,3,256]{2,1,0:T(4,128)S(1)}, u32[]{:S(2)}, u32[]{:S(2)}) async-start(f32[128,3,256]{2,1,0:T(4,128)} %broadcast_in_dim.170), calls=%async_computation.4 | async-start | bytes 1048576 | tf_op jit(solution)/shard_map/all_to_all | solution.py:22
  363.6 1.6 copy-start.6
  365.2 2.6 copy-start.3
  367.8 2.6 copy-start.4
  419.0 31.6 %copy-start.1 = (bf16[32,512]{1,0:T(8,128)(2,1)S(1)}, bf16[32,512]{1,0:T(8,128)(2,1)}, u32[]{:S(2)}) copy-start(bf16[32,512]{1,0:T(8,128)(2,1)} %param.14) | copy-start | bytes 98308
  434.9 14.7 %all-to-all-start.7 = ((bf16[8,4,5376]{2,1,0:T(4,128)(2,1)}), bf16[8,4,5376]{2,1,0:T(4,128)(2,1)S(1)}, u32[]{:S(2)}, u32[]{:S(2)}) async-start(bf16[8,4,5376]{2,1,0:T(4,128)(2,1)} %broadcast_in_dim.175), calls=%async_computation.7 | async-start | bytes 688128 | tf_op jit(solution)/shard_map/all_to_all | solution.py:22

commit v5 on v2

--- a/solution.py
+++ b/solution.py
@@ -1,6 +1,8 @@
 import jax
 import jax.numpy as jnp
 from jax import lax
+from jax.experimental import pallas as pl
+from jax.experimental.pallas import tpu as pltpu
 from jax.sharding import Mesh
 from jax.sharding import PartitionSpec as P
 
@@ -52,6 +54,145 @@
     top = jnp.max(stats[:, 0], axis=0)
     total = jnp.sum(stats[:, 1] * jnp.exp(stats[:, 0] - top[None]), axis=0)
     return jnp.stack([top, total, jnp.sum(stats[:, 2], axis=0)])
+
+
+NT = (((1,), (1,)), ((), ()))
+
+
+def placed_rows(parts):
+    starts = [0]
+    for part in parts:
+        starts.append(starts[-1] + part.shape[0])
+    return starts
+
+
+def logits_kernel(rows, target_column, *refs):
+    parts, (logits, stats, held, held_rows, arrivals, rows_arrival) = refs[:-6], refs[-6:]
+    starts = placed_rows(parts)
+    rows_copy = pltpu.make_async_copy(rows, held_rows, rows_arrival)
+    rows_copy.start()
+    copies = [
+        pltpu.make_async_copy(part, held.at[pl.ds(start, part.shape[0])], arrivals.at[k])
+        for k, (part, start) in enumerate(zip(parts, starts))
+    ]
+    for copy in copies:
+        copy.start()
+    rows_copy.wait()
+    depth = parts[0].shape[0]
+    top = total = picked = None
+    for start in range(0, starts[-1], depth):
+        for copy, at in zip(copies, starts):
+            if start <= at < start + depth:
+                copy.wait()
+        block = lax.dot_general(
+            held[pl.ds(start, depth), :], held_rows[...], NT, preferred_element_type=jnp.float32
+        )
+        logits[pl.ds(start, depth), :] = block
+        hit = lax.broadcasted_iota(jnp.int32, block.shape, 0) + start == target_column[...]
+        block_picked = jnp.sum(jnp.where(hit, block, 0.0), axis=0, keepdims=True)
+        block_top = jnp.max(block, axis=0, keepdims=True)
+        new_top = block_top if start == 0 else jnp.maximum(top, block_top)
+        block_total = jnp.sum(jnp.exp(block - new_top), axis=0, keepdims=True)
+        total = block_total if start == 0 else total * jnp.exp(top - new_top) + block_total
+        picked = block_picked if start == 0 else picked + block_picked
+        top = new_top
+    line = lax.broadcasted_iota(jnp.int32, stats.shape, 0)
+    stats[...] = jnp.where(line == 0, top, jnp.where(line == 1, total, picked))
+
+
+def gradient_kernel(logits, target_column, log_total, token_weight, *refs):
+    parts, (terms, held, held_logits, grad, arrivals, logits_arrival) = refs[:-6], refs[-6:]
+    starts = placed_rows(parts)
+    tile = held.shape[2]
+    steps = terms.shape[1] // tile
+
+    def fetch(step):
+        slot = step % 2
+        copies = [
+            pltpu.make_async_copy(
+                part.at[:, pl.ds(step * tile, tile)],
+                held.at[slot, pl.ds(start, part.shape[0])],
+                arrivals.at[slot, k],
+            )
+            for k, (part, start) in enumerate(zip(parts, starts))
+        ]
+        for copy in copies:
+            copy.start()
+        return copies
+
+    logits_copy = pltpu.make_async_copy(logits, held_logits, logits_arrival)
+    logits_copy.start()
+    coming = fetch(0)
+    logits_copy.wait()
+    chunk = parts[0].shape[0] // 2
+    for start in range(0, starts[-1], chunk):
+        block = held_logits[pl.ds(start, chunk), :]
+        hit = lax.broadcasted_iota(jnp.int32, block.shape, 0) + start == target_column[...]
+        block = jnp.where(hit, 1.0, 0.0) - jnp.exp(block - log_total[...])
+        grad[:, pl.ds(start, chunk)] = (token_weight[...] * block).T.astype(jnp.bfloat16)
+    for step in range(steps):
+        following = fetch(step + 1) if step + 1 < steps else None
+        for copy in coming:
+            copy.wait()
+        coming = following
+        terms[:, pl.ds(step * tile, tile)] = jnp.dot(
+            grad[...], held[step % 2], preferred_element_type=jnp.float32
+        ).astype(jnp.bfloat16)
+
+
+def slab_logits(rows, target_column, parts):
+    width = rows.shape[1]
+    count, entries = rows.shape[0], placed_rows(parts)[-1]
+    whole = pl.BlockSpec(memory_space=pltpu.VMEM)
+    remain = pl.BlockSpec(memory_space=pltpu.HBM)
+    return pl.pallas_call(
+        logits_kernel,
+        out_shape=(
+            jax.ShapeDtypeStruct((entries, count), jnp.float32),
+            jax.ShapeDtypeStruct((8, count), jnp.float32),
+        ),
+        in_specs=[remain, whole] + [remain] * len(parts),
+        out_specs=[whole, whole],
+        scratch_shapes=[
+            pltpu.VMEM((entries, width), jnp.bfloat16),
+            pltpu.VMEM((count, width), jnp.bfloat16),
+            pltpu.SemaphoreType.DMA((len(parts),)),
+            pltpu.SemaphoreType.DMA,
+        ],
+        compiler_params=pltpu.CompilerParams(vmem_limit_bytes=44 * 1024 * 1024),
+        cost_estimate=pl.CostEstimate(
+            flops=2 * count * entries * width,
+            bytes_accessed=2 * entries * width,
+            transcendentals=count * entries,
+        ),
+    )(rows, target_column, *parts)
+
+
+def slab_gradient(logits, target_column, log_total, token_weight, parts):
+    width = parts[0].shape[1]
+    entries, count = logits.shape
+    tile = next(t for t in (768, 512, 256, 128) if width % t == 0)
+    whole = pl.BlockSpec(memory_space=pltpu.VMEM)
+    remain = pl.BlockSpec(memory_space=pltpu.HBM)
+    return pl.pallas_call(
+        gradient_kernel,
+        out_shape=jax.ShapeDtypeStruct((count, width), jnp.bfloat16),
+        in_specs=[remain] + [whole] * 3 + [remain] * len(parts),
+        out_specs=whole,
+        scratch_shapes=[
+            pltpu.VMEM((2, entries, tile), jnp.bfloat16),
+            pltpu.VMEM((entries, count), jnp.float32),
+            pltpu.VMEM((count, entries), jnp.bfloat16),
+            pltpu.SemaphoreType.DMA((2, len(parts))),
+            pltpu.SemaphoreType.DMA,
+        ],
+        compiler_params=pltpu.CompilerParams(vmem_limit_bytes=44 * 1024 * 1024),
+        cost_estimate=pl.CostEstimate(
+            flops=2 * count * entries * width,
+            bytes_accessed=2 * entries * width,
+            transcendentals=count * entries,
+        ),
+    )(logits, target_column, log_total, token_weight, *parts)
 
 
 def body(
@@ -81,23 +222,32 @@
     planes = XS * YS
     layer = lax.axis_index(Z)
     layers = lax.axis_size(Z)
-    parity = lax.axis_index("zl")
+    along_x, along_y = lax.axis_index("x"), lax.axis_index("y")
+    parity = (along_x + along_y) % 2
     dp_index = plane * CS + core
 
-    half_slab = vocab_slab // 2
-    ring = range(layers)
-    from_next = lax.ppermute(embedding[:half_slab], Z, [((k + 1) % layers, k) for k in ring])
-    from_prev = lax.ppermute(embedding[half_slab:], Z, [(k, (k + 1) % layers) for k in ring])
-    near = jnp.concatenate([from_next, from_prev], axis=0)
-    table = jnp.concatenate(
-        [embedding, lax.ppermute(embedding, "c", SWAP), near, lax.ppermute(near, "c", SWAP)], axis=0
+    quarter = vocab_slab // 4
+
+    def from_neighbour(part, axes, ahead):
+        size = lax.axis_size(axes)
+        pairs = [((k + ahead) % size, k) for k in range(size)]
+        return lax.ppermute(embedding[part * quarter : (part + 1) * quarter], axes, pairs)
+
+    pieces = (
+        from_neighbour(0, "x", 1),
+        from_neighbour(1, "x", -1),
+        from_neighbour(2, "y", 1),
+        from_neighbour(3, "y", -1),
     )
     slab_column = jnp.arange(vocab_slab, dtype=jnp.int32)
-    near_layer = jnp.where(slab_column < half_slab, layer + 1, layer - 1) % layers
+    source = slab_column // quarter
+    near_x = along_x + jnp.where(source == 0, 1, 0) - jnp.where(source == 1, 1, 0)
+    near_y = along_y + jnp.where(source == 2, 1, 0) - jnp.where(source == 3, 1, 0)
+    near_plane = near_x % XS * YS + near_y % YS
     entry = jnp.concatenate(
         [
-            ((plane * CS + which) * layers + held_layer) * vocab_slab + slab_column
-            for held_layer in (layer, near_layer)
+            ((at_plane * CS + which) * layers + layer) * vocab_slab + slab_column
+            for at_plane in (plane, near_plane)
             for which in (core, 1 - core)
         ]
     )
@@ -133,6 +283,7 @@
     )
     partial_value = jnp.dot(attended, out_proj, preferred_element_type=jnp.float32)
 
+
     share = row_count // layers
     head_total = summed(partial_value, Z)
     my_residual = lax.dynamic_slice_in_dim(residual, layer * share, share)
@@ -141,37 +292,55 @@
     normed = (hidden * norm_factor * norm_gain).astype(jnp.bfloat16)
 
     pairs = layers // 2
-    normed = spread(normed, "zh").reshape(pairs * share, width)
+    by_parity = spread(normed, Z)
+    by_parity, pieces, own = lax.optimization_barrier((by_parity, pieces, embedding))
+    swapped = [lax.ppermute(part, "c", SWAP) for part in (own,) + tuple(pieces)]
+    parts = (embedding, swapped[0]) + tuple(pieces) + tuple(swapped[1:])
+    by_parity = by_parity.reshape(pairs, 2, share, width).transpose(1, 0, 2, 3)
+    by_parity = by_parity.reshape(2, pairs * share, width)
     rows_here = planes * pairs * share
-    every_row = spread(normed, ("x", "y")).reshape(rows_here, width)
+    to_plane = jnp.arange(planes)
+    to_odd = ((to_plane // YS + to_plane) % 2 == 1)[:, None, None]
+    outgoing = jnp.where(to_odd, by_parity[1][None], by_parity[0][None])
+    every_row = lax.all_to_all(outgoing, ("x", "y"), 0, 0, tiled=True).reshape(rows_here, width)
 
     def of_rows(values):
         return values.reshape(planes, CS, pairs, 2, share)[:, core, :, parity].reshape(rows_here)
 
-    logits = lax.dot_general(
-        every_row, table, (((1,), (1,)), ((), ())), preferred_element_type=jnp.float32
-    )
-    hit = entry[None, :] == of_rows(targets)[:, None]
-    top = jnp.max(logits, axis=1)
-    total = jnp.sum(jnp.exp(logits - top[:, None]), axis=1)
-    picked = jnp.sum(jnp.where(hit, logits, 0.0), axis=1)
-    stats = jnp.stack([top, total, picked])
-    stats = merged(spread(stats, "zh"))
-    stats = merged(spread(stats, ("x", "y")))
-    log_total = stats[0] + jnp.log(stats[1])
-    first_row = (plane * pairs + lax.axis_index("zh")) * share
-    logprob = lax.dynamic_slice_in_dim(stats[2] - log_total, first_row, share)
-    logprob = spread(logprob, Z).reshape(row_count)
+    hit = entry[:, None] == of_rows(targets)[None, :]
+    numbers = jnp.arange(entry.shape[0], dtype=jnp.int32)[:, None]
+    target_column = jnp.max(jnp.where(hit, numbers, -1), axis=0, keepdims=True)
+    logits, stats = slab_logits(every_row, target_column, parts)
+    stats = merged(spread(stats[:3], Z))
+    stats = spread(stats, ("x", "y")).reshape(XS // 2, 2, YS // 2, 2, 3, rows_here)
+
+    def of_parity(odd):
+        picks = [stats[:, at_x, :, (at_x + odd) % 2] for at_x in range(2)]
+        return merged(jnp.stack(picks).reshape(-1, 3, rows_here))
+
+    stats = jnp.stack([of_parity(0), of_parity(1)])
+    log_total = stats[:, 0] + jnp.log(stats[:, 1])
+    every_logprob = (stats[:, 2] - log_total).reshape(2, planes, pairs, share)
+    logprob = every_logprob[:, plane].transpose(1, 0, 2).reshape(row_count)
 
     row_ids = jnp.arange(targets.shape[0], dtype=jnp.int32)
     live_token = row_ids % CLEN < jnp.repeat(completion_lengths, CLEN)
     token_weight = of_rows(jnp.where(live_token, -jnp.repeat(advantages, CLEN), 0.0))
-    logit_grad = (
-        token_weight[:, None] * (hit.astype(jnp.float32) - jnp.exp(logits - log_total[:, None]))
-    ).astype(jnp.bfloat16)
-    terms = jnp.dot(logit_grad, table, preferred_element_type=jnp.float32)
-    summed_rows = summed(terms.astype(jnp.bfloat16), ("x", "y"))
-    normed_grad = summed(summed_rows, "zh")
+    terms = slab_gradient(
+        logits, target_column, log_total[parity][None], token_weight[None], parts
+    )
+    arrived = lax.all_to_all(
+        terms.reshape(planes, pairs * share, width), ("x", "y"), 0, 0, tiled=True
+    )
+    arrived = arrived.astype(jnp.float32)
+    both = jnp.stack(
+        [
+            jnp.sum(jnp.where(to_odd, 0.0, arrived), axis=0),
+            jnp.sum(jnp.where(to_odd, arrived, 0.0), axis=0),
+        ]
+    )
+    both = both.reshape(2, pairs, share, width).transpose(1, 0, 2, 3).reshape(row_count, width)
+    normed_grad = summed(both.astype(jnp.bfloat16), Z)
     hidden_grad = norm_gain * norm_factor * normed_grad - hidden * norm_factor**3 * jnp.mean(
         norm_gain * normed_grad * hidden, axis=-1, keepdims=True
     )

time: 291 us -> 280 us (0.962)
  Pallas kernels: 0 us -> 31.5 us
  local copies, waits for them, and re-layouts: 41.2 us -> 15.9 us
  matrix products: 29.9 us -> 5.31 us
  blocking collectives: 33.4 us -> 50.2 us
  starting transfers between devices: 57.3 us -> 51.3 us
  waiting for transfers between devices: 117 us -> 113 us
    all_to_all x0 -> x1, blocking collectives: none -> 36.5 us  [body(): lax.all_to_all(terms.reshape(planes, pairs * share, width), ('x', 'y'), 0...]
    pallas_call x0 -> x2, Pallas kernels: none -> 31.5 us  [the longest x1 17.3 us: slab_logits(): pl.pallas_call(logits_kernel, out_shape=(jax.ShapeDtypeStruct((entries, c...]
    all_to_all x0 -> x1, waiting for transfers between devices: none -> 29.1 us  [body(): lax.all_to_all(outgoing, ('x', 'y'), 0, 0, tiled=True)]
    dot_general x2 -> x0, matrix products: 24.5 us -> none  [the longest x1 14.2 us: body(): terms = jnp.dot(logit_grad, table, preferred_element_type=jnp.float32)]
    all_to_all x1, blocking collectives: 33.4 us -> 13.7 us  [summed(): arrived = lax.all_to_all(pieces, axes, 0, 0, tiled=True)]
    all_to_all x7 -> x5, waiting for transfers between devices: 70.7 us -> 51.8 us  [spread(): return lax.all_to_all(copies, axes, 0, 0, tiled=True)]
    unnamed x38 -> x24, local copies, waits for them, and re-layouts: 16.6 us -> 0.08 us
    ppermute x4 -> x9, waiting for transfers between devices: 35.2 us -> 20 us  [the longest x4 13.1 us: from_neighbour(): lax.ppermute(embedding[part * quarter:(part + 1) * quarter], axes, pairs)]
  transfers between devices with their start and end apart: 14 -> 17, of which waited for: 10 -> 16; matrix products, arithmetic and copies ran while one was open for 16% -> 5% of each run, Pallas kernels for 0% -> 0%
where the time goes in v5:
time: 280 us; the launch traced here: 279 us
  waiting for transfers between devices  113 us (40%)
  starting transfers between devices  51.3 us (18%)
  blocking collectives  50.2 us (18%)
  Pallas kernels  31.5 us (11%)
  local copies, waits for them, and re-layouts  15.9 us (6%)
  other arithmetic  10.3 us (4%)
  matrix products  5.31 us (2%)
    all_to_all x5, waiting for transfers between devices, spread(): return lax.all_to_all(copies, axes, 0, 0, tiled=True)  51.8 us
    all_to_all x1, blocking collectives, body(): lax.all_to_all(terms.reshape(planes, pairs * share, width), ('x', 'y'), 0...  36.5 us
    all_to_all x1, waiting for transfers between devices, body(): lax.all_to_all(outgoing, ('x', 'y'), 0, 0, tiled=True)  29.1 us
    all_to_all x5, starting transfers between devices, spread(): return lax.all_to_all(copies, axes, 0, 0, tiled=True)  28.8 us
    pallas_call x1, Pallas kernels, slab_logits(): pl.pallas_call(logits_kernel, out_shape=(jax.ShapeDtypeStruct((entries, c...  17.3 us
    pallas_call x1, Pallas kernels, slab_gradient(): pl.pallas_call(gradient_kernel, out_shape=jax.ShapeDtypeStruct((count, wi...  14.2 us
    all_to_all x1, blocking collectives, summed(): arrived = lax.all_to_all(pieces, axes, 0, 0, tiled=True)  13.7 us
    ppermute x4, waiting for transfers between devices, from_neighbour(): lax.ppermute(embedding[part * quarter:(part + 1) * quarter], axes, pairs)  13.1 us
  transfers between devices with their start and end apart: 17, of which 16 were waited for; matrix products, arithmetic and copies ran while one was open for 5% of the time, Pallas kernels for 0%

profile of v5, /device:TPU:2, one launch (start us, length us, event | category | flops | bytes accessed | tf_op | source)
XLA Modules:
  0.0 279.0 jit_solution(4168829901203157920)
XLA Ops:
  1.5 1.6 broadcast_in_dim.173
  3.1 7.6 %all-to-all-start = ((bf16[16,128,512]{2,1,0:T(8,128)(2,1)}), bf16[16,128,512]{2,1,0:T(8,128)(2,1)S(1)}, u32[]{:S(2)}, u32[]{:S(2)}) async-start(bf16[16,128,512]{2,1,0:T(8,128)(2,1)} %broadcast_in_dim.173), calls=%async_computation | async-start | bytes 4194304 | tf_op jit(solution)/shard_map/all_to_all | solution.py:22
  11.5 26.3 %all-to-all-done = bf16[16,128,512]{2,1,0:T(8,128)(2,1)S(1)} async-done(((bf16[16,128,512]{2,1,0:T(8,128)(2,1)}), bf16[16,128,512]{2,1,0:T(8,128)(2,1)S(1)}, u32[]{:S(2)}, u32[]{:S(2)}) %all-to-all-start) | async-done | bytes 2097184 | tf_op jit(solution)/shard_map/all_to_all | solution.py:22
  37.9 1.4 gather_fusion.1
  40.0 1.4 collective-permute-done
  43.2 4.4 %fusion.3 = f32[8,4,5376]{2,1,0:T(4,128)} fusion(bf16[8,4,512]{2,1,0:T(4,128)(2,1)S(1)} %convert_element_type.46, bf16[512,5376]{1,0:T(8,128)(2,1)} %param.25), kind=kOutput, calls=%fused_computation.8 | convolution fusion | flops 176160768 | bytes 6225920 | tf_op jit(solution)/shard_map/dot_general | solution.py:284
  47.7 8.5 %all-to-all-start.1 = ((f32[8,4,5376]{2,1,0:T(4,128)}), f32[8,4,5376]{2,1,0:T(4,128)S(1)}, u32[]{:S(2)}, u32[]{:S(2)}) async-start(f32[8,4,5376]{2,1,0:T(4,128)} %fusion.3), calls=%async_computation.1 | async-start | bytes 1376256 | tf_op jit(solution)/shard_map/all_to_all | solution.py:28
  56.1 5.1 %fusion.70 = (bf16[128,5376]{1,0:T(8,128)(2,1)}, bf16[128,5376]{1,0:T(8,128)(2,1)}, bf16[128,5376]{1,0:T(8,128)(2,1)}, bf16[128,5376]{1,0:T(8,128)(2,1)}) fusion(bf16[512,5376]{1,0:T(8,128)(2,1)} %refs_0_.3), kind=kLoop, calls=%fused_computation.168 | loop fusion | bytes 11010048 | tf_op jit(solution)/shard_map/slice | solution.py:234
  61.2 3.3 %collective-permute-start.1 = (bf16[128,5376]{1,0:T(8,128)(2,1)}, bf16[128,5376]{1,0:T(8,128)(2,1)S(1)}, u32[]{:S(2)}, u32[]{:S(2)}) collective-permute-start(bf16[128,5376]{1,0:T(8,128)(2,1)} %get-tuple-element.31), channel_id=1, source_target_pairs={{64,0},{128,64},{192,128},{0,192},{65,1},{129,65},{193,129},{1,193... | collective-permute-start | bytes 4128776 | tf_op jit(solution)/shard_map/ppermute | solution.py:234
  64.7 1.8 collective-permute-start.4
  66.6 10.9 %all-to-all-done.1 = f32[8,4,5376]{2,1,0:T(4,128)S(1)} async-done(((f32[8,4,5376]{2,1,0:T(4,128)}), f32[8,4,5376]{2,1,0:T(4,128)S(1)}, u32[]{:S(2)}, u32[]{:S(2)}) %all-to-all-start.1) | async-done | bytes 688160 | tf_op jit(solution)/shard_map/all_to_all | solution.py:28
  78.2 1.1 multiply_reduce_fusion.1
  81.1 3.4 %all-to-all-start.2 = ((bf16[8,4,5376]{2,1,0:T(4,128)(2,1)}), bf16[8,4,5376]{2,1,0:T(4,128)(2,1)S(1)}, u32[]{:S(2)}, u32[]{:S(2)}) async-start(bf16[8,4,5376]{2,1,0:T(4,128)(2,1)} %broadcast_in_dim.178), calls=%async_computation.2 | async-start | bytes 688128 | tf_op jit(solution)/shard_map/all_to_all | solution.py:22
  84.6 9.7 %collective-permute-done.1.refs_2_ = bf16[128,5376]{1,0:T(8,128)(2,1)S(1)} collective-permute-done((bf16[128,5376]{1,0:T(8,128)(2,1)}, bf16[128,5376]{1,0:T(8,128)(2,1)S(1)}, u32[]{:S(2)}, u32[]{:S(2)}) %collective-permute-start.1) | collective-permute-done | bytes 1376288 | tf_op jit(solution)/shard_map/ppermute | solution.py:234
  94.3 2.1 collective-permute-done.2.refs_3_
  96.5 1.2 collective-permute-done.4.refs_5_
  98.8 1.9 broadcast_select_fusion
  100.8 7.7 %all-to-all-start.3 = ((bf16[16,16,5376]{2,1,0:T(8,128)(2,1)}), bf16[16,16,5376]{2,1,0:T(8,128)(2,1)}, u32[]{:S(2)}, u32[]{:S(2)}) async-start(bf16[16,16,5376]{2,1,0:T(8,128)(2,1)} %broadcast_select_fusion), calls=%async_computation.3 | async-start | bytes 5505024 | tf_op jit(solution)/shard_map/all_to_all | solution.py:305
  111.7 3.9 %collective-permute-done.7.refs_7_ = bf16[128,5376]{1,0:T(8,128)(2,1)} collective-permute-done((bf16[128,5376]{1,0:T(8,128)(2,1)S(1)}, bf16[128,5376]{1,0:T(8,128)(2,1)}, u32[]{:S(2)}, u32[]{:S(2)}) %collective-permute-start.7) | collective-permute-done | bytes 1376288 | tf_op jit(solution)/shard_map/ppermute | solution.py:297
  115.9 2.0 collective-permute-done.9.refs_9_
  117.9 29.1 %all-to-all-done.3 = bf16[16,16,5376]{2,1,0:T(8,128)(2,1)} async-done(((bf16[16,16,5376]{2,1,0:T(8,128)(2,1)}), bf16[16,16,5376]{2,1,0:T(8,128)(2,1)}, u32[]{:S(2)}, u32[]{:S(2)}) %all-to-all-start.3) | async-done | bytes 2752544 | tf_op jit(solution)/shard_map/all_to_all | solution.py:305
  147.0 17.3 %shard_map.149 = (f32[2048,256]{1,0:T(8,128)}, f32[8,256]{1,0:T(8,128)S(1)}) custom-call(bf16[256,5376]{1,0:T(8,128)(2,1)} %bitcast.23.rows, s32[1,256]{1,0:T(1,128)S(1)} %bitcast.163, bf16[512,5376]{1,0:T(8,128)(2,1)} %refs_0_.3, bf16[512,5376]{1,0:T(8,128)(2,1)} %collective-permute-done.5.refs_1_, bf16[128,5376]{1,0:T(8,128)(2,1)S(1)} %collective-permute-done.1.refs_2_, ...), custom_call_target="tpu_custom_call" | custom-call | flops 5637144576 | bytes 22020096 | tf_op jit(solution)/shard_map/pallas_call | solution.py:148
  164.9 4.5 %all-to-all-start.4 = ((f32[8,3,256]{2,1,0:T(4,128)}), f32[8,3,256]{2,1,0:T(4,128)S(1)}, u32[]{:S(2)}, u32[]{:S(2)}) async-start(f32[8,3,256]{2,1,0:T(4,128)} %broadcast_in_dim.186), calls=%async_computation.4 | async-start | bytes 65536 | tf_op jit(solution)/shard_map/all_to_all | solution.py:22
  169.4 8.0 %all-to-all-done.4 = f32[8,3,256]{2,1,0:T(4,128)S(1)} async-done(((f32[8,3,256]{2,1,0:T(4,128)}), f32[8,3,256]{2,1,0:T(4,128)S(1)}, u32[]{:S(2)}, u32[]{:S(2)}) %all-to-all-start.4) | async-done | bytes 24608 | tf_op jit(solution)/shard_map/all_to_all | solution.py:22
  178.2 9.8 %all-to-all-start.5 = ((f32[16,3,256]{2,1,0:T(4,128)}), f32[16,3,256]{2,1,0:T(4,128)S(1)}, u32[]{:S(2)}, u32[]{:S(2)}) async-start(f32[16,3,256]{2,1,0:T(4,128)} %broadcast_in_dim.187), calls=%async_computation.5 | async-start | bytes 131072 | tf_op jit(solution)/shard_map/all_to_all | solution.py:22
  188.2 6.0 %all-to-all-done.5 = f32[16,3,256]{2,1,0:T(4,128)S(1)} async-done(((f32[16,3,256]{2,1,0:T(4,128)}), f32[16,3,256]{2,1,0:T(4,128)S(1)}, u32[]{:S(2)}, u32[]{:S(2)}) %all-to-all-start.5) | async-done | bytes 49184 | tf_op jit(solution)/shard_map/all_to_all | solution.py:22
  194.6 14.2 %shard_map.150 = bf16[256,5376]{1,0:T(8,128)(2,1)} custom-call(f32[2048,256]{1,0:T(8,128)} %get-tuple-element.17.logits, s32[1,256]{1,0:T(1,128)S(1)} %bitcast.164, f32[1,256]{1,0:T(1,128)S(1)} %fusion.47.log_total, f32[1,256]{1,0:T(1,128)S(1)} %broadcast_in_dim_reshape_squeeze.4.token_weight, bf16[512,5376]{1,0:T(8,128)(2,1)} %refs_0_.3, ...), custom_call_target="tpu_custom_call" | custom-call | flops 5637144576 | bytes 22020096 | tf_op jit(solution)/shard_map/pallas_call | solution.py:177
  208.8 36.5 %all_to_all.45 = bf16[16,16,5376]{2,1,0:T(8,128)(2,1)S(1)} all-to-all(bf16[16,16,5376]{2,1,0:T(8,128)(2,1)} %bitcast.165), channel_id=1, replica_groups=mesh['x'=4,'y'=4,'c'=2,'zh'=4,'zl'=2] {'x','y'}, dimensions={0} | all-to-all | bytes 5505024 | tf_op jit(solution)/shard_map/all_to_all | solution.py:332
  246.6 13.7 %all_to_all.46 = bf16[8,4,5376]{2,1,0:T(4,128)(2,1)S(1)} all-to-all(bf16[8,4,5376]{2,1,0:T(4,128)(2,1)S(1)} %bitcast.167), channel_id=1, replica_groups=mesh['x'=4,'y'=4,'c'=2,'zh'=4,'zl'=2] {'zh','zl'}, dimensions={0} | all-to-all | bytes 688128 | tf_op jit(solution)/shard_map/all_to_all | solution.py:28
  260.5 1.1 multiply_reduce_fusion
  263.4 3.4 %all-to-all-start.8 = ((bf16[8,4,5376]{2,1,0:T(4,128)(2,1)}), bf16[8,4,5376]{2,1,0:T(4,128)(2,1)S(1)}, u32[]{:S(2)}, u32[]{:S(2)}) async-start(bf16[8,4,5376]{2,1,0:T(4,128)(2,1)} %broadcast_in_dim.193), calls=%async_computation.8 | async-start | bytes 688128 | tf_op jit(solution)/shard_map/all_to_all | solution.py:22
  267.6 10.5 %all-to-all-done.8 = bf16[8,4,5376]{2,1,0:T(4,128)(2,1)S(1)} async-done(((bf16[8,4,5376]{2,1,0:T(4,128)(2,1)}), bf16[8,4,5376]{2,1,0:T(4,128)(2,1)S(1)}, u32[]{:S(2)}, u32[]{:S(2)}) %all-to-all-start.8) | async-done | bytes 344096 | tf_op jit(solution)/shard_map/all_to_all | solution.py:22
  (123 shorter events, 18.3 us)
Async XLA Ops:
  0.6 41.6 %copy-start = (bf16[32,512]{1,0:T(8,128)(2,1)S(1)}, bf16[32,512]{1,0:T(8,128)(2,1)}, u32[]{:S(2)}) copy-start(bf16[32,512]{1,0:T(8,128)(2,1)} %param.14) | copy-start | bytes 98308
  3.1 7.6 %copy-start.5 = (s32[128]{0:T(128)S(1)}, s32[128]{0:T(128)}, u32[]{:S(2)}) copy-start(s32[128]{0:T(128)} %param.20) | copy-start | bytes 1540
  3.1 7.8 %copy-start.1 = (s32[32]{0:T(128)S(1)}, s32[32]{0:T(128)}, u32[]{:S(2)}) copy-start(s32[32]{0:T(128)} %param.19) | copy-start | bytes 388
  3.1 34.8 %all-to-all-start = ((bf16[16,128,512]{2,1,0:T(8,128)(2,1)}), bf16[16,128,512]{2,1,0:T(8,128)(2,1)S(1)}, u32[]{:S(2)}, u32[]{:S(2)}) async-start(bf16[16,128,512]{2,1,0:T(8,128)(2,1)} %broadcast_in_dim.173), calls=%async_computation | async-start | bytes 4194304 | tf_op jit(solution)/shard_map/all_to_all | solution.py:22
  39.2 2.1 collective-permute-start
  40.0 2.3 copy-start.8
  41.5 1.2 copy-start.7
  47.7 29.8 %all-to-all-start.1 = ((f32[8,4,5376]{2,1,0:T(4,128)}), f32[8,4,5376]{2,1,0:T(4,128)S(1)}, u32[]{:S(2)}, u32[]{:S(2)}) async-start(f32[8,4,5376]{2,1,0:T(4,128)} %fusion.3), calls=%async_computation.1 | async-start | bytes 1376256 | tf_op jit(solution)/shard_map/all_to_all | solution.py:28
  56.1 23.2 %copy-start.3 = (f32[5376]{0:T(1024)S(1)}, f32[5376]{0:T(1024)}, u32[]{:S(2)}) copy-start(f32[5376]{0:T(1024)} %param.26) | copy-start | bytes 64516
  61.2 33.1 %collective-permute-start.1 = (bf16[128,5376]{1,0:T(8,128)(2,1)}, bf16[128,5376]{1,0:T(8,128)(2,1)S(1)}, u32[]{:S(2)}, u32[]{:S(2)}) collective-permute-start(bf16[128,5376]{1,0:T(8,128)(2,1)} %get-tuple-element.31), channel_id=1, source_target_pairs={{64,0},{128,64},{192,128},{0,192},{65,1},{129,65},{193,129},{1,193... | collective-permute-start | bytes 4128776 | tf_op jit(solution)/shard_map/ppermute | solution.py:234
  64.5 31.9 %collective-permute-start.2 = (bf16[128,5376]{1,0:T(8,128)(2,1)}, bf16[128,5376]{1,0:T(8,128)(2,1)S(1)}, u32[]{:S(2)}, u32[]{:S(2)}) collective-permute-start(bf16[128,5376]{1,0:T(8,128)(2,1)} %get-tuple-element.30), channel_id=1, source_target_pairs={{192,0},{0,64},{64,128},{128,192},{193,1},{1,65},{65,129},{129,193... | collective-permute-start | bytes 4128776 | tf_op jit(solution)/shard_map/ppermute | solution.py:234
  64.5 32.0 %collective-permute-start.3 = (bf16[128,5376]{1,0:T(8,128)(2,1)}, bf16[128,5376]{1,0:T(8,128)(2,1)}, u32[]{:S(2)}, u32[]{:S(2)}) collective-permute-start(bf16[128,5376]{1,0:T(8,128)(2,1)} %get-tuple-element.29), channel_id=1, source_target_pairs={{16,0},{32,16},{48,32},{0,48},{17,1},{33,17},{49,33},{1,49},{18,2}... | collective-permute-start | bytes 4128776 | tf_op jit(solution)/shard_map/ppermute | solution.py:234
  64.7 33.0 %collective-permute-start.4 = (bf16[128,5376]{1,0:T(8,128)(2,1)}, bf16[128,5376]{1,0:T(8,128)(2,1)}, u32[]{:S(2)}, u32[]{:S(2)}) collective-permute-start(bf16[128,5376]{1,0:T(8,128)(2,1)} %get-tuple-element.28), channel_id=1, source_target_pairs={{48,0},{0,16},{16,32},{32,48},{49,1},{1,17},{17,33},{33,49},{50,2}... | collective-permute-start | bytes 4128776 | tf_op jit(solution)/shard_map/ppermute | solution.py:234
  81.1 17.5 %all-to-all-start.2 = ((bf16[8,4,5376]{2,1,0:T(4,128)(2,1)}), bf16[8,4,5376]{2,1,0:T(4,128)(2,1)S(1)}, u32[]{:S(2)}, u32[]{:S(2)}) async-start(bf16[8,4,5376]{2,1,0:T(4,128)(2,1)} %broadcast_in_dim.178), calls=%async_computation.2 | async-start | bytes 688128 | tf_op jit(solution)/shard_map/all_to_all | solution.py:22
  98.6 48.4 %collective-permute-start.5 = (bf16[512,5376]{1,0:T(8,128)(2,1)}, bf16[512,5376]{1,0:T(8,128)(2,1)}, u32[]{:S(2)}, u32[]{:S(2)}) collective-permute-start(bf16[512,5376]{1,0:T(8,128)(2,1)} %refs_0_.3), channel_id=1, source_target_pairs={{0,8},{8,0},{1,9},{9,1},{2,10},{10,2},{3,11},{11,3},{4,12},{12,4},... | collective-permute-start | bytes 16515080 | tf_op jit(solution)/shard_map/ppermute | solution.py:297
  100.8 8.7 %copy-start.4 = (s32[1024]{0:T(1024)S(1)}, s32[1024]{0:T(1024)}, u32[]{:S(2)}) copy-start(s32[1024]{0:T(1024)} %param.22) | copy-start | bytes 12292
  100.8 9.2 %copy-start.9 = (f32[128]{0:T(128)S(1)}, f32[128]{0:T(128)}, u32[]{:S(2)}) copy-start(f32[128]{0:T(128)} %param.23) | copy-start | bytes 1540
  100.8 9.4 %copy-start.6 = (s32[128]{0:T(128)S(1)}, s32[128]{0:T(128)}, u32[]{:S(2)}) copy-start(s32[128]{0:T(128)} %param.21) | copy-start | bytes 1540
  100.8 46.2 %all-to-all-start.3 = ((bf16[16,16,5376]{2,1,0:T(8,128)(2,1)}), bf16[16,16,5376]{2,1,0:T(8,128)(2,1)}, u32[]{:S(2)}, u32[]{:S(2)}) async-start(bf16[16,16,5376]{2,1,0:T(8,128)(2,1)} %broadcast_select_fusion), calls=%async_computation.3 | async-start | bytes 5505024 | tf_op jit(solution)/shard_map/all_to_all | solution.py:305
  108.5 3.3 %collective-permute-start.6 = (bf16[128,5376]{1,0:T(8,128)(2,1)S(1)}, bf16[128,5376]{1,0:T(8,128)(2,1)}, u32[]{:S(2)}, u32[]{:S(2)}) collective-permute-start(bf16[128,5376]{1,0:T(8,128)(2,1)S(1)} %collective-permute-done.1.refs_2_), channel_id=1, source_target_pairs={{0,8},{8,0},{1,9},{9,1},{2,10},{10,2},{3,11},{11,3},{4,12},{12,4},... | collective-permute-start | bytes 4128776 | tf_op jit(solution)/shard_map/ppermute | solution.py:297
  108.7 7.0 %collective-permute-start.7 = (bf16[128,5376]{1,0:T(8,128)(2,1)S(1)}, bf16[128,5376]{1,0:T(8,128)(2,1)}, u32[]{:S(2)}, u32[]{:S(2)}) collective-permute-start(bf16[128,5376]{1,0:T(8,128)(2,1)S(1)} %collective-permute-done.2.refs_3_), channel_id=1, source_target_pairs={{0,8},{8,0},{1,9},{9,1},{2,10},{10,2},{3,11},{11,3},{4,12},{12,4},... | collective-permute-start | bytes 4128776 | tf_op jit(solution)/shard_map/ppermute | solution.py:297
  109.0 6.9 %collective-permute-start.8 = (bf16[128,5376]{1,0:T(8,128)(2,1)}, bf16[128,5376]{1,0:T(8,128)(2,1)}, u32[]{:S(2)}, u32[]{:S(2)}) collective-permute-start(bf16[128,5376]{1,0:T(8,128)(2,1)} %collective-permute-done.3.refs_4_), channel_id=1, source_target_pairs={{0,8},{8,0},{1,9},{9,1},{2,10},{10,2},{3,11},{11,3},{4,12},{12,4},... | collective-permute-start | bytes 4128776 | tf_op jit(solution)/shard_map/ppermute | solution.py:297
  109.2 8.7 %collective-permute-start.9 = (bf16[128,5376]{1,0:T(8,128)(2,1)}, bf16[128,5376]{1,0:T(8,128)(2,1)}, u32[]{:S(2)}, u32[]{:S(2)}) collective-permute-start(bf16[128,5376]{1,0:T(8,128)(2,1)} %collective-permute-done.4.refs_5_), channel_id=1, source_target_pairs={{0,8},{8,0},{1,9},{9,1},{2,10},{10,2},{3,11},{11,3},{4,12},{12,4},... | collective-permute-start | bytes 4128776 | tf_op jit(solution)/shard_map/ppermute | solution.py:297
  164.9 12.5 %all-to-all-start.4 = ((f32[8,3,256]{2,1,0:T(4,128)}), f32[8,3,256]{2,1,0:T(4,128)S(1)}, u32[]{:S(2)}, u32[]{:S(2)}) async-start(f32[8,3,256]{2,1,0:T(4,128)} %broadcast_in_dim.186), calls=%async_computation.4 | async-start | bytes 65536 | tf_op jit(solution)/shard_map/all_to_all | solution.py:22
  178.2 16.1 %all-to-all-start.5 = ((f32[16,3,256]{2,1,0:T(4,128)}), f32[16,3,256]{2,1,0:T(4,128)S(1)}, u32[]{:S(2)}, u32[]{:S(2)}) async-start(f32[16,3,256]{2,1,0:T(4,128)} %broadcast_in_dim.187), calls=%async_computation.5 | async-start | bytes 131072 | tf_op jit(solution)/shard_map/all_to_all | solution.py:22
  245.3 15.2 %copy-start.2 = (f32[4,5376]{1,0:T(4,128)S(1)}, f32[4,5376]{1,0:T(4,128)}, u32[]{:S(2)}) copy-start(f32[4,5376]{1,0:T(4,128)} %reduce_sum.118) | copy-start | bytes 258052
  263.4 14.7 %all-to-all-start.8 = ((bf16[8,4,5376]{2,1,0:T(4,128)(2,1)}), bf16[8,4,5376]{2,1,0:T(4,128)(2,1)S(1)}, u32[]{:S(2)}, u32[]{:S(2)}) async-start(bf16[8,4,5376]{2,1,0:T(4,128)(2,1)} %broadcast_in_dim.193), calls=%async_computation.8 | async-start | bytes 688128 | tf_op jit(solution)/shard_map/all_to_all | solution.py:22

commit v6 on v5

--- a/solution.py
+++ b/solution.py
@@ -66,55 +66,57 @@
     return starts
 
 
-def logits_kernel(rows, target_column, *refs):
-    parts, (logits, stats, held, held_rows, arrivals, rows_arrival) = refs[:-6], refs[-6:]
-    starts = placed_rows(parts)
+def logits_kernel(rows, target_column, own, across, *refs):
+    pieces, (logits, stats, near, held_rows, arrivals, rows_arrival) = refs[:-6], refs[-6:]
     rows_copy = pltpu.make_async_copy(rows, held_rows, rows_arrival)
     rows_copy.start()
     copies = [
-        pltpu.make_async_copy(part, held.at[pl.ds(start, part.shape[0])], arrivals.at[k])
-        for k, (part, start) in enumerate(zip(parts, starts))
+        pltpu.make_async_copy(piece, near.at[pl.ds(start, piece.shape[0])], arrivals.at[k])
+        for k, (piece, start) in enumerate(zip(pieces, placed_rows(pieces)))
     ]
     for copy in copies:
         copy.start()
     rows_copy.wait()
-    depth = parts[0].shape[0]
+    depth = own.shape[0]
+    half = len(pieces) // 2
     top = total = picked = None
-    for start in range(0, starts[-1], depth):
-        for copy, at in zip(copies, starts):
-            if start <= at < start + depth:
-                copy.wait()
+    for k in range(4):
+        start = k * depth
+        for copy in copies[(k - 2) * half : (k - 1) * half] if k >= 2 else ():
+            copy.wait()
+        slab = (own, across)[k] if k < 2 else near.at[pl.ds((k - 2) * depth, depth)]
         block = lax.dot_general(
-            held[pl.ds(start, depth), :], held_rows[...], NT, preferred_element_type=jnp.float32
+            held_rows[...], slab[...], NT, preferred_element_type=jnp.float32
         )
-        logits[pl.ds(start, depth), :] = block
-        hit = lax.broadcasted_iota(jnp.int32, block.shape, 0) + start == target_column[...]
-        block_picked = jnp.sum(jnp.where(hit, block, 0.0), axis=0, keepdims=True)
-        block_top = jnp.max(block, axis=0, keepdims=True)
-        new_top = block_top if start == 0 else jnp.maximum(top, block_top)
-        block_total = jnp.sum(jnp.exp(block - new_top), axis=0, keepdims=True)
-        total = block_total if start == 0 else total * jnp.exp(top - new_top) + block_total
-        picked = block_picked if start == 0 else picked + block_picked
+        logits[:, pl.ds(start, depth)] = block
+        hit = lax.broadcasted_iota(jnp.int32, block.shape, 1) + start == target_column[...]
+        block_picked = jnp.sum(jnp.where(hit, block, 0.0), axis=1, keepdims=True)
+        block_top = jnp.max(block, axis=1, keepdims=True)
+        new_top = block_top if k == 0 else jnp.maximum(top, block_top)
+        block_total = jnp.sum(jnp.exp(block - new_top), axis=1, keepdims=True)
+        total = block_total if k == 0 else total * jnp.exp(top - new_top) + block_total
+        picked = block_picked if k == 0 else picked + block_picked
         top = new_top
-    line = lax.broadcasted_iota(jnp.int32, stats.shape, 0)
-    stats[...] = jnp.where(line == 0, top, jnp.where(line == 1, total, picked))
-
-
-def gradient_kernel(logits, target_column, log_total, token_weight, *refs):
-    parts, (terms, held, held_logits, grad, arrivals, logits_arrival) = refs[:-6], refs[-6:]
-    starts = placed_rows(parts)
-    tile = held.shape[2]
+    lane = lax.broadcasted_iota(jnp.int32, stats.shape, 1)
+    stats[...] = jnp.where(lane == 0, top, jnp.where(lane == 1, total, picked))
+
+
+def gradient_kernel(logits, target_column, log_total, token_weight, own, across, *refs):
+    pieces, (terms, near, held_logits, grad, arrivals, logits_arrival) = refs[:-6], refs[-6:]
+    starts = placed_rows(pieces)
+    tile = near.shape[2]
     steps = terms.shape[1] // tile
+    depth = own.shape[0]
 
     def fetch(step):
         slot = step % 2
         copies = [
             pltpu.make_async_copy(
-                part.at[:, pl.ds(step * tile, tile)],
-                held.at[slot, pl.ds(start, part.shape[0])],
+                piece.at[:, pl.ds(step * tile, tile)],
+                near.at[slot, pl.ds(start, piece.shape[0])],
                 arrivals.at[slot, k],
             )
-            for k, (part, start) in enumerate(zip(parts, starts))
+            for k, (piece, start) in enumerate(zip(pieces, starts))
         ]
         for copy in copies:
             copy.start()
@@ -124,75 +126,82 @@
     logits_copy.start()
     coming = fetch(0)
     logits_copy.wait()
-    chunk = parts[0].shape[0] // 2
-    for start in range(0, starts[-1], chunk):
-        block = held_logits[pl.ds(start, chunk), :]
-        hit = lax.broadcasted_iota(jnp.int32, block.shape, 0) + start == target_column[...]
+    for start in range(0, 4 * depth, depth):
+        block = held_logits[:, pl.ds(start, depth)]
+        hit = lax.broadcasted_iota(jnp.int32, block.shape, 1) + start == target_column[...]
         block = jnp.where(hit, 1.0, 0.0) - jnp.exp(block - log_total[...])
-        grad[:, pl.ds(start, chunk)] = (token_weight[...] * block).T.astype(jnp.bfloat16)
+        grad[:, pl.ds(start, depth)] = (token_weight[...] * block).astype(jnp.bfloat16)
     for step in range(steps):
         following = fetch(step + 1) if step + 1 < steps else None
+        here = pl.ds(step * tile, tile)
+        mixed = jnp.dot(
+            grad[:, pl.ds(0, depth)], own[:, here], preferred_element_type=jnp.float32
+        ) + jnp.dot(
+            grad[:, pl.ds(depth, depth)], across[:, here], preferred_element_type=jnp.float32
+        )
         for copy in coming:
             copy.wait()
         coming = following
-        terms[:, pl.ds(step * tile, tile)] = jnp.dot(
-            grad[...], held[step % 2], preferred_element_type=jnp.float32
-        ).astype(jnp.bfloat16)
-
-
-def slab_logits(rows, target_column, parts):
-    width = rows.shape[1]
-    count, entries = rows.shape[0], placed_rows(parts)[-1]
-    whole = pl.BlockSpec(memory_space=pltpu.VMEM)
-    remain = pl.BlockSpec(memory_space=pltpu.HBM)
+        mixed += jnp.dot(
+            grad[:, pl.ds(2 * depth, 2 * depth)],
+            near[step % 2],
+            preferred_element_type=jnp.float32,
+        )
+        terms[:, here] = mixed.astype(jnp.bfloat16)
+
+
+WHOLE = pl.BlockSpec(memory_space=pltpu.VMEM)
+REMAIN = pl.BlockSpec(memory_space=pltpu.HBM)
+LIMIT = pltpu.CompilerParams(vmem_limit_bytes=26 * 1024 * 1024)
+
+
+def slab_cost(count, entries, width):
+    return pl.CostEstimate(
+        flops=2 * count * entries * width,
+        bytes_accessed=2 * entries * width,
+        transcendentals=count * entries,
+    )
+
+
+def slab_logits(rows, target_column, slabs, pieces):
+    (count, width), depth = rows.shape, slabs[0].shape[0]
     return pl.pallas_call(
         logits_kernel,
         out_shape=(
-            jax.ShapeDtypeStruct((entries, count), jnp.float32),
-            jax.ShapeDtypeStruct((8, count), jnp.float32),
+            jax.ShapeDtypeStruct((count, 4 * depth), jnp.float32),
+            jax.ShapeDtypeStruct((count, 128), jnp.float32),
         ),
-        in_specs=[remain, whole] + [remain] * len(parts),
-        out_specs=[whole, whole],
+        in_specs=[REMAIN] + [WHOLE] * 3 + [REMAIN] * len(pieces),
+        out_specs=[WHOLE, WHOLE],
         scratch_shapes=[
-            pltpu.VMEM((entries, width), jnp.bfloat16),
+            pltpu.VMEM((2 * depth, width), jnp.bfloat16),
             pltpu.VMEM((count, width), jnp.bfloat16),
-            pltpu.SemaphoreType.DMA((len(parts),)),
+            pltpu.SemaphoreType.DMA((len(pieces),)),
             pltpu.SemaphoreType.DMA,
         ],
-        compiler_params=pltpu.CompilerParams(vmem_limit_bytes=44 * 1024 * 1024),
-        cost_estimate=pl.CostEstimate(
-            flops=2 * count * entries * width,
-            bytes_accessed=2 * entries * width,
-            transcendentals=count * entries,
-        ),
-    )(rows, target_column, *parts)
-
-
-def slab_gradient(logits, target_column, log_total, token_weight, parts):
-    width = parts[0].shape[1]
-    entries, count = logits.shape
-    tile = next(t for t in (768, 512, 256, 128) if width % t == 0)
-    whole = pl.BlockSpec(memory_space=pltpu.VMEM)
-    remain = pl.BlockSpec(memory_space=pltpu.HBM)
+        compiler_params=LIMIT,
+        cost_estimate=slab_cost(count, 4 * depth, width),
+    )(rows, target_column, *slabs, *pieces)
+
+
+def slab_gradient(logits, target_column, log_total, token_weight, slabs, pieces):
+    (depth, width), count = slabs[0].shape, logits.shape[0]
+    tile = next(t for t in (1792, 512, 256, 128) if width % t == 0)
     return pl.pallas_call(
         gradient_kernel,
         out_shape=jax.ShapeDtypeStruct((count, width), jnp.bfloat16),
-        in_specs=[remain] + [whole] * 3 + [remain] * len(parts),
-        out_specs=whole,
+        in_specs=[REMAIN] + [WHOLE] * 5 + [REMAIN] * len(pieces),
+        out_specs=WHOLE,
         scratch_shapes=[
-            pltpu.VMEM((2, entries, tile), jnp.bfloat16),
-            pltpu.VMEM((entries, count), jnp.float32),
-            pltpu.VMEM((count, entries), jnp.bfloat16),
-            pltpu.SemaphoreType.DMA((2, len(parts))),
+            pltpu.VMEM((2, 2 * depth, tile), jnp.bfloat16),
+            pltpu.VMEM((count, 4 * depth), jnp.float32),
+            pltpu.VMEM((count, 4 * depth), jnp.bfloat16),
+            pltpu.SemaphoreType.DMA((2, len(pieces))),
             pltpu.SemaphoreType.DMA,
         ],
-        compiler_params=pltpu.CompilerParams(vmem_limit_bytes=44 * 1024 * 1024),
-        cost_estimate=pl.CostEstimate(
-            flops=2 * count * entries * width,
-            bytes_accessed=2 * entries * width,
-            transcendentals=count * entries,
-        ),
-    )(logits, target_column, log_total, token_weight, *parts)
+        compiler_params=LIMIT,
+        cost_estimate=slab_cost(count, 4 * depth, width),
+    )(logits, target_column, log_total, token_weight, *slabs, *pieces)
 
 
 def body(
@@ -295,7 +304,7 @@
     by_parity = spread(normed, Z)
     by_parity, pieces, own = lax.optimization_barrier((by_parity, pieces, embedding))
     swapped = [lax.ppermute(part, "c", SWAP) for part in (own,) + tuple(pieces)]
-    parts = (embedding, swapped[0]) + tuple(pieces) + tuple(swapped[1:])
+    slabs, near = (embedding, swapped[0]), tuple(pieces) + tuple(swapped[1:])
     by_parity = by_parity.reshape(pairs, 2, share, width).transpose(1, 0, 2, 3)
     by_parity = by_parity.reshape(2, pairs * share, width)
     rows_here = planes * pairs * share
@@ -307,11 +316,11 @@
     def of_rows(values):
         return values.reshape(planes, CS, pairs, 2, share)[:, core, :, parity].reshape(rows_here)
 
-    hit = entry[:, None] == of_rows(targets)[None, :]
-    numbers = jnp.arange(entry.shape[0], dtype=jnp.int32)[:, None]
-    target_column = jnp.max(jnp.where(hit, numbers, -1), axis=0, keepdims=True)
-    logits, stats = slab_logits(every_row, target_column, parts)
-    stats = merged(spread(stats[:3], Z))
+    hit = entry[None, :] == of_rows(targets)[:, None]
+    numbers = jnp.arange(entry.shape[0], dtype=jnp.int32)[None, :]
+    target_column = jnp.max(jnp.where(hit, numbers, -1), axis=1, keepdims=True)
+    logits, stats = slab_logits(every_row, target_column, slabs, near)
+    stats = merged(spread(stats[:, :3].T, Z))
     stats = spread(stats, ("x", "y")).reshape(XS // 2, 2, YS // 2, 2, 3, rows_here)
 
     def of_parity(odd):
@@ -327,7 +336,7 @@
     live_token = row_ids % CLEN < jnp.repeat(completion_lengths, CLEN)
     token_weight = of_rows(jnp.where(live_token, -jnp.repeat(advantages, CLEN), 0.0))
     terms = slab_gradient(
-        logits, target_column, log_total[parity][None], token_weight[None], parts
+        logits, target_column, log_total[parity][:, None], token_weight[:, None], slabs, near
     )
     arrived = lax.all_to_all(
         terms.reshape(planes, pairs * share, width), ("x", "y"), 0, 0, tiled=True

time: 280 us -> 282 us (level)
  local copies, waits for them, and re-layouts: 15.9 us -> 28.3 us
  Pallas kernels: 31.5 us -> 23.3 us
    unnamed x24 -> x44, local copies, waits for them, and re-layouts: 0.08 us -> 12.2 us
    pallas_call x1, Pallas kernels: 17.3 us -> 10.1 us  [slab_logits(): pl.pallas_call(logits_kernel, out_shape=(jax.ShapeDtypeStruct((count, 4 *...]
where the time goes in v6:
time: 282 us; the launch traced here: 281 us
  waiting for transfers between devices  113 us (40%)
  starting transfers between devices  50.7 us (18%)
  blocking collectives  49.2 us (17%)
  local copies, waits for them, and re-layouts  28.3 us (10%)
  Pallas kernels  23.3 us (8%)
  other arithmetic  10.2 us (4%)
  matrix products  5.31 us (2%)
    all_to_all x5, waiting for transfers between devices, spread(): return lax.all_to_all(copies, axes, 0, 0, tiled=True)  51.8 us
    all_to_all x1, blocking collectives, body(): lax.all_to_all(terms.reshape(planes, pairs * share, width), ('x', 'y'), 0...  35.5 us
    all_to_all x1, waiting for transfers between devices, body(): lax.all_to_all(outgoing, ('x', 'y'), 0, 0, tiled=True)  29 us
    all_to_all x5, starting transfers between devices, spread(): return lax.all_to_all(copies, axes, 0, 0, tiled=True)  28.8 us
    all_to_all x1, blocking collectives, summed(): arrived = lax.all_to_all(pieces, axes, 0, 0, tiled=True)  13.7 us
    pallas_call x1, Pallas kernels, slab_gradient(): pl.pallas_call(gradient_kernel, out_shape=jax.ShapeDtypeStruct((count, wi...  13.2 us
    ppermute x4, waiting for transfers between devices, from_neighbour(): lax.ppermute(embedding[part * quarter:(part + 1) * quarter], axes, pairs)  13.1 us
    unnamed x44, local copies, waits for them, and re-layouts  12.2 us
  transfers between devices with their start and end apart: 17, of which 16 were waited for; matrix products, arithmetic and copies ran while one was open for 5% of the time, Pallas kernels for 0%

profile of v6, /device:TPU:2, one launch (start us, length us, event | category | flops | bytes accessed | tf_op | source)
XLA Modules:
  0.0 281.2 jit_solution(8574138795150002988)
XLA Ops:
  1.5 1.6 broadcast_in_dim.173
  3.1 7.6 %all-to-all-start = ((bf16[16,128,512]{2,1,0:T(8,128)(2,1)}), bf16[16,128,512]{2,1,0:T(8,128)(2,1)S(1)}, u32[]{:S(2)}, u32[]{:S(2)}) async-start(bf16[16,128,512]{2,1,0:T(8,128)(2,1)} %broadcast_in_dim.173), calls=%async_computation | async-start | bytes 4194304 | tf_op jit(solution)/shard_map/all_to_all | solution.py:22
  11.5 26.3 %all-to-all-done = bf16[16,128,512]{2,1,0:T(8,128)(2,1)S(1)} async-done(((bf16[16,128,512]{2,1,0:T(8,128)(2,1)}), bf16[16,128,512]{2,1,0:T(8,128)(2,1)S(1)}, u32[]{:S(2)}, u32[]{:S(2)}) %all-to-all-start) | async-done | bytes 2097184 | tf_op jit(solution)/shard_map/all_to_all | solution.py:22
  40.0 1.4 collective-permute-done
  43.2 4.4 %fusion.3 = f32[8,4,5376]{2,1,0:T(4,128)} fusion(bf16[8,4,512]{2,1,0:T(4,128)(2,1)S(1)} %convert_element_type.46, bf16[512,5376]{1,0:T(8,128)(2,1)} %param.25), kind=kOutput, calls=%fused_computation.8 | convolution fusion | flops 176160768 | bytes 6225920 | tf_op jit(solution)/shard_map/dot_general | solution.py:293
  47.7 8.5 %all-to-all-start.1 = ((f32[8,4,5376]{2,1,0:T(4,128)}), f32[8,4,5376]{2,1,0:T(4,128)S(1)}, u32[]{:S(2)}, u32[]{:S(2)}) async-start(f32[8,4,5376]{2,1,0:T(4,128)} %fusion.3), calls=%async_computation.1 | async-start | bytes 1376256 | tf_op jit(solution)/shard_map/all_to_all | solution.py:28
  56.1 5.1 %fusion.68 = (bf16[128,5376]{1,0:T(8,128)(2,1)}, bf16[128,5376]{1,0:T(8,128)(2,1)}, bf16[128,5376]{1,0:T(8,128)(2,1)}, bf16[128,5376]{1,0:T(8,128)(2,1)}) fusion(bf16[512,5376]{1,0:T(8,128)(2,1)} %own.3), kind=kLoop, calls=%fused_computation.164 | loop fusion | bytes 11010048 | tf_op jit(solution)/shard_map/slice | solution.py:243
  61.2 3.3 %collective-permute-start.1 = (bf16[128,5376]{1,0:T(8,128)(2,1)}, bf16[128,5376]{1,0:T(8,128)(2,1)S(1)}, u32[]{:S(2)}, u32[]{:S(2)}) collective-permute-start(bf16[128,5376]{1,0:T(8,128)(2,1)} %get-tuple-element.31), channel_id=1, source_target_pairs={{64,0},{128,64},{192,128},{0,192},{65,1},{129,65},{193,129},{1,193... | collective-permute-start | bytes 4128776 | tf_op jit(solution)/shard_map/ppermute | solution.py:243
  64.7 1.8 collective-permute-start.4
  66.6 10.9 %all-to-all-done.1 = f32[8,4,5376]{2,1,0:T(4,128)S(1)} async-done(((f32[8,4,5376]{2,1,0:T(4,128)}), f32[8,4,5376]{2,1,0:T(4,128)S(1)}, u32[]{:S(2)}, u32[]{:S(2)}) %all-to-all-start.1) | async-done | bytes 688160 | tf_op jit(solution)/shard_map/all_to_all | solution.py:28
  81.1 3.4 %all-to-all-start.2 = ((bf16[8,4,5376]{2,1,0:T(4,128)(2,1)}), bf16[8,4,5376]{2,1,0:T(4,128)(2,1)S(1)}, u32[]{:S(2)}, u32[]{:S(2)}) async-start(bf16[8,4,5376]{2,1,0:T(4,128)(2,1)} %broadcast_in_dim.178), calls=%async_computation.2 | async-start | bytes 688128 | tf_op jit(solution)/shard_map/all_to_all | solution.py:22
  84.6 9.7 %collective-permute-done.1.refs_0_ = bf16[128,5376]{1,0:T(8,128)(2,1)S(1)} collective-permute-done((bf16[128,5376]{1,0:T(8,128)(2,1)}, bf16[128,5376]{1,0:T(8,128)(2,1)S(1)}, u32[]{:S(2)}, u32[]{:S(2)}) %collective-permute-start.1) | collective-permute-done | bytes 1376288 | tf_op jit(solution)/shard_map/ppermute | solution.py:243
  94.3 2.1 collective-permute-done.2.refs_1_
  98.8 1.8 broadcast_select_fusion
  100.7 7.0 %all-to-all-start.3 = ((bf16[16,16,5376]{2,1,0:T(8,128)(2,1)}), bf16[16,16,5376]{2,1,0:T(8,128)(2,1)S(1)}, u32[]{:S(2)}, u32[]{:S(2)}) async-start(bf16[16,16,5376]{2,1,0:T(8,128)(2,1)} %broadcast_select_fusion), calls=%async_computation.3 | async-start | bytes 5505024 | tf_op jit(solution)/shard_map/all_to_all | solution.py:314
  111.2 2.0 collective-permute-done.7.refs_5_
  113.1 2.0 collective-permute-done.8.refs_6_
  115.1 2.0 collective-permute-done.9.refs_7_
  117.1 29.0 %all-to-all-done.3 = bf16[16,16,5376]{2,1,0:T(8,128)(2,1)S(1)} async-done(((bf16[16,16,5376]{2,1,0:T(8,128)(2,1)}), bf16[16,16,5376]{2,1,0:T(8,128)(2,1)S(1)}, u32[]{:S(2)}, u32[]{:S(2)}) %all-to-all-start.3) | async-done | bytes 2752544 | tf_op jit(solution)/shard_map/all_to_all | solution.py:314
  146.1 2.6 copy-done.1
  151.3 10.1 %shard_map.149 = (f32[256,2048]{1,0:T(8,128)S(1)}, f32[256,128]{1,0:T(8,128)S(1)}) custom-call(bf16[256,5376]{1,0:T(8,128)(2,1)S(1)} %bitcast.167, s32[256,1]{1,0:T(8,128)S(1)} %copy.141.target_column, bf16[512,5376]{1,0:T(8,128)(2,1)S(1)} %copy-done.1, bf16[512,5376]{1,0:T(8,128)(2,1)} %collective-permute-done.5.across, bf16[128,5376]{1,0:T(8,128)(2,1)S(1)} %copy-done.4, ...), custom_call_target="tpu_custom_call" | custom-call | flops 5637144576 | bytes 22020096 | tf_op jit(solution)/shard_map/pallas_call | solution.py:168
  163.6 4.5 %all-to-all-start.4 = ((f32[8,3,256]{2,1,0:T(4,128)}), f32[8,3,256]{2,1,0:T(4,128)S(1)}, u32[]{:S(2)}, u32[]{:S(2)}) async-start(f32[8,3,256]{2,1,0:T(4,128)} %broadcast_in_dim.186), calls=%async_computation.4 | async-start | bytes 65536 | tf_op jit(solution)/shard_map/all_to_all | solution.py:22
  168.0 8.0 %all-to-all-done.4 = f32[8,3,256]{2,1,0:T(4,128)S(1)} async-done(((f32[8,3,256]{2,1,0:T(4,128)}), f32[8,3,256]{2,1,0:T(4,128)S(1)}, u32[]{:S(2)}, u32[]{:S(2)}) %all-to-all-start.4) | async-done | bytes 24608 | tf_op jit(solution)/shard_map/all_to_all | solution.py:22
  176.8 9.8 %all-to-all-start.5 = ((f32[16,3,256]{2,1,0:T(4,128)}), f32[16,3,256]{2,1,0:T(4,128)S(1)}, u32[]{:S(2)}, u32[]{:S(2)}) async-start(f32[16,3,256]{2,1,0:T(4,128)} %broadcast_in_dim.187), calls=%async_computation.5 | async-start | bytes 131072 | tf_op jit(solution)/shard_map/all_to_all | solution.py:22
  186.8 6.1 %all-to-all-done.5 = f32[16,3,256]{2,1,0:T(4,128)S(1)} async-done(((f32[16,3,256]{2,1,0:T(4,128)}), f32[16,3,256]{2,1,0:T(4,128)S(1)}, u32[]{:S(2)}, u32[]{:S(2)}) %all-to-all-start.5) | async-done | bytes 49184 | tf_op jit(solution)/shard_map/all_to_all | solution.py:22
  193.4 2.6 copy-done.2
  197.3 1.6 copy-done.10
  198.9 13.2 %shard_map.150 = bf16[256,5376]{1,0:T(8,128)(2,1)S(1)} custom-call(f32[256,2048]{1,0:T(8,128)S(1)} %copy-done.10, s32[256,1]{1,0:T(8,128)S(1)} %copy.141.target_column, f32[256,1]{1,0:T(8,128)S(1)} %copy.154.log_total, f32[256,1]{1,0:T(8,128)S(1)} %broadcast_in_dim_reshape_squeeze.5.token_weight, bf16[512,5376]{1,0:T(8,128)(2,1)S(1)} %copy-done.2, ...), custom_call_target="tpu_custom_call" | custom-call | flops 5637144576 | bytes 22020096 | tf_op jit(solution)/shard_map/pallas_call | solution.py:190
  212.1 35.5 %all_to_all.45 = bf16[16,16,5376]{2,1,0:T(8,128)(2,1)S(1)} all-to-all(bf16[16,16,5376]{2,1,0:T(8,128)(2,1)S(1)} %bitcast.168), channel_id=1, replica_groups=mesh['x'=4,'y'=4,'c'=2,'zh'=4,'zl'=2] {'x','y'}, dimensions={0} | all-to-all | bytes 5505024 | tf_op jit(solution)/shard_map/all_to_all | solution.py:341
  248.8 13.7 %all_to_all.46 = bf16[8,4,5376]{2,1,0:T(4,128)(2,1)S(1)} all-to-all(bf16[8,4,5376]{2,1,0:T(4,128)(2,1)S(1)} %bitcast.170), channel_id=1, replica_groups=mesh['x'=4,'y'=4,'c'=2,'zh'=4,'zl'=2] {'zh','zl'}, dimensions={0} | all-to-all | bytes 688128 | tf_op jit(solution)/shard_map/all_to_all | solution.py:28
  265.6 3.4 %all-to-all-start.8 = ((bf16[8,4,5376]{2,1,0:T(4,128)(2,1)}), bf16[8,4,5376]{2,1,0:T(4,128)(2,1)S(1)}, u32[]{:S(2)}, u32[]{:S(2)}) async-start(bf16[8,4,5376]{2,1,0:T(4,128)(2,1)} %broadcast_in_dim.193), calls=%async_computation.8 | async-start | bytes 688128 | tf_op jit(solution)/shard_map/all_to_all | solution.py:22
  269.8 10.5 %all-to-all-done.8 = bf16[8,4,5376]{2,1,0:T(4,128)(2,1)S(1)} async-done(((bf16[8,4,5376]{2,1,0:T(4,128)(2,1)}), bf16[8,4,5376]{2,1,0:T(4,128)(2,1)S(1)}, u32[]{:S(2)}, u32[]{:S(2)}) %all-to-all-start.8) | async-done | bytes 344096 | tf_op jit(solution)/shard_map/all_to_all | solution.py:22
  (144 shorter events, 28.6 us)
Async XLA Ops:
  0.6 41.6 %copy-start = (bf16[32,512]{1,0:T(8,128)(2,1)S(1)}, bf16[32,512]{1,0:T(8,128)(2,1)}, u32[]{:S(2)}) copy-start(bf16[32,512]{1,0:T(8,128)(2,1)} %param.14) | copy-start | bytes 98308
  3.1 7.6 %copy-start.15 = (s32[128]{0:T(128)S(1)}, s32[128]{0:T(128)}, u32[]{:S(2)}) copy-start(s32[128]{0:T(128)} %param.20) | copy-start | bytes 1540
  3.1 7.8 %copy-start.11 = (s32[32]{0:T(128)S(1)}, s32[32]{0:T(128)}, u32[]{:S(2)}) copy-start(s32[32]{0:T(128)} %param.19) | copy-start | bytes 388
  3.1 34.8 %all-to-all-start = ((bf16[16,128,512]{2,1,0:T(8,128)(2,1)}), bf16[16,128,512]{2,1,0:T(8,128)(2,1)S(1)}, u32[]{:S(2)}, u32[]{:S(2)}) async-start(bf16[16,128,512]{2,1,0:T(8,128)(2,1)} %broadcast_in_dim.173), calls=%async_computation | async-start | bytes 4194304 | tf_op jit(solution)/shard_map/all_to_all | solution.py:22
  39.2 2.1 collective-permute-start
  40.0 2.3 copy-start.18
  47.7 29.8 %all-to-all-start.1 = ((f32[8,4,5376]{2,1,0:T(4,128)}), f32[8,4,5376]{2,1,0:T(4,128)S(1)}, u32[]{:S(2)}, u32[]{:S(2)}) async-start(f32[8,4,5376]{2,1,0:T(4,128)} %fusion.3), calls=%async_computation.1 | async-start | bytes 1376256 | tf_op jit(solution)/shard_map/all_to_all | solution.py:28
  56.1 23.2 %copy-start.13 = (f32[5376]{0:T(1024)S(1)}, f32[5376]{0:T(1024)}, u32[]{:S(2)}) copy-start(f32[5376]{0:T(1024)} %param.26) | copy-start | bytes 64516
  61.2 33.1 %collective-permute-start.1 = (bf16[128,5376]{1,0:T(8,128)(2,1)}, bf16[128,5376]{1,0:T(8,128)(2,1)S(1)}, u32[]{:S(2)}, u32[]{:S(2)}) collective-permute-start(bf16[128,5376]{1,0:T(8,128)(2,1)} %get-tuple-element.31), channel_id=1, source_target_pairs={{64,0},{128,64},{192,128},{0,192},{65,1},{129,65},{193,129},{1,193... | collective-permute-start | bytes 4128776 | tf_op jit(solution)/shard_map/ppermute | solution.py:243
  64.5 31.9 %collective-permute-start.2 = (bf16[128,5376]{1,0:T(8,128)(2,1)}, bf16[128,5376]{1,0:T(8,128)(2,1)S(1)}, u32[]{:S(2)}, u32[]{:S(2)}) collective-permute-start(bf16[128,5376]{1,0:T(8,128)(2,1)} %get-tuple-element.30), channel_id=1, source_target_pairs={{192,0},{0,64},{64,128},{128,192},{193,1},{1,65},{65,129},{129,193... | collective-permute-start | bytes 4128776 | tf_op jit(solution)/shard_map/ppermute | solution.py:243
  64.5 32.0 %collective-permute-start.3 = (bf16[128,5376]{1,0:T(8,128)(2,1)}, bf16[128,5376]{1,0:T(8,128)(2,1)}, u32[]{:S(2)}, u32[]{:S(2)}) collective-permute-start(bf16[128,5376]{1,0:T(8,128)(2,1)} %get-tuple-element.29), channel_id=1, source_target_pairs={{16,0},{32,16},{48,32},{0,48},{17,1},{33,17},{49,33},{1,49},{18,2}... | collective-permute-start | bytes 4128776 | tf_op jit(solution)/shard_map/ppermute | solution.py:243
  64.7 33.0 %collective-permute-start.4 = (bf16[128,5376]{1,0:T(8,128)(2,1)}, bf16[128,5376]{1,0:T(8,128)(2,1)}, u32[]{:S(2)}, u32[]{:S(2)}) collective-permute-start(bf16[128,5376]{1,0:T(8,128)(2,1)} %get-tuple-element.28), channel_id=1, source_target_pairs={{48,0},{0,16},{16,32},{32,48},{49,1},{1,17},{17,33},{33,49},{50,2}... | collective-permute-start | bytes 4128776 | tf_op jit(solution)/shard_map/ppermute | solution.py:243
  81.1 17.5 %all-to-all-start.2 = ((bf16[8,4,5376]{2,1,0:T(4,128)(2,1)}), bf16[8,4,5376]{2,1,0:T(4,128)(2,1)S(1)}, u32[]{:S(2)}, u32[]{:S(2)}) async-start(bf16[8,4,5376]{2,1,0:T(4,128)(2,1)} %broadcast_in_dim.178), calls=%async_computation.2 | async-start | bytes 688128 | tf_op jit(solution)/shard_map/all_to_all | solution.py:22
  94.3 6.4 %copy-start.3 = (bf16[128,5376]{1,0:T(8,128)(2,1)}, bf16[128,5376]{1,0:T(8,128)(2,1)S(1)}, u32[]{:S(2)}) copy-start(bf16[128,5376]{1,0:T(8,128)(2,1)S(1)} %collective-permute-done.1.refs_0_) | copy-start | bytes 4128772
  96.4 4.3 %copy-start.6 = (bf16[128,5376]{1,0:T(8,128)(2,1)}, bf16[128,5376]{1,0:T(8,128)(2,1)S(1)}, u32[]{:S(2)}) copy-start(bf16[128,5376]{1,0:T(8,128)(2,1)S(1)} %collective-permute-done.2.refs_1_) | copy-start | bytes 4128772
  98.6 47.5 %collective-permute-start.5 = (bf16[512,5376]{1,0:T(8,128)(2,1)}, bf16[512,5376]{1,0:T(8,128)(2,1)}, u32[]{:S(2)}, u32[]{:S(2)}) collective-permute-start(bf16[512,5376]{1,0:T(8,128)(2,1)} %own.3), channel_id=1, source_target_pairs={{0,8},{8,0},{1,9},{9,1},{2,10},{10,2},{3,11},{11,3},{4,12},{12,4},... | collective-permute-start | bytes 16515080 | tf_op jit(solution)/shard_map/ppermute | solution.py:306
  100.7 8.1 %copy-start.14 = (s32[1024]{0:T(1024)S(1)}, s32[1024]{0:T(1024)}, u32[]{:S(2)}) copy-start(s32[1024]{0:T(1024)} %param.22) | copy-start | bytes 12292
  100.7 9.2 %copy-start.19 = (f32[128]{0:T(128)S(1)}, f32[128]{0:T(128)}, u32[]{:S(2)}) copy-start(f32[128]{0:T(128)} %param.23) | copy-start | bytes 1540
  100.7 9.3 %copy-start.16 = (s32[128]{0:T(128)S(1)}, s32[128]{0:T(128)}, u32[]{:S(2)}) copy-start(s32[128]{0:T(128)} %param.21) | copy-start | bytes 1540
  100.7 45.4 %all-to-all-start.3 = ((bf16[16,16,5376]{2,1,0:T(8,128)(2,1)}), bf16[16,16,5376]{2,1,0:T(8,128)(2,1)S(1)}, u32[]{:S(2)}, u32[]{:S(2)}) async-start(bf16[16,16,5376]{2,1,0:T(8,128)(2,1)} %broadcast_select_fusion), calls=%async_computation.3 | async-start | bytes 5505024 | tf_op jit(solution)/shard_map/all_to_all | solution.py:314
  107.7 3.5 %collective-permute-start.6 = (bf16[128,5376]{1,0:T(8,128)(2,1)}, bf16[128,5376]{1,0:T(8,128)(2,1)}, u32[]{:S(2)}, u32[]{:S(2)}) collective-permute-start(bf16[128,5376]{1,0:T(8,128)(2,1)} %copy-done.3), channel_id=1, source_target_pairs={{0,8},{8,0},{1,9},{9,1},{2,10},{10,2},{3,11},{11,3},{4,12},{12,4},... | collective-permute-start | bytes 4128776 | tf_op jit(solution)/shard_map/ppermute | solution.py:306
  107.9 5.2 %collective-permute-start.7 = (bf16[128,5376]{1,0:T(8,128)(2,1)}, bf16[128,5376]{1,0:T(8,128)(2,1)}, u32[]{:S(2)}, u32[]{:S(2)}) collective-permute-start(bf16[128,5376]{1,0:T(8,128)(2,1)} %copy-done.6), channel_id=1, source_target_pairs={{0,8},{8,0},{1,9},{9,1},{2,10},{10,2},{3,11},{11,3},{4,12},{12,4},... | collective-permute-start | bytes 4128776 | tf_op jit(solution)/shard_map/ppermute | solution.py:306
  108.2 6.9 %collective-permute-start.8 = (bf16[128,5376]{1,0:T(8,128)(2,1)}, bf16[128,5376]{1,0:T(8,128)(2,1)}, u32[]{:S(2)}, u32[]{:S(2)}) collective-permute-start(bf16[128,5376]{1,0:T(8,128)(2,1)} %collective-permute-done.3.refs_2_), channel_id=1, source_target_pairs={{0,8},{8,0},{1,9},{9,1},{2,10},{10,2},{3,11},{11,3},{4,12},{12,4},... | collective-permute-start | bytes 4128776 | tf_op jit(solution)/shard_map/ppermute | solution.py:306
  108.4 8.7 %collective-permute-start.9 = (bf16[128,5376]{1,0:T(8,128)(2,1)}, bf16[128,5376]{1,0:T(8,128)(2,1)}, u32[]{:S(2)}, u32[]{:S(2)}) collective-permute-start(bf16[128,5376]{1,0:T(8,128)(2,1)} %collective-permute-done.4.refs_3_), channel_id=1, source_target_pairs={{0,8},{8,0},{1,9},{9,1},{2,10},{10,2},{3,11},{11,3},{4,12},{12,4},... | collective-permute-start | bytes 4128776 | tf_op jit(solution)/shard_map/ppermute | solution.py:306
  146.1 2.6 copy-start.1
  162.8 30.5 %copy-start.5 = (bf16[128,5376]{1,0:T(8,128)(2,1)S(1)}, bf16[128,5376]{1,0:T(8,128)(2,1)}, u32[]{:S(2)}) copy-start(bf16[128,5376]{1,0:T(8,128)(2,1)} %copy-done.3) | copy-start | bytes 4128772
  163.6 12.5 %all-to-all-start.4 = ((f32[8,3,256]{2,1,0:T(4,128)}), f32[8,3,256]{2,1,0:T(4,128)S(1)}, u32[]{:S(2)}, u32[]{:S(2)}) async-start(f32[8,3,256]{2,1,0:T(4,128)} %broadcast_in_dim.186), calls=%async_computation.4 | async-start | bytes 65536 | tf_op jit(solution)/shard_map/all_to_all | solution.py:22
  176.8 16.1 %all-to-all-start.5 = ((f32[16,3,256]{2,1,0:T(4,128)}), f32[16,3,256]{2,1,0:T(4,128)S(1)}, u32[]{:S(2)}, u32[]{:S(2)}) async-start(f32[16,3,256]{2,1,0:T(4,128)} %broadcast_in_dim.187), calls=%async_computation.5 | async-start | bytes 131072 | tf_op jit(solution)/shard_map/all_to_all | solution.py:22
  193.4 2.6 copy-start.2
  197.3 1.6 copy-start.10
  247.5 15.2 %copy-start.12 = (f32[4,5376]{1,0:T(4,128)S(1)}, f32[4,5376]{1,0:T(4,128)}, u32[]{:S(2)}) copy-start(f32[4,5376]{1,0:T(4,128)} %reduce_sum.118) | copy-start | bytes 258052
  265.6 14.7 %all-to-all-start.8 = ((bf16[8,4,5376]{2,1,0:T(4,128)(2,1)}), bf16[8,4,5376]{2,1,0:T(4,128)(2,1)S(1)}, u32[]{:S(2)}, u32[]{:S(2)}) async-start(bf16[8,4,5376]{2,1,0:T(4,128)(2,1)} %broadcast_in_dim.193), calls=%async_computation.8 | async-start | bytes 688128 | tf_op jit(solution)/shard_map/all_to_all | solution.py:22
  (5 other events, 6.6 us)

commit v7 on v5

--- a/solution.py
+++ b/solution.py
@@ -85,19 +85,19 @@
             if start <= at < start + depth:
                 copy.wait()
         block = lax.dot_general(
-            held[pl.ds(start, depth), :], held_rows[...], NT, preferred_element_type=jnp.float32
+            held_rows[...], held[pl.ds(start, depth), :], NT, preferred_element_type=jnp.float32
         )
-        logits[pl.ds(start, depth), :] = block
-        hit = lax.broadcasted_iota(jnp.int32, block.shape, 0) + start == target_column[...]
-        block_picked = jnp.sum(jnp.where(hit, block, 0.0), axis=0, keepdims=True)
-        block_top = jnp.max(block, axis=0, keepdims=True)
+        logits[:, pl.ds(start, depth)] = block
+        hit = lax.broadcasted_iota(jnp.int32, block.shape, 1) + start == target_column[...]
+        block_picked = jnp.sum(jnp.where(hit, block, 0.0), axis=1, keepdims=True)
+        block_top = jnp.max(block, axis=1, keepdims=True)
         new_top = block_top if start == 0 else jnp.maximum(top, block_top)
-        block_total = jnp.sum(jnp.exp(block - new_top), axis=0, keepdims=True)
+        block_total = jnp.sum(jnp.exp(block - new_top), axis=1, keepdims=True)
         total = block_total if start == 0 else total * jnp.exp(top - new_top) + block_total
         picked = block_picked if start == 0 else picked + block_picked
         top = new_top
-    line = lax.broadcasted_iota(jnp.int32, stats.shape, 0)
-    stats[...] = jnp.where(line == 0, top, jnp.where(line == 1, total, picked))
+    lane = lax.broadcasted_iota(jnp.int32, stats.shape, 1)
+    stats[...] = jnp.where(lane == 0, top, jnp.where(lane == 1, total, picked))
 
 
 def gradient_kernel(logits, target_column, log_total, token_weight, *refs):
@@ -124,12 +124,12 @@
     logits_copy.start()
     coming = fetch(0)
     logits_copy.wait()
-    chunk = parts[0].shape[0] // 2
-    for start in range(0, starts[-1], chunk):
-        block = held_logits[pl.ds(start, chunk), :]
-        hit = lax.broadcasted_iota(jnp.int32, block.shape, 0) + start == target_column[...]
+    depth = parts[0].shape[0]
+    for start in range(0, starts[-1], depth):
+        block = held_logits[:, pl.ds(start, depth)]
+        hit = lax.broadcasted_iota(jnp.int32, block.shape, 1) + start == target_column[...]
         block = jnp.where(hit, 1.0, 0.0) - jnp.exp(block - log_total[...])
-        grad[:, pl.ds(start, chunk)] = (token_weight[...] * block).T.astype(jnp.bfloat16)
+        grad[:, pl.ds(start, depth)] = (token_weight[...] * block).astype(jnp.bfloat16)
     for step in range(steps):
         following = fetch(step + 1) if step + 1 < steps else None
         for copy in coming:
@@ -148,8 +148,8 @@
     return pl.pallas_call(
         logits_kernel,
         out_shape=(
-            jax.ShapeDtypeStruct((entries, count), jnp.float32),
-            jax.ShapeDtypeStruct((8, count), jnp.float32),
+            jax.ShapeDtypeStruct((count, entries), jnp.float32),
+            jax.ShapeDtypeStruct((count, 128), jnp.float32),
         ),
         in_specs=[remain, whole] + [remain] * len(parts),
         out_specs=[whole, whole],
@@ -159,7 +159,7 @@
             pltpu.SemaphoreType.DMA((len(parts),)),
             pltpu.SemaphoreType.DMA,
         ],
-        compiler_params=pltpu.CompilerParams(vmem_limit_bytes=44 * 1024 * 1024),
+        compiler_params=pltpu.CompilerParams(vmem_limit_bytes=48 * 1024 * 1024),
         cost_estimate=pl.CostEstimate(
             flops=2 * count * entries * width,
             bytes_accessed=2 * entries * width,
@@ -170,8 +170,8 @@
 
 def slab_gradient(logits, target_column, log_total, token_weight, parts):
     width = parts[0].shape[1]
-    entries, count = logits.shape
-    tile = next(t for t in (768, 512, 256, 128) if width % t == 0)
+    count, entries = logits.shape
+    tile = next(t for t in (1792, 512, 256, 128) if width % t == 0)
     whole = pl.BlockSpec(memory_space=pltpu.VMEM)
     remain = pl.BlockSpec(memory_space=pltpu.HBM)
     return pl.pallas_call(
@@ -181,12 +181,12 @@
         out_specs=whole,
         scratch_shapes=[
             pltpu.VMEM((2, entries, tile), jnp.bfloat16),
-            pltpu.VMEM((entries, count), jnp.float32),
+            pltpu.VMEM((count, entries), jnp.float32),
             pltpu.VMEM((count, entries), jnp.bfloat16),
             pltpu.SemaphoreType.DMA((2, len(parts))),
             pltpu.SemaphoreType.DMA,
         ],
-        compiler_params=pltpu.CompilerParams(vmem_limit_bytes=44 * 1024 * 1024),
+        compiler_params=pltpu.CompilerParams(vmem_limit_bytes=48 * 1024 * 1024),
         cost_estimate=pl.CostEstimate(
             flops=2 * count * entries * width,
             bytes_accessed=2 * entries * width,
@@ -211,6 +211,26 @@
     norm_gain,
     embedding,
 ):
+    held = jnp.concatenate([prompt_keys[0], prompt_values[0]], axis=1)
+    arrived, rest = lax.optimization_barrier(
+        (
+            spread(held, ("x", "y")),
+            (
+                queries,
+                own_keys,
+                own_values,
+                prompt_lengths,
+                completion_prompt,
+                completion_lengths,
+                targets,
+                advantages,
+                residual,
+                embedding,
+            ),
+        )
+    )
+    queries, own_keys, own_values, prompt_lengths, completion_prompt = rest[:5]
+    completion_lengths, targets, advantages, residual, embedding = rest[5:]
     row_count, width = residual.shape
     comp_count = row_count // CLEN
     heads_here = queries.shape[1] // HDIM
@@ -252,8 +272,6 @@
         ]
     )
 
-    held = jnp.concatenate([prompt_keys[0], prompt_values[0]], axis=1)
-    arrived = spread(held, ("x", "y"))
     by_device = completion_prompt.reshape(planes * CS, comp_count)
     my_prompts = by_device[dp_index]
     partner_prompts = by_device[plane * CS + (1 - core)]
@@ -307,12 +325,22 @@
     def of_rows(values):
         return values.reshape(planes, CS, pairs, 2, share)[:, core, :, parity].reshape(rows_here)
 
-    hit = entry[:, None] == of_rows(targets)[None, :]
-    numbers = jnp.arange(entry.shape[0], dtype=jnp.int32)[:, None]
-    target_column = jnp.max(jnp.where(hit, numbers, -1), axis=0, keepdims=True)
+    hit = entry[None, :] == of_rows(targets)[:, None]
+    numbers = jnp.arange(entry.shape[0], dtype=jnp.int32)[None, :]
+    target_column = jnp.max(jnp.where(hit, numbers, -1), axis=1, keepdims=True)
+    row_ids = jnp.arange(targets.shape[0], dtype=jnp.int32)
+    live_token = row_ids % CLEN < jnp.repeat(completion_lengths, CLEN)
+    token_weight = of_rows(jnp.where(live_token, -jnp.repeat(advantages, CLEN), 0.0))[:, None]
     logits, stats = slab_logits(every_row, target_column, parts)
-    stats = merged(spread(stats[:3], Z))
-    stats = spread(stats, ("x", "y")).reshape(XS // 2, 2, YS // 2, 2, 3, rows_here)
+
+    stats, later = lax.optimization_barrier(
+        (stats[:, :3].T, (logits, target_column, token_weight, hidden, norm_factor, norm_gain))
+    )
+    stats, later = lax.optimization_barrier((spread(stats, Z), later))
+    stats, later = lax.optimization_barrier((merged(stats), later))
+    stats, later = lax.optimization_barrier((spread(stats, ("x", "y")), later))
+    logits, target_column, token_weight, hidden, norm_factor, norm_gain = later
+    stats = stats.reshape(XS // 2, 2, YS // 2, 2, 3, rows_here)
 
     def of_parity(odd):
         picks = [stats[:, at_x, :, (at_x + odd) % 2] for at_x in range(2)]
@@ -323,11 +351,8 @@
     every_logprob = (stats[:, 2] - log_total).reshape(2, planes, pairs, share)
     logprob = every_logprob[:, plane].transpose(1, 0, 2).reshape(row_count)
 
-    row_ids = jnp.arange(targets.shape[0], dtype=jnp.int32)
-    live_token = row_ids % CLEN < jnp.repeat(completion_lengths, CLEN)
-    token_weight = of_rows(jnp.where(live_token, -jnp.repeat(advantages, CLEN), 0.0))
     terms = slab_gradient(
-        logits, target_column, log_total[parity][None], token_weight[None], parts
+        logits, target_column, log_total[parity][:, None], token_weight, parts
     )
     arrived = lax.all_to_all(
         terms.reshape(planes, pairs * share, width), ("x", "y"), 0, 0, tiled=True
@@ -344,7 +369,8 @@
     hidden_grad = norm_gain * norm_factor * normed_grad - hidden * norm_factor**3 * jnp.mean(
         norm_gain * normed_grad * hidden, axis=-1, keepdims=True
     )
-    hidden_grad = spread(hidden_grad.astype(jnp.bfloat16), Z).reshape(row_count, width)
+    hidden_grad, logprob = lax.optimization_barrier((hidden_grad.astype(jnp.bfloat16), logprob))
+    hidden_grad = spread(hidden_grad, Z).reshape(row_count, width)
     return (logprob, hidden_grad.astype(jnp.float32))
 
 

time: 280 us -> 274 us (0.979)
  blocking collectives: 50.2 us -> 80.5 us
  waiting for transfers between devices: 113 us -> 98.2 us
  starting transfers between devices: 51.3 us -> 37.8 us
  Pallas kernels: 31.5 us -> 26.1 us
    all_to_all x1 -> x3, blocking collectives: 13.7 us -> 44 us  [spread(): return lax.all_to_all(copies, axes, 0, 0, tiled=True)]
    all_to_all x5 -> x2, waiting for transfers between devices: 51.8 us -> 27.1 us  [spread(): return lax.all_to_all(copies, axes, 0, 0, tiled=True)]
    all_to_all x5 -> x2, starting transfers between devices: 28.8 us -> 11 us  [spread(): return lax.all_to_all(copies, axes, 0, 0, tiled=True)]
    all_to_all x1 -> x2, waiting for transfers between devices: 10.9 us -> 20.2 us  [summed(): arrived = lax.all_to_all(pieces, axes, 0, 0, tiled=True)]
    pallas_call x1, Pallas kernels: 17.3 us -> 13.8 us  [slab_logits(): pl.pallas_call(logits_kernel, out_shape=(jax.ShapeDtypeStruct((count, ent...]
    all_to_all x1 -> x2, starting transfers between devices: 8.47 us -> 11.9 us  [summed(): arrived = lax.all_to_all(pieces, axes, 0, 0, tiled=True)]
  transfers between devices with their start and end apart: 17 -> 15, of which waited for: 16 -> 11; matrix products, arithmetic and copies ran while one was open for 5% -> 6% of each run, Pallas kernels for 0% -> 0%
where the time goes in v7:
time: 274 us
  waiting for transfers between devices  98.2 us (36%)
  blocking collectives  80.5 us (29%)
  starting transfers between devices  37.8 us (14%)
  Pallas kernels  26.1 us (10%)
  local copies, waits for them, and re-layouts  16.2 us (6%)
  other arithmetic  8.29 us (3%)
  matrix products  5.31 us (2%)
    all_to_all x3, blocking collectives, spread(): return lax.all_to_all(copies, axes, 0, 0, tiled=True)  44 us
    all_to_all x1, blocking collectives, body(): lax.all_to_all(terms.reshape(planes, pairs * share, width), ('x', 'y'), 0...  36.5 us
    all_to_all x1, waiting for transfers between devices, body(): lax.all_to_all(outgoing, ('x', 'y'), 0, 0, tiled=True)  29.3 us
    all_to_all x2, waiting for transfers between devices, spread(): return lax.all_to_all(copies, axes, 0, 0, tiled=True)  27.1 us
    all_to_all x2, waiting for transfers between devices, summed(): arrived = lax.all_to_all(pieces, axes, 0, 0, tiled=True)  20.2 us
    ppermute x4, waiting for transfers between devices, from_neighbour(): lax.ppermute(embedding[part * quarter:(part + 1) * quarter], axes, pairs)  14.5 us
    pallas_call x1, Pallas kernels, slab_logits(): pl.pallas_call(logits_kernel, out_shape=(jax.ShapeDtypeStruct((count, ent...  13.8 us
    pallas_call x1, Pallas kernels, slab_gradient(): pl.pallas_call(gradient_kernel, out_shape=jax.ShapeDtypeStruct((count, wi...  12.3 us
  transfers between devices with their start and end apart: 15, of which 11 were waited for; matrix products, arithmetic and copies ran while one was open for 6% of the time, Pallas kernels for 0%

profile of v7, /device:TPU:2, one launch (start us, length us, event | category | flops | bytes accessed | tf_op | source)
XLA Modules:
  0.0 273.6 jit_solution(10859034642640989046)
XLA Ops:
  1.5 1.6 broadcast_in_dim.172
  3.1 7.6 %all-to-all-start = ((bf16[16,128,512]{2,1,0:T(8,128)(2,1)}), bf16[16,128,512]{2,1,0:T(8,128)(2,1)S(1)}, u32[]{:S(2)}, u32[]{:S(2)}) async-start(bf16[16,128,512]{2,1,0:T(8,128)(2,1)} %broadcast_in_dim.172), calls=%async_computation | async-start | bytes 4194304 | tf_op jit(solution)/shard_map/all_to_all | solution.py:22
  10.7 27.1 %all-to-all-done = bf16[16,128,512]{2,1,0:T(8,128)(2,1)S(1)} async-done(((bf16[16,128,512]{2,1,0:T(8,128)(2,1)}), bf16[16,128,512]{2,1,0:T(8,128)(2,1)S(1)}, u32[]{:S(2)}, u32[]{:S(2)}) %all-to-all-start) | async-done | bytes 2097184 | tf_op jit(solution)/shard_map/all_to_all | solution.py:22
  38.0 1.4 gather_fusion.1
  43.4 4.4 %fusion.3 = f32[8,4,5376]{2,1,0:T(4,128)} fusion(bf16[8,4,512]{2,1,0:T(4,128)(2,1)S(1)} %convert_element_type.46, bf16[512,5376]{1,0:T(8,128)(2,1)} %param.25), kind=kOutput, calls=%fused_computation.8 | convolution fusion | flops 176160768 | bytes 6225920 | tf_op jit(solution)/shard_map/dot_general | solution.py:302
  47.8 8.5 %all-to-all-start.1 = ((f32[8,4,5376]{2,1,0:T(4,128)}), f32[8,4,5376]{2,1,0:T(4,128)S(1)}, u32[]{:S(2)}, u32[]{:S(2)}) async-start(f32[8,4,5376]{2,1,0:T(4,128)} %fusion.3), calls=%async_computation.1 | async-start | bytes 1376256 | tf_op jit(solution)/shard_map/all_to_all | solution.py:28
  56.3 5.1 %fusion.69 = (bf16[128,5376]{1,0:T(8,128)(2,1)}, bf16[128,5376]{1,0:T(8,128)(2,1)}, bf16[128,5376]{1,0:T(8,128)(2,1)}, bf16[128,5376]{1,0:T(8,128)(2,1)}) fusion(bf16[512,5376]{1,0:T(8,128)(2,1)} %refs_0_.1), kind=kLoop, calls=%fused_computation.169 | loop fusion | bytes 11010048 | tf_op jit(solution)/shard_map/slice | solution.py:254
  61.9 2.7 collective-permute-start.3
  64.6 2.3 collective-permute-start.2
  66.9 1.1 collective-permute-start.1
  67.9 9.7 %all-to-all-done.1 = f32[8,4,5376]{2,1,0:T(4,128)S(1)} async-done(((f32[8,4,5376]{2,1,0:T(4,128)}), f32[8,4,5376]{2,1,0:T(4,128)S(1)}, u32[]{:S(2)}, u32[]{:S(2)}) %all-to-all-start.1) | async-done | bytes 688160 | tf_op jit(solution)/shard_map/all_to_all | solution.py:28
  78.3 1.1 multiply_reduce_fusion.1
  80.4 3.4 %all-to-all-start.2 = ((bf16[8,4,5376]{2,1,0:T(4,128)(2,1)}), bf16[8,4,5376]{2,1,0:T(4,128)(2,1)S(1)}, u32[]{:S(2)}, u32[]{:S(2)}) async-start(bf16[8,4,5376]{2,1,0:T(4,128)(2,1)} %broadcast_in_dim.178), calls=%async_computation.2 | async-start | bytes 688128 | tf_op jit(solution)/shard_map/all_to_all | solution.py:22
  83.8 10.9 %collective-permute-done.4.refs_5_ = bf16[128,5376]{1,0:T(8,128)(2,1)S(1)} collective-permute-done((bf16[128,5376]{1,0:T(8,128)(2,1)}, bf16[128,5376]{1,0:T(8,128)(2,1)S(1)}, u32[]{:S(2)}, u32[]{:S(2)}) %collective-permute-start.4) | collective-permute-done | bytes 1376288 | tf_op jit(solution)/shard_map/ppermute | solution.py:254
  94.7 3.1 %collective-permute-done.2.refs_3_ = bf16[128,5376]{1,0:T(8,128)(2,1)} collective-permute-done((bf16[128,5376]{1,0:T(8,128)(2,1)}, bf16[128,5376]{1,0:T(8,128)(2,1)}, u32[]{:S(2)}, u32[]{:S(2)}) %collective-permute-start.2) | collective-permute-done | bytes 1376288 | tf_op jit(solution)/shard_map/ppermute | solution.py:254
  99.1 1.0 broadcast_in_dim.179
  100.1 1.9 broadcast_select_fusion
  102.0 7.2 %all-to-all-start.3 = ((bf16[16,16,5376]{2,1,0:T(8,128)(2,1)}), bf16[16,16,5376]{2,1,0:T(8,128)(2,1)}, u32[]{:S(2)}, u32[]{:S(2)}) async-start(bf16[16,16,5376]{2,1,0:T(8,128)(2,1)} %broadcast_select_fusion), calls=%async_computation.3 | async-start | bytes 5505024 | tf_op jit(solution)/shard_map/all_to_all | solution.py:323
  112.7 3.9 %collective-permute-done.7.refs_7_ = bf16[128,5376]{1,0:T(8,128)(2,1)} collective-permute-done((bf16[128,5376]{1,0:T(8,128)(2,1)}, bf16[128,5376]{1,0:T(8,128)(2,1)}, u32[]{:S(2)}, u32[]{:S(2)}) %collective-permute-start.7) | collective-permute-done | bytes 1376288 | tf_op jit(solution)/shard_map/ppermute | solution.py:315
  116.7 1.8 collective-permute-done.9.refs_9_
  118.4 29.3 %all-to-all-done.3 = bf16[16,16,5376]{2,1,0:T(8,128)(2,1)} async-done(((bf16[16,16,5376]{2,1,0:T(8,128)(2,1)}), bf16[16,16,5376]{2,1,0:T(8,128)(2,1)}, u32[]{:S(2)}, u32[]{:S(2)}) %all-to-all-start.3) | async-done | bytes 2752544 | tf_op jit(solution)/shard_map/all_to_all | solution.py:323
  147.8 13.8 %shard_map.149 = (f32[256,2048]{1,0:T(8,128)}, f32[256,128]{1,0:T(8,128)S(1)}) custom-call(bf16[256,5376]{1,0:T(8,128)(2,1)} %bitcast.23.rows, s32[256,1]{1,0:T(8,128)S(1)} %copy.141.target_column, bf16[512,5376]{1,0:T(8,128)(2,1)} %refs_0_.1, bf16[512,5376]{1,0:T(8,128)(2,1)} %collective-permute-done.5.refs_1_, ...), custom_call_target="tpu_custom_call" | custom-call | flops 5637144576 | bytes 22020096 | tf_op jit(solution)/shard_map/pallas_call | solution.py:148
  161.7 14.5 %all_to_all.45 = f32[8,3,256]{2,1,0:T(4,128)S(1)} all-to-all(f32[8,3,256]{2,1,0:T(4,128)S(1)} %broadcast_in_dim.190), channel_id=1, replica_groups=mesh['x'=4,'y'=4,'c'=2,'zh'=4,'zl'=2] {'zh','zl'}, dimensions={0} | all-to-all | bytes 49152 | tf_op jit(solution)/shard_map/all_to_all | solution.py:22
  176.3 15.8 %all_to_all.46 = f32[16,3,256]{2,1,0:T(4,128)S(1)} all-to-all(f32[16,3,256]{2,1,0:T(4,128)S(1)} %broadcast_in_dim.191), channel_id=1, replica_groups=mesh['x'=4,'y'=4,'c'=2,'zh'=4,'zl'=2] {'x','y'}, dimensions={0} | all-to-all | bytes 98304 | tf_op jit(solution)/shard_map/all_to_all | solution.py:22
  192.9 12.3 %shard_map.150 = bf16[256,5376]{1,0:T(8,128)(2,1)} custom-call(f32[256,2048]{1,0:T(8,128)} %get-tuple-element.93.logits, s32[256,1]{1,0:T(8,128)S(1)} %copy.152.target_column, f32[256,1]{1,0:T(8,128)S(1)} %copy.153.log_total, f32[256,1]{1,0:T(8,128)S(1)} %copy.154.token_weight, bf16[512,5376]{1,0:T(8,128)(2,1)} %refs_0_.1, ...), custom_call_target="tpu_custom_call" | custom-call | flops 5637144576 | bytes 22020096 | tf_op jit(solution)/shard_map/pallas_call | solution.py:177
  205.2 36.5 %all_to_all.47 = bf16[16,16,5376]{2,1,0:T(8,128)(2,1)S(1)} all-to-all(bf16[16,16,5376]{2,1,0:T(8,128)(2,1)} %bitcast.168), channel_id=1, replica_groups=mesh['x'=4,'y'=4,'c'=2,'zh'=4,'zl'=2] {'x','y'}, dimensions={0} | all-to-all | bytes 5505024 | tf_op jit(solution)/shard_map/all_to_all | solution.py:357
  241.7 1.0 fusion.1
  242.8 1.0 pad_maximum_fusion
  243.7 3.4 %all-to-all-start.7 = ((bf16[8,4,5376]{2,1,0:T(4,128)(2,1)}), bf16[8,4,5376]{2,1,0:T(4,128)(2,1)S(1)}, u32[]{:S(2)}, u32[]{:S(2)}) async-start(bf16[8,4,5376]{2,1,0:T(4,128)(2,1)} %bitcast.48), calls=%async_computation.7 | async-start | bytes 688128 | tf_op jit(solution)/shard_map/all_to_all | solution.py:28
  247.9 10.5 %all-to-all-done.7 = bf16[8,4,5376]{2,1,0:T(4,128)(2,1)S(1)} async-done(((bf16[8,4,5376]{2,1,0:T(4,128)(2,1)}), bf16[8,4,5376]{2,1,0:T(4,128)(2,1)S(1)}, u32[]{:S(2)}, u32[]{:S(2)}) %all-to-all-start.7) | async-done | bytes 344096 | tf_op jit(solution)/shard_map/all_to_all | solution.py:28
  259.0 13.7 %all_to_all.48 = bf16[8,4,5376]{2,1,0:T(4,128)(2,1)S(1)} all-to-all(bf16[8,4,5376]{2,1,0:T(4,128)(2,1)S(1)} %broadcast_in_dim.193), channel_id=1, replica_groups=mesh['x'=4,'y'=4,'c'=2,'zh'=4,'zl'=2] {'zh','zl'}, dimensions={0} | all-to-all | bytes 688128 | tf_op jit(solution)/shard_map/all_to_all | solution.py:22
  272.7 0.9 reshape.398
  (126 shorter events, 14.0 us)
Async XLA Ops:
  0.6 41.8 %copy-start = (bf16[32,512]{1,0:T(8,128)(2,1)S(1)}, bf16[32,512]{1,0:T(8,128)(2,1)}, u32[]{:S(2)}) copy-start(bf16[32,512]{1,0:T(8,128)(2,1)} %param.14) | copy-start | bytes 98308
  3.1 34.8 %copy-start.4 = (s32[128]{0:T(128)S(1)}, s32[128]{0:T(128)}, u32[]{:S(2)}) copy-start(s32[128]{0:T(128)} %param.20) | copy-start | bytes 1540
  3.1 34.8 %all-to-all-start = ((bf16[16,128,512]{2,1,0:T(8,128)(2,1)}), bf16[16,128,512]{2,1,0:T(8,128)(2,1)S(1)}, u32[]{:S(2)}, u32[]{:S(2)}) async-start(bf16[16,128,512]{2,1,0:T(8,128)(2,1)} %broadcast_in_dim.172), calls=%async_computation | async-start | bytes 4194304 | tf_op jit(solution)/shard_map/all_to_all | solution.py:22
  10.7 29.3 %copy-start.1 = (s32[32]{0:T(128)S(1)}, s32[32]{0:T(128)}, u32[]{:S(2)}) copy-start(s32[32]{0:T(128)} %param.19) | copy-start | bytes 388
  39.4 2.1 collective-permute-start
  40.7 1.7 copy-start.7
  41.6 1.2 copy-start.6
  47.8 29.8 %all-to-all-start.1 = ((f32[8,4,5376]{2,1,0:T(4,128)}), f32[8,4,5376]{2,1,0:T(4,128)S(1)}, u32[]{:S(2)}, u32[]{:S(2)}) async-start(f32[8,4,5376]{2,1,0:T(4,128)} %fusion.3), calls=%async_computation.1 | async-start | bytes 1376256 | tf_op jit(solution)/shard_map/all_to_all | solution.py:28
  56.3 23.2 %copy-start.2 = (f32[5376]{0:T(1024)S(1)}, f32[5376]{0:T(1024)}, u32[]{:S(2)}) copy-start(f32[5376]{0:T(1024)} %param.26) | copy-start | bytes 64516
  61.3 33.4 %collective-permute-start.4 = (bf16[128,5376]{1,0:T(8,128)(2,1)}, bf16[128,5376]{1,0:T(8,128)(2,1)S(1)}, u32[]{:S(2)}, u32[]{:S(2)}) collective-permute-start(bf16[128,5376]{1,0:T(8,128)(2,1)} %get-tuple-element.110), channel_id=1, source_target_pairs={{48,0},{0,16},{16,32},{32,48},{49,1},{1,17},{17,33},{33,49},{50,2}... | collective-permute-start | bytes 4128776 | tf_op jit(solution)/shard_map/ppermute | solution.py:254
  61.9 32.8 %collective-permute-start.3 = (bf16[128,5376]{1,0:T(8,128)(2,1)}, bf16[128,5376]{1,0:T(8,128)(2,1)S(1)}, u32[]{:S(2)}, u32[]{:S(2)}) collective-permute-start(bf16[128,5376]{1,0:T(8,128)(2,1)} %get-tuple-element.111), channel_id=1, source_target_pairs={{16,0},{32,16},{48,32},{0,48},{17,1},{33,17},{49,33},{1,49},{18,2}... | collective-permute-start | bytes 4128776 | tf_op jit(solution)/shard_map/ppermute | solution.py:254
  64.6 33.3 %collective-permute-start.2 = (bf16[128,5376]{1,0:T(8,128)(2,1)}, bf16[128,5376]{1,0:T(8,128)(2,1)}, u32[]{:S(2)}, u32[]{:S(2)}) collective-permute-start(bf16[128,5376]{1,0:T(8,128)(2,1)} %get-tuple-element.112), channel_id=1, source_target_pairs={{192,0},{0,64},{64,128},{128,192},{193,1},{1,65},{65,129},{129,193... | collective-permute-start | bytes 4128776 | tf_op jit(solution)/shard_map/ppermute | solution.py:254
  66.9 31.4 %collective-permute-start.1 = (bf16[128,5376]{1,0:T(8,128)(2,1)}, bf16[128,5376]{1,0:T(8,128)(2,1)}, u32[]{:S(2)}, u32[]{:S(2)}) collective-permute-start(bf16[128,5376]{1,0:T(8,128)(2,1)} %get-tuple-element.113), channel_id=1, source_target_pairs={{64,0},{128,64},{192,128},{0,192},{65,1},{129,65},{193,129},{1,193... | collective-permute-start | bytes 4128776 | tf_op jit(solution)/shard_map/ppermute | solution.py:254
  80.4 17.9 %all-to-all-start.2 = ((bf16[8,4,5376]{2,1,0:T(4,128)(2,1)}), bf16[8,4,5376]{2,1,0:T(4,128)(2,1)S(1)}, u32[]{:S(2)}, u32[]{:S(2)}) async-start(bf16[8,4,5376]{2,1,0:T(4,128)(2,1)} %broadcast_in_dim.178), calls=%async_computation.2 | async-start | bytes 688128 | tf_op jit(solution)/shard_map/all_to_all | solution.py:22
  98.3 49.5 %collective-permute-start.5 = (bf16[512,5376]{1,0:T(8,128)(2,1)}, bf16[512,5376]{1,0:T(8,128)(2,1)}, u32[]{:S(2)}, u32[]{:S(2)}) collective-permute-start(bf16[512,5376]{1,0:T(8,128)(2,1)} %refs_0_.1), channel_id=1, source_target_pairs={{0,8},{8,0},{1,9},{9,1},{2,10},{10,2},{3,11},{11,3},{4,12},{12,4},... | collective-permute-start | bytes 16515080 | tf_op jit(solution)/shard_map/ppermute | solution.py:315
  102.0 8.4 %copy-start.8 = (f32[128]{0:T(128)S(1)}, f32[128]{0:T(128)}, u32[]{:S(2)}) copy-start(f32[128]{0:T(128)} %param.23) | copy-start | bytes 1540
  102.0 8.6 %copy-start.5 = (s32[128]{0:T(128)S(1)}, s32[128]{0:T(128)}, u32[]{:S(2)}) copy-start(s32[128]{0:T(128)} %param.21) | copy-start | bytes 1540
  102.0 9.0 %copy-start.3 = (s32[1024]{0:T(1024)S(1)}, s32[1024]{0:T(1024)}, u32[]{:S(2)}) copy-start(s32[1024]{0:T(1024)} %param.22) | copy-start | bytes 12292
  102.0 45.7 %all-to-all-start.3 = ((bf16[16,16,5376]{2,1,0:T(8,128)(2,1)}), bf16[16,16,5376]{2,1,0:T(8,128)(2,1)}, u32[]{:S(2)}, u32[]{:S(2)}) async-start(bf16[16,16,5376]{2,1,0:T(8,128)(2,1)} %broadcast_select_fusion), calls=%async_computation.3 | async-start | bytes 5505024 | tf_op jit(solution)/shard_map/all_to_all | solution.py:323
  109.3 3.5 %collective-permute-start.6 = (bf16[128,5376]{1,0:T(8,128)(2,1)}, bf16[128,5376]{1,0:T(8,128)(2,1)}, u32[]{:S(2)}, u32[]{:S(2)}) collective-permute-start(bf16[128,5376]{1,0:T(8,128)(2,1)} %collective-permute-done.1.refs_2_), channel_id=1, source_target_pairs={{0,8},{8,0},{1,9},{9,1},{2,10},{10,2},{3,11},{11,3},{4,12},{12,4},... | collective-permute-start | bytes 4128776 | tf_op jit(solution)/shard_map/ppermute | solution.py:315
  109.5 7.2 %collective-permute-start.7 = (bf16[128,5376]{1,0:T(8,128)(2,1)}, bf16[128,5376]{1,0:T(8,128)(2,1)}, u32[]{:S(2)}, u32[]{:S(2)}) collective-permute-start(bf16[128,5376]{1,0:T(8,128)(2,1)} %collective-permute-done.2.refs_3_), channel_id=1, source_target_pairs={{0,8},{8,0},{1,9},{9,1},{2,10},{10,2},{3,11},{11,3},{4,12},{12,4},... | collective-permute-start | bytes 4128776 | tf_op jit(solution)/shard_map/ppermute | solution.py:315
  109.8 6.9 %collective-permute-start.8 = (bf16[128,5376]{1,0:T(8,128)(2,1)S(1)}, bf16[128,5376]{1,0:T(8,128)(2,1)}, u32[]{:S(2)}, u32[]{:S(2)}) collective-permute-start(bf16[128,5376]{1,0:T(8,128)(2,1)S(1)} %collective-permute-done.3.refs_4_), channel_id=1, source_target_pairs={{0,8},{8,0},{1,9},{9,1},{2,10},{10,2},{3,11},{11,3},{4,12},{12,4},... | collective-permute-start | bytes 4128776 | tf_op jit(solution)/shard_map/ppermute | solution.py:315
  110.0 8.4 %collective-permute-start.9 = (bf16[128,5376]{1,0:T(8,128)(2,1)S(1)}, bf16[128,5376]{1,0:T(8,128)(2,1)}, u32[]{:S(2)}, u32[]{:S(2)}) collective-permute-start(bf16[128,5376]{1,0:T(8,128)(2,1)S(1)} %collective-permute-done.4.refs_5_), channel_id=1, source_target_pairs={{0,8},{8,0},{1,9},{9,1},{2,10},{10,2},{3,11},{11,3},{4,12},{12,4},... | collective-permute-start | bytes 4128776 | tf_op jit(solution)/shard_map/ppermute | solution.py:315
  243.7 14.7 %all-to-all-start.7 = ((bf16[8,4,5376]{2,1,0:T(4,128)(2,1)}), bf16[8,4,5376]{2,1,0:T(4,128)(2,1)S(1)}, u32[]{:S(2)}, u32[]{:S(2)}) async-start(bf16[8,4,5376]{2,1,0:T(4,128)(2,1)} %bitcast.48), calls=%async_computation.7 | async-start | bytes 688128 | tf_op jit(solution)/shard_map/all_to_all | solution.py:28

commit v8 on v7

--- a/solution.py
+++ b/solution.py
@@ -50,6 +50,12 @@
     )
 
 
+def spread_stats(stats, axes):
+    filled = jnp.concatenate([stats.reshape(-1), jnp.zeros_like(stats[0])])
+    arrived = spread(filled.reshape(-1, 128), axes)
+    return arrived.reshape(arrived.shape[0], 4, -1)[:, :3]
+
+
 def merged(stats):
     top = jnp.max(stats[:, 0], axis=0)
     total = jnp.sum(stats[:, 1] * jnp.exp(stats[:, 0] - top[None]), axis=0)
@@ -67,17 +73,14 @@
 
 
 def logits_kernel(rows, target_column, *refs):
-    parts, (logits, stats, held, held_rows, arrivals, rows_arrival) = refs[:-6], refs[-6:]
+    parts, (logits, stats, held, arrivals) = refs[:-4], refs[-4:]
     starts = placed_rows(parts)
-    rows_copy = pltpu.make_async_copy(rows, held_rows, rows_arrival)
-    rows_copy.start()
     copies = [
         pltpu.make_async_copy(part, held.at[pl.ds(start, part.shape[0])], arrivals.at[k])
         for k, (part, start) in enumerate(zip(parts, starts))
     ]
     for copy in copies:
         copy.start()
-    rows_copy.wait()
     depth = parts[0].shape[0]
     top = total = picked = None
     for start in range(0, starts[-1], depth):
@@ -85,7 +88,7 @@
             if start <= at < start + depth:
                 copy.wait()
         block = lax.dot_general(
-            held_rows[...], held[pl.ds(start, depth), :], NT, preferred_element_type=jnp.float32
+            rows[...], held[pl.ds(start, depth), :], NT, preferred_element_type=jnp.float32
         )
         logits[:, pl.ds(start, depth)] = block
         hit = lax.broadcasted_iota(jnp.int32, block.shape, 1) + start == target_column[...]
@@ -151,15 +154,13 @@
             jax.ShapeDtypeStruct((count, entries), jnp.float32),
             jax.ShapeDtypeStruct((count, 128), jnp.float32),
         ),
-        in_specs=[remain, whole] + [remain] * len(parts),
+        in_specs=[whole, whole] + [remain] * len(parts),
         out_specs=[whole, whole],
         scratch_shapes=[
             pltpu.VMEM((entries, width), jnp.bfloat16),
-            pltpu.VMEM((count, width), jnp.bfloat16),
             pltpu.SemaphoreType.DMA((len(parts),)),
-            pltpu.SemaphoreType.DMA,
         ],
-        compiler_params=pltpu.CompilerParams(vmem_limit_bytes=48 * 1024 * 1024),
+        compiler_params=pltpu.CompilerParams(vmem_limit_bytes=32 * 1024 * 1024),
         cost_estimate=pl.CostEstimate(
             flops=2 * count * entries * width,
             bytes_accessed=2 * entries * width,
@@ -336,9 +337,9 @@
     stats, later = lax.optimization_barrier(
         (stats[:, :3].T, (logits, target_column, token_weight, hidden, norm_factor, norm_gain))
     )
-    stats, later = lax.optimization_barrier((spread(stats, Z), later))
+    stats, later = lax.optimization_barrier((spread_stats(stats, Z), later))
     stats, later = lax.optimization_barrier((merged(stats), later))
-    stats, later = lax.optimization_barrier((spread(stats, ("x", "y")), later))
+    stats, later = lax.optimization_barrier((spread_stats(stats, ("x", "y")), later))
     logits, target_column, token_weight, hidden, norm_factor, norm_gain = later
     stats = stats.reshape(XS // 2, 2, YS // 2, 2, 3, rows_here)
 

time: 274 us -> 276 us (level)
  local copies, waits for them, and re-layouts: 16.2 us -> 24.2 us
  Pallas kernels: 26.1 us -> 20.8 us
    unnamed x22 -> x38, local copies, waits for them, and re-layouts: 0.08 us -> 8 us
    pallas_call x1, Pallas kernels: 13.8 us -> 8.38 us  [slab_logits(): pl.pallas_call(logits_kernel, out_shape=(jax.ShapeDtypeStruct((count, ent...]
  transfers between devices with their start and end apart: 15 -> 15, of which waited for: 11 -> 12; matrix products, arithmetic and copies ran while one was open for 6% -> 6% of each run, Pallas kernels for 0% -> 0%
where the time goes in v8:
time: 276 us; the launch traced here: 275 us
  waiting for transfers between devices  97.4 us (35%)
  blocking collectives  80.4 us (29%)
  starting transfers between devices  37.5 us (14%)
  local copies, waits for them, and re-layouts  24.2 us (9%)
  Pallas kernels  20.8 us (8%)
  other arithmetic  8.19 us (3%)
  matrix products  5.31 us (2%)
    all_to_all x3, blocking collectives, spread(): return lax.all_to_all(copies, axes, 0, 0, tiled=True)  44.5 us
    all_to_all x1, blocking collectives, body(): lax.all_to_all(terms.reshape(planes, pairs * share, width), ('x', 'y'), 0...  35.9 us
    all_to_all x1, waiting for transfers between devices, body(): lax.all_to_all(outgoing, ('x', 'y'), 0, 0, tiled=True)  28.3 us
    all_to_all x2, waiting for transfers between devices, spread(): return lax.all_to_all(copies, axes, 0, 0, tiled=True)  27.1 us
    all_to_all x2, waiting for transfers between devices, summed(): arrived = lax.all_to_all(pieces, axes, 0, 0, tiled=True)  20.2 us
    ppermute x4, waiting for transfers between devices, from_neighbour(): lax.ppermute(embedding[part * quarter:(part + 1) * quarter], axes, pairs)  14.5 us
    pallas_call x1, Pallas kernels, slab_gradient(): pl.pallas_call(gradient_kernel, out_shape=jax.ShapeDtypeStruct((count, wi...  12.4 us
    all_to_all x2, starting transfers between devices, summed(): arrived = lax.all_to_all(pieces, axes, 0, 0, tiled=True)  11.9 us
  transfers between devices with their start and end apart: 15, of which 12 were waited for; matrix products, arithmetic and copies ran while one was open for 6% of the time, Pallas kernels for 0%

profile of v8, /device:TPU:2, one launch (start us, length us, event | category | flops | bytes accessed | tf_op | source)
XLA Modules:
  0.0 275.1 jit_solution(5872385800070125442)
XLA Ops:
  1.5 1.6 broadcast_in_dim.174
  3.1 7.6 %all-to-all-start = ((bf16[16,128,512]{2,1,0:T(8,128)(2,1)}), bf16[16,128,512]{2,1,0:T(8,128)(2,1)S(1)}, u32[]{:S(2)}, u32[]{:S(2)}) async-start(bf16[16,128,512]{2,1,0:T(8,128)(2,1)} %broadcast_in_dim.174), calls=%async_computation | async-start | bytes 4194304 | tf_op jit(solution)/shard_map/all_to_all | solution.py:22
  10.7 27.1 %all-to-all-done = bf16[16,128,512]{2,1,0:T(8,128)(2,1)S(1)} async-done(((bf16[16,128,512]{2,1,0:T(8,128)(2,1)}), bf16[16,128,512]{2,1,0:T(8,128)(2,1)S(1)}, u32[]{:S(2)}, u32[]{:S(2)}) %all-to-all-start) | async-done | bytes 2097184 | tf_op jit(solution)/shard_map/all_to_all | solution.py:22
  38.0 1.4 gather_fusion.1
  43.4 4.4 %fusion.3 = f32[8,4,5376]{2,1,0:T(4,128)} fusion(bf16[8,4,512]{2,1,0:T(4,128)(2,1)S(1)} %convert_element_type.46, bf16[512,5376]{1,0:T(8,128)(2,1)} %param.25), kind=kOutput, calls=%fused_computation.8 | convolution fusion | flops 176160768 | bytes 6225920 | tf_op jit(solution)/shard_map/dot_general | solution.py:303
  47.8 8.5 %all-to-all-start.1 = ((f32[8,4,5376]{2,1,0:T(4,128)}), f32[8,4,5376]{2,1,0:T(4,128)S(1)}, u32[]{:S(2)}, u32[]{:S(2)}) async-start(f32[8,4,5376]{2,1,0:T(4,128)} %fusion.3), calls=%async_computation.1 | async-start | bytes 1376256 | tf_op jit(solution)/shard_map/all_to_all | solution.py:28
  56.3 5.1 %fusion.69 = (bf16[128,5376]{1,0:T(8,128)(2,1)}, bf16[128,5376]{1,0:T(8,128)(2,1)}, bf16[128,5376]{1,0:T(8,128)(2,1)}, bf16[128,5376]{1,0:T(8,128)(2,1)}) fusion(bf16[512,5376]{1,0:T(8,128)(2,1)} %refs_0_.1), kind=kLoop, calls=%fused_computation.171 | loop fusion | bytes 11010048 | tf_op jit(solution)/shard_map/slice | solution.py:255
  61.9 2.7 collective-permute-start.3
  64.6 2.3 collective-permute-start.2
  67.9 9.7 %all-to-all-done.1 = f32[8,4,5376]{2,1,0:T(4,128)S(1)} async-done(((f32[8,4,5376]{2,1,0:T(4,128)}), f32[8,4,5376]{2,1,0:T(4,128)S(1)}, u32[]{:S(2)}, u32[]{:S(2)}) %all-to-all-start.1) | async-done | bytes 688160 | tf_op jit(solution)/shard_map/all_to_all | solution.py:28
  80.4 3.4 %all-to-all-start.2 = ((bf16[8,4,5376]{2,1,0:T(4,128)(2,1)}), bf16[8,4,5376]{2,1,0:T(4,128)(2,1)S(1)}, u32[]{:S(2)}, u32[]{:S(2)}) async-start(bf16[8,4,5376]{2,1,0:T(4,128)(2,1)} %broadcast_in_dim.180), calls=%async_computation.2 | async-start | bytes 688128 | tf_op jit(solution)/shard_map/all_to_all | solution.py:22
  83.8 10.9 %collective-permute-done.4.refs_5_ = bf16[128,5376]{1,0:T(8,128)(2,1)S(1)} collective-permute-done((bf16[128,5376]{1,0:T(8,128)(2,1)}, bf16[128,5376]{1,0:T(8,128)(2,1)S(1)}, u32[]{:S(2)}, u32[]{:S(2)}) %collective-permute-start.4) | collective-permute-done | bytes 1376288 | tf_op jit(solution)/shard_map/ppermute | solution.py:255
  94.7 3.1 %collective-permute-done.2.refs_3_ = bf16[128,5376]{1,0:T(8,128)(2,1)} collective-permute-done((bf16[128,5376]{1,0:T(8,128)(2,1)}, bf16[128,5376]{1,0:T(8,128)(2,1)}, u32[]{:S(2)}, u32[]{:S(2)}) %collective-permute-start.2) | collective-permute-done | bytes 1376288 | tf_op jit(solution)/shard_map/ppermute | solution.py:255
  100.1 1.8 broadcast_select_fusion
  101.9 6.9 %all-to-all-start.3 = ((bf16[16,16,5376]{2,1,0:T(8,128)(2,1)}), bf16[16,16,5376]{2,1,0:T(8,128)(2,1)S(1)}, u32[]{:S(2)}, u32[]{:S(2)}) async-start(bf16[16,16,5376]{2,1,0:T(8,128)(2,1)} %broadcast_select_fusion), calls=%async_computation.3 | async-start | bytes 5505024 | tf_op jit(solution)/shard_map/all_to_all | solution.py:324
  112.4 2.0 collective-permute-done.7.refs_7_
  114.3 2.0 collective-permute-done.8.refs_8_
  116.3 2.0 collective-permute-done.9.refs_9_
  118.3 28.3 %all-to-all-done.3 = bf16[16,16,5376]{2,1,0:T(8,128)(2,1)S(1)} async-done(((bf16[16,16,5376]{2,1,0:T(8,128)(2,1)}), bf16[16,16,5376]{2,1,0:T(8,128)(2,1)S(1)}, u32[]{:S(2)}, u32[]{:S(2)}) %all-to-all-start.3) | async-done | bytes 2752544 | tf_op jit(solution)/shard_map/all_to_all | solution.py:324
  146.6 2.6 copy-done.1
  149.2 1.3 copy-done.3
  150.5 1.3 copy-done.6
  151.8 8.4 %shard_map.149 = (f32[256,2048]{1,0:T(8,128)S(1)}, f32[256,128]{1,0:T(8,128)S(1)}) custom-call(bf16[256,5376]{1,0:T(8,128)(2,1)S(1)} %bitcast.174, s32[256,1]{1,0:T(8,128)S(1)} %copy.123.target_column, bf16[512,5376]{1,0:T(8,128)(2,1)S(1)} %copy-done.1, bf16[512,5376]{1,0:T(8,128)(2,1)} %collective-permute-done.5.refs_1_, ...), custom_call_target="tpu_custom_call" | custom-call | flops 5637144576 | bytes 22020096 | tf_op jit(solution)/shard_map/pallas_call | solution.py:151
  160.2 1.3 copy-done.8
  161.7 14.9 %all_to_all.45 = f32[8,8,128]{2,1,0:T(8,128)S(1)} all-to-all(f32[8,8,128]{2,1,0:T(8,128)S(1)} %broadcast_in_dim.193), channel_id=1, replica_groups=mesh['x'=4,'y'=4,'c'=2,'zh'=4,'zl'=2] {'zh','zl'}, dimensions={0} | all-to-all | bytes 65536 | tf_op jit(solution)/shard_map/all_to_all | solution.py:22
  176.8 15.9 %all_to_all.46 = f32[16,8,128]{2,1,0:T(8,128)S(1)} all-to-all(f32[16,8,128]{2,1,0:T(8,128)S(1)} %broadcast_in_dim.195), channel_id=1, replica_groups=mesh['x'=4,'y'=4,'c'=2,'zh'=4,'zl'=2] {'x','y'}, dimensions={0} | all-to-all | bytes 131072 | tf_op jit(solution)/shard_map/all_to_all | solution.py:22
  193.5 1.3 copy-done.7
  194.9 12.4 %shard_map.150 = bf16[256,5376]{1,0:T(8,128)(2,1)} custom-call(f32[256,2048]{1,0:T(8,128)} %copy-done.8, s32[256,1]{1,0:T(8,128)S(1)} %copy.134.target_column, f32[256,1]{1,0:T(8,128)S(1)} %copy.135.log_total, f32[256,1]{1,0:T(8,128)S(1)} %copy.136.token_weight, bf16[512,5376]{1,0:T(8,128)(2,1)} %refs_0_.1, ...), custom_call_target="tpu_custom_call" | custom-call | flops 5637144576 | bytes 22020096 | tf_op jit(solution)/shard_map/pallas_call | solution.py:178
  207.3 35.9 %all_to_all.47 = bf16[16,16,5376]{2,1,0:T(8,128)(2,1)S(1)} all-to-all(bf16[16,16,5376]{2,1,0:T(8,128)(2,1)} %bitcast.175), channel_id=1, replica_groups=mesh['x'=4,'y'=4,'c'=2,'zh'=4,'zl'=2] {'x','y'}, dimensions={0} | all-to-all | bytes 5505024 | tf_op jit(solution)/shard_map/all_to_all | solution.py:358
  245.2 3.4 %all-to-all-start.7 = ((bf16[8,4,5376]{2,1,0:T(4,128)(2,1)}), bf16[8,4,5376]{2,1,0:T(4,128)(2,1)S(1)}, u32[]{:S(2)}, u32[]{:S(2)}) async-start(bf16[8,4,5376]{2,1,0:T(4,128)(2,1)} %bitcast.50), calls=%async_computation.7 | async-start | bytes 688128 | tf_op jit(solution)/shard_map/all_to_all | solution.py:28
  249.4 10.5 %all-to-all-done.7 = bf16[8,4,5376]{2,1,0:T(4,128)(2,1)S(1)} async-done(((bf16[8,4,5376]{2,1,0:T(4,128)(2,1)}), bf16[8,4,5376]{2,1,0:T(4,128)(2,1)S(1)}, u32[]{:S(2)}, u32[]{:S(2)}) %all-to-all-start.7) | async-done | bytes 344096 | tf_op jit(solution)/shard_map/all_to_all | solution.py:28
  260.5 13.7 %all_to_all.48 = bf16[8,4,5376]{2,1,0:T(4,128)(2,1)S(1)} all-to-all(bf16[8,4,5376]{2,1,0:T(4,128)(2,1)S(1)} %broadcast_in_dim.197), channel_id=1, replica_groups=mesh['x'=4,'y'=4,'c'=2,'zh'=4,'zl'=2] {'zh','zl'}, dimensions={0} | all-to-all | bytes 688128 | tf_op jit(solution)/shard_map/all_to_all | solution.py:22
  (148 shorter events, 20.0 us)
Async XLA Ops:
  0.6 41.8 %copy-start = (bf16[32,512]{1,0:T(8,128)(2,1)S(1)}, bf16[32,512]{1,0:T(8,128)(2,1)}, u32[]{:S(2)}) copy-start(bf16[32,512]{1,0:T(8,128)(2,1)} %param.14) | copy-start | bytes 98308
  3.1 34.8 %copy-start.12 = (s32[128]{0:T(128)S(1)}, s32[128]{0:T(128)}, u32[]{:S(2)}) copy-start(s32[128]{0:T(128)} %param.20) | copy-start | bytes 1540
  3.1 34.8 %all-to-all-start = ((bf16[16,128,512]{2,1,0:T(8,128)(2,1)}), bf16[16,128,512]{2,1,0:T(8,128)(2,1)S(1)}, u32[]{:S(2)}, u32[]{:S(2)}) async-start(bf16[16,128,512]{2,1,0:T(8,128)(2,1)} %broadcast_in_dim.174), calls=%async_computation | async-start | bytes 4194304 | tf_op jit(solution)/shard_map/all_to_all | solution.py:22
  10.7 29.3 %copy-start.9 = (s32[32]{0:T(128)S(1)}, s32[32]{0:T(128)}, u32[]{:S(2)}) copy-start(s32[32]{0:T(128)} %param.19) | copy-start | bytes 388
  39.4 2.1 collective-permute-start
  40.7 1.7 copy-start.15
  41.6 1.2 copy-start.14
  47.8 29.8 %all-to-all-start.1 = ((f32[8,4,5376]{2,1,0:T(4,128)}), f32[8,4,5376]{2,1,0:T(4,128)S(1)}, u32[]{:S(2)}, u32[]{:S(2)}) async-start(f32[8,4,5376]{2,1,0:T(4,128)} %fusion.3), calls=%async_computation.1 | async-start | bytes 1376256 | tf_op jit(solution)/shard_map/all_to_all | solution.py:28
  56.3 23.2 %copy-start.10 = (f32[5376]{0:T(1024)S(1)}, f32[5376]{0:T(1024)}, u32[]{:S(2)}) copy-start(f32[5376]{0:T(1024)} %param.26) | copy-start | bytes 64516
  61.3 33.4 %collective-permute-start.4 = (bf16[128,5376]{1,0:T(8,128)(2,1)}, bf16[128,5376]{1,0:T(8,128)(2,1)S(1)}, u32[]{:S(2)}, u32[]{:S(2)}) collective-permute-start(bf16[128,5376]{1,0:T(8,128)(2,1)} %get-tuple-element.110), channel_id=1, source_target_pairs={{48,0},{0,16},{16,32},{32,48},{49,1},{1,17},{17,33},{33,49},{50,2}... | collective-permute-start | bytes 4128776 | tf_op jit(solution)/shard_map/ppermute | solution.py:255
  61.9 32.8 %collective-permute-start.3 = (bf16[128,5376]{1,0:T(8,128)(2,1)}, bf16[128,5376]{1,0:T(8,128)(2,1)S(1)}, u32[]{:S(2)}, u32[]{:S(2)}) collective-permute-start(bf16[128,5376]{1,0:T(8,128)(2,1)} %get-tuple-element.111), channel_id=1, source_target_pairs={{16,0},{32,16},{48,32},{0,48},{17,1},{33,17},{49,33},{1,49},{18,2}... | collective-permute-start | bytes 4128776 | tf_op jit(solution)/shard_map/ppermute | solution.py:255
  64.6 33.3 %collective-permute-start.2 = (bf16[128,5376]{1,0:T(8,128)(2,1)}, bf16[128,5376]{1,0:T(8,128)(2,1)}, u32[]{:S(2)}, u32[]{:S(2)}) collective-permute-start(bf16[128,5376]{1,0:T(8,128)(2,1)} %get-tuple-element.112), channel_id=1, source_target_pairs={{192,0},{0,64},{64,128},{128,192},{193,1},{1,65},{65,129},{129,193... | collective-permute-start | bytes 4128776 | tf_op jit(solution)/shard_map/ppermute | solution.py:255
  66.9 31.4 %collective-permute-start.1 = (bf16[128,5376]{1,0:T(8,128)(2,1)}, bf16[128,5376]{1,0:T(8,128)(2,1)}, u32[]{:S(2)}, u32[]{:S(2)}) collective-permute-start(bf16[128,5376]{1,0:T(8,128)(2,1)} %get-tuple-element.113), channel_id=1, source_target_pairs={{64,0},{128,64},{192,128},{0,192},{65,1},{129,65},{193,129},{1,193... | collective-permute-start | bytes 4128776 | tf_op jit(solution)/shard_map/ppermute | solution.py:255
  80.4 17.9 %all-to-all-start.2 = ((bf16[8,4,5376]{2,1,0:T(4,128)(2,1)}), bf16[8,4,5376]{2,1,0:T(4,128)(2,1)S(1)}, u32[]{:S(2)}, u32[]{:S(2)}) async-start(bf16[8,4,5376]{2,1,0:T(4,128)(2,1)} %broadcast_in_dim.180), calls=%async_computation.2 | async-start | bytes 688128 | tf_op jit(solution)/shard_map/all_to_all | solution.py:22
  94.7 7.2 %copy-start.2 = (bf16[128,5376]{1,0:T(8,128)(2,1)}, bf16[128,5376]{1,0:T(8,128)(2,1)S(1)}, u32[]{:S(2)}) copy-start(bf16[128,5376]{1,0:T(8,128)(2,1)S(1)} %collective-permute-done.4.refs_5_) | copy-start | bytes 4128772
  94.7 7.2 %copy-start.5 = (bf16[128,5376]{1,0:T(8,128)(2,1)}, bf16[128,5376]{1,0:T(8,128)(2,1)S(1)}, u32[]{:S(2)}) copy-start(bf16[128,5376]{1,0:T(8,128)(2,1)S(1)} %collective-permute-done.3.refs_4_) | copy-start | bytes 4128772
  98.3 48.3 %collective-permute-start.5 = (bf16[512,5376]{1,0:T(8,128)(2,1)}, bf16[512,5376]{1,0:T(8,128)(2,1)}, u32[]{:S(2)}, u32[]{:S(2)}) collective-permute-start(bf16[512,5376]{1,0:T(8,128)(2,1)} %refs_0_.1), channel_id=1, source_target_pairs={{0,8},{8,0},{1,9},{9,1},{2,10},{10,2},{3,11},{11,3},{4,12},{12,4},... | collective-permute-start | bytes 16515080 | tf_op jit(solution)/shard_map/ppermute | solution.py:316
  101.9 8.2 %copy-start.16 = (f32[128]{0:T(128)S(1)}, f32[128]{0:T(128)}, u32[]{:S(2)}) copy-start(f32[128]{0:T(128)} %param.23) | copy-start | bytes 1540
  101.9 8.3 %copy-start.13 = (s32[128]{0:T(128)S(1)}, s32[128]{0:T(128)}, u32[]{:S(2)}) copy-start(s32[128]{0:T(128)} %param.21) | copy-start | bytes 1540
  101.9 8.7 %copy-start.11 = (s32[1024]{0:T(1024)S(1)}, s32[1024]{0:T(1024)}, u32[]{:S(2)}) copy-start(s32[1024]{0:T(1024)} %param.22) | copy-start | bytes 12292
  101.9 44.7 %all-to-all-start.3 = ((bf16[16,16,5376]{2,1,0:T(8,128)(2,1)}), bf16[16,16,5376]{2,1,0:T(8,128)(2,1)S(1)}, u32[]{:S(2)}, u32[]{:S(2)}) async-start(bf16[16,16,5376]{2,1,0:T(8,128)(2,1)} %broadcast_select_fusion), calls=%async_computation.3 | async-start | bytes 5505024 | tf_op jit(solution)/shard_map/all_to_all | solution.py:324
  108.9 3.5 %collective-permute-start.6 = (bf16[128,5376]{1,0:T(8,128)(2,1)}, bf16[128,5376]{1,0:T(8,128)(2,1)}, u32[]{:S(2)}, u32[]{:S(2)}) collective-permute-start(bf16[128,5376]{1,0:T(8,128)(2,1)} %collective-permute-done.1.refs_2_), channel_id=1, source_target_pairs={{0,8},{8,0},{1,9},{9,1},{2,10},{10,2},{3,11},{11,3},{4,12},{12,4},... | collective-permute-start | bytes 4128776 | tf_op jit(solution)/shard_map/ppermute | solution.py:316
  108.9 5.4 %collective-permute-start.7 = (bf16[128,5376]{1,0:T(8,128)(2,1)}, bf16[128,5376]{1,0:T(8,128)(2,1)}, u32[]{:S(2)}, u32[]{:S(2)}) collective-permute-start(bf16[128,5376]{1,0:T(8,128)(2,1)} %collective-permute-done.2.refs_3_), channel_id=1, source_target_pairs={{0,8},{8,0},{1,9},{9,1},{2,10},{10,2},{3,11},{11,3},{4,12},{12,4},... | collective-permute-start | bytes 4128776 | tf_op jit(solution)/shard_map/ppermute | solution.py:316
  109.4 6.9 %collective-permute-start.8 = (bf16[128,5376]{1,0:T(8,128)(2,1)}, bf16[128,5376]{1,0:T(8,128)(2,1)}, u32[]{:S(2)}, u32[]{:S(2)}) collective-permute-start(bf16[128,5376]{1,0:T(8,128)(2,1)} %copy-done.5), channel_id=1, source_target_pairs={{0,8},{8,0},{1,9},{9,1},{2,10},{10,2},{3,11},{11,3},{4,12},{12,4},... | collective-permute-start | bytes 4128776 | tf_op jit(solution)/shard_map/ppermute | solution.py:316
  109.5 8.8 %collective-permute-start.9 = (bf16[128,5376]{1,0:T(8,128)(2,1)}, bf16[128,5376]{1,0:T(8,128)(2,1)}, u32[]{:S(2)}, u32[]{:S(2)}) collective-permute-start(bf16[128,5376]{1,0:T(8,128)(2,1)} %copy-done.2), channel_id=1, source_target_pairs={{0,8},{8,0},{1,9},{9,1},{2,10},{10,2},{3,11},{11,3},{4,12},{12,4},... | collective-permute-start | bytes 4128776 | tf_op jit(solution)/shard_map/ppermute | solution.py:316
  146.6 2.6 copy-start.1
  149.2 1.3 copy-start.3
  150.5 1.3 copy-start.6
  160.2 1.3 copy-start.8
  161.6 31.9 %copy-start.4 = (bf16[128,5376]{1,0:T(8,128)(2,1)S(1)}, bf16[128,5376]{1,0:T(8,128)(2,1)}, u32[]{:S(2)}) copy-start(bf16[128,5376]{1,0:T(8,128)(2,1)} %copy-done.2) | copy-start | bytes 4128772
  193.5 1.3 copy-start.7
  245.2 14.7 %all-to-all-start.7 = ((bf16[8,4,5376]{2,1,0:T(4,128)(2,1)}), bf16[8,4,5376]{2,1,0:T(4,128)(2,1)S(1)}, u32[]{:S(2)}, u32[]{:S(2)}) async-start(bf16[8,4,5376]{2,1,0:T(4,128)(2,1)} %bitcast.50), calls=%async_computation.7 | async-start | bytes 688128 | tf_op jit(solution)/shard_map/all_to_all | solution.py:28
